TPU v7x, 768 devices: a whole 4x8x12 slice. The times are simulated.
768 devices in a mesh: depth: 12 (over z_hi, x), freq: 64 (over y, z_lo, core).
Axes of the slice: x: 4, y: 8, z: 12 (z_hi: 3, z_lo: 4; z = z_hi * 4 + z_lo), core: 2. Of those that a mesh axis runs over, the one named last changes fastest.
Arguments:
- surface: bfloat16 [256, 2, 64, 256], P('freq'), may hold values from -6 to 6
- regions: int32 [12, 64, 256], P('depth'), may hold values from 0 to 3
- table: bfloat16 [256, 4, 2, 2, 25], P('freq'), may hold values from -1 to 1
- source: bfloat16 [12, 256, 2, 64, 256], P('depth', 'freq'), may hold values from -6 to 6
Outputs:
- image: float32 [12, 32, 64, 256], P('depth', None, 'freq')
All inputs are finite; a program needn't handle non-finite values.
Results may differ from a plain program's by a relative error of at most 0.011.
Values may be sent and summed in bfloat16 or wider, within the bound.
No kernel may reach another device: no remote copies, remote signals or barrier semaphores. Data moves between devices by JAX's collectives and lax.ppermute only.
A program may use at most 32 MiB of HBM per device.

v0:
```python
import math

import jax
import jax.numpy as jnp
from jax import lax
from jax.sharding import PartitionSpec as P

H = 32


def passed_along(block, axis, distance):
    devices = range(lax.axis_size(axis))
    route = [(i - distance, i) for i in devices if i - distance in devices]
    return lax.ppermute(block, axis, route)


def band_matrices(taps, extent):
    count = taps.shape[-1]
    positions = jnp.arange(extent)
    offset_table = positions[None, :] - positions[:, None] + count // 2
    onehot = (offset_table[:, :, None] == jnp.arange(count)[None, None, :]).astype(jnp.float32)
    return jnp.einsum("...t,ijt->...ij", taps.astype(jnp.float32), onehot).astype(jnp.bfloat16)


def complex_pass(wavefield, bands, region_masks, along_first):
    accumulated = jnp.zeros(wavefield.shape, jnp.float32)
    wave_real = wavefield[:, 0]
    wave_imag = wavefield[:, 1]
    for region in range(bands.shape[1]):
        band_real = bands[:, region, 0]
        band_imag = bands[:, region, 1]

        def product(band, signal):
            if along_first:
                return jnp.einsum("bxk,bky->bxy", band, signal, preferred_element_type=jnp.float32)
            return jnp.einsum("bxk,byk->bxy", signal, band, preferred_element_type=jnp.float32)

        real_part = product(band_real, wave_real) - product(band_imag, wave_imag)
        imag_part = product(band_real, wave_imag) + product(band_imag, wave_real)
        accumulated = accumulated + region_masks[region] * jnp.stack([real_part, imag_part], axis=1)
    return accumulated.astype(jnp.bfloat16)


def offset_image(wavefield, source_field):
    reach = H // 2
    lateral = wavefield.shape[2]
    padded_wave = jnp.pad(wavefield, ((0, 0), (0, 0), (reach, reach), (0, 0)))
    padded_source = jnp.pad(source_field, ((0, 0), (0, 0), (reach, reach), (0, 0)))
    images = []
    for shift_value in range(-reach, reach):
        first = padded_wave[:, :, reach + shift_value : reach + shift_value + lateral].astype(
            jnp.float32
        )
        second = padded_source[:, :, reach - shift_value : reach - shift_value + lateral].astype(
            jnp.float32
        )
        images.append(jnp.sum(first * second, axis=(0, 1)))
    return jnp.stack(images)


def body(surface, regions, table, source):
    local_freqs = surface.shape[0]
    lateral_first = surface.shape[2]
    lateral_second = surface.shape[3]
    region_count = table.shape[1]
    region_masks = (regions[0][None] == jnp.arange(region_count)[:, None, None]).astype(jnp.float32)
    band_first = band_matrices(table[:, :, 0], lateral_first)
    band_second = band_matrices(table[:, :, 1], lateral_second)
    batch_count = local_freqs // local_freqs
    sections = lax.axis_size("depth")
    depth_index = lax.axis_index("depth")

    def advance_tick(step_number, state_pair):
        incoming, results = state_pair
        batch_index = step_number - depth_index
        active = jnp.logical_and(batch_index >= 0, batch_index < batch_count)
        entering = jnp.where(depth_index == 0, surface, incoming)

        def extrapolate():
            between = complex_pass(entering, band_first, region_masks, True)
            return complex_pass(between, band_second, region_masks, False)

        def resting():
            return jnp.zeros_like(entering)

        leaving = lax.cond(active, extrapolate, resting)
        results = jnp.where(active, leaving, results)
        incoming = passed_along(leaving, "depth", 1)
        return (incoming, results)

    initial = (jnp.zeros((local_freqs,) + surface.shape[1:], jnp.bfloat16), jnp.zeros_like(surface))
    finished = lax.fori_loop(0, sections + batch_count - 1, advance_tick, initial)
    scale = 1.0 / math.sqrt(local_freqs * lax.axis_size("freq"))
    partial_value = offset_image(finished[1], source[0]) * scale
    mine = lax.psum_scatter(partial_value, "freq", scatter_dimension=1, tiled=True)
    return mine[None]


def solution(mesh):
    in_specs = (
        P("freq", None, None, None),
        P("depth", None, None),
        P("freq", None, None, None, None),
        P("depth", "freq", None, None, None),
    )
    out_specs = P("depth", None, "freq", None)
    return jax.shard_map(body, mesh=mesh, in_specs=in_specs, out_specs=out_specs, check_vma=False)
```

profile of v0, /device:TPU:1, one launch (start us, length us, event | category | flops | bytes accessed | tf_op | source)
XLA Modules:
  0.0 692.1 jit_solution(13642068793251386499)
XLA Ops:
  6.6 0.7 fusion.121
  7.3 2.3 fusion.114
  9.7 4.4 copy.15
  14.1 0.4 fusion.117
  14.8 175.3 %while.17 = (s32[]{:T(128)}, bf16[4,2,64,256]{3,2,0,1:T(8,128)(2,1)S(1)}, bf16[4,2,64,256]{3,2,0,1:T(8,128)(2,1)S(1)}, s32[]{:T(128)}, pred[]{:T(512)}, /*index=...) while((s32[]{:T(128)}, ...), condition=%wide.region_3.4_spmd.clone, body=%wide.region_0.3_spmd.clone.sunk | while | flops 675807232 | bytes 51708184 | solution.py:92
  15.1 8.2 %conditional.3 = (bf16[4,2,64,256]{3,2,0,1:T(8,128)(2,1)S(1)}) conditional(s32[]{:T(128)} %convert_element_type.378, () %tuple.80, (f32[4,64,256]{2,1,0:T(8,128)S(1)}, pred[]{:T(512)}, bf16[4,2,64,256]{3,2,0,1:T(8,128)(2,1)S(1)}, bf16[4,2,64,256]{3,2,0,1:T(8,128)(2,1)S(1)}, bf16[4,4,2,64,64]{4,3,0,2,1:T(8,128)(2,1)S(1)}, ...), branch_computations={%region_1.1_spmd, %region_2.2_spmd} | conditional | flops 675414016 | bytes 49545252 | solution.py:86
  18.1 0.4 copy-done
  18.8 0.3 fusion.11
  19.1 0.3 fusion.28
  19.4 0.3 fusion.10
  19.7 0.3 fusion.36
  19.9 0.3 fusion.13
  20.2 0.3 fusion.34
  20.5 0.3 fusion.12
  20.8 0.3 fusion.42
  21.1 0.3 fusion.15
  21.4 0.3 fusion.40
  21.7 0.3 fusion.14
  22.0 0.3 fusion.48
  22.2 0.3 fusion.17
  22.5 0.3 fusion.46
  22.8 0.3 fusion.16
  23.3 1.3 collective-permute-start
  24.7 3.2 collective-permute-done
  28.0 12.0 %collective-permute-start = (bf16[4,2,64,256]{3,2,0,1:T(8,128)(2,1)S(1)}, bf16[4,2,64,256]{3,2,0,1:T(8,128)(2,1)S(1)}, u32[]{:S(2)}, u32[]{:S(2)}) collective-permute-start(bf16[4,2,64,256]{3,2,0,1:T(8,128)(2,1)S(1)} %get-tuple-element.405), channel_id=1, source_target_pairs={{0,64},{64,128},{128,192},{192,256},{256,320},{320,384},{384,448},... | collective-permute-start | bytes 786440 | tf_op jit(solution)/shard_map/while/body/eval_jaxpr/ppermute | solution.py:14
  40.1 3.2 collective-permute-done
  43.3 3.8 collective-permute-start
  47.3 3.2 collective-permute-done
  50.5 10.1 %collective-permute-start = (bf16[4,2,64,256]{3,2,0,1:T(8,128)(2,1)S(1)}, bf16[4,2,64,256]{3,2,0,1:T(8,128)(2,1)S(1)}, u32[]{:S(2)}, u32[]{:S(2)}) collective-permute-start(bf16[4,2,64,256]{3,2,0,1:T(8,128)(2,1)S(1)} %get-tuple-element.405), channel_id=1, source_target_pairs={{0,64},{64,128},{128,192},{192,256},{256,320},{320,384},{384,448},... | collective-permute-start | bytes 786440 | tf_op jit(solution)/shard_map/while/body/eval_jaxpr/ppermute | solution.py:14
  60.8 5.5 collective-permute-done
  66.3 3.8 collective-permute-start
  70.3 3.2 collective-permute-done
  73.5 11.0 %collective-permute-start = (bf16[4,2,64,256]{3,2,0,1:T(8,128)(2,1)S(1)}, bf16[4,2,64,256]{3,2,0,1:T(8,128)(2,1)S(1)}, u32[]{:S(2)}, u32[]{:S(2)}) collective-permute-start(bf16[4,2,64,256]{3,2,0,1:T(8,128)(2,1)S(1)} %get-tuple-element.405), channel_id=1, source_target_pairs={{0,64},{64,128},{128,192},{192,256},{256,320},{320,384},{384,448},... | collective-permute-start | bytes 786440 | tf_op jit(solution)/shard_map/while/body/eval_jaxpr/ppermute | solution.py:14
  84.6 5.3 collective-permute-done
  90.0 3.8 collective-permute-start
  94.0 3.2 collective-permute-done
  97.2 12.8 %collective-permute-start = (bf16[4,2,64,256]{3,2,0,1:T(8,128)(2,1)S(1)}, bf16[4,2,64,256]{3,2,0,1:T(8,128)(2,1)S(1)}, u32[]{:S(2)}, u32[]{:S(2)}) collective-permute-start(bf16[4,2,64,256]{3,2,0,1:T(8,128)(2,1)S(1)} %get-tuple-element.405), channel_id=1, source_target_pairs={{0,64},{64,128},{128,192},{192,256},{256,320},{320,384},{384,448},... | collective-permute-start | bytes 786440 | tf_op jit(solution)/shard_map/while/body/eval_jaxpr/ppermute | solution.py:14
  110.2 3.2 collective-permute-done
  113.4 16.7 %collective-permute-start = (bf16[4,2,64,256]{3,2,0,1:T(8,128)(2,1)S(1)}, bf16[4,2,64,256]{3,2,0,1:T(8,128)(2,1)S(1)}, u32[]{:S(2)}, u32[]{:S(2)}) collective-permute-start(bf16[4,2,64,256]{3,2,0,1:T(8,128)(2,1)S(1)} %get-tuple-element.405), channel_id=1, source_target_pairs={{0,64},{64,128},{128,192},{192,256},{256,320},{320,384},{384,448},... | collective-permute-start | bytes 786440 | tf_op jit(solution)/shard_map/while/body/eval_jaxpr/ppermute | solution.py:14
  130.3 4.5 collective-permute-done
  134.8 15.9 %collective-permute-start = (bf16[4,2,64,256]{3,2,0,1:T(8,128)(2,1)S(1)}, bf16[4,2,64,256]{3,2,0,1:T(8,128)(2,1)S(1)}, u32[]{:S(2)}, u32[]{:S(2)}) collective-permute-start(bf16[4,2,64,256]{3,2,0,1:T(8,128)(2,1)S(1)} %get-tuple-element.405), channel_id=1, source_target_pairs={{0,64},{64,128},{128,192},{192,256},{256,320},{320,384},{384,448},... | collective-permute-start | bytes 786440 | tf_op jit(solution)/shard_map/while/body/eval_jaxpr/ppermute | solution.py:14
  150.8 3.2 collective-permute-done
  154.0 9.9 %collective-permute-start = (bf16[4,2,64,256]{3,2,0,1:T(8,128)(2,1)S(1)}, bf16[4,2,64,256]{3,2,0,1:T(8,128)(2,1)S(1)}, u32[]{:S(2)}, u32[]{:S(2)}) collective-permute-start(bf16[4,2,64,256]{3,2,0,1:T(8,128)(2,1)S(1)} %get-tuple-element.405), channel_id=1, source_target_pairs={{0,64},{64,128},{128,192},{192,256},{256,320},{320,384},{384,448},... | collective-permute-start | bytes 786440 | tf_op jit(solution)/shard_map/while/body/eval_jaxpr/ppermute | solution.py:14
  164.1 3.2 collective-permute-done
  167.3 19.5 %collective-permute-start = (bf16[4,2,64,256]{3,2,0,1:T(8,128)(2,1)S(1)}, bf16[4,2,64,256]{3,2,0,1:T(8,128)(2,1)S(1)}, u32[]{:S(2)}, u32[]{:S(2)}) collective-permute-start(bf16[4,2,64,256]{3,2,0,1:T(8,128)(2,1)S(1)} %get-tuple-element.405), channel_id=1, source_target_pairs={{0,64},{64,128},{128,192},{192,256},{256,320},{320,384},{384,448},... | collective-permute-start | bytes 786440 | tf_op jit(solution)/shard_map/while/body/eval_jaxpr/ppermute | solution.py:14
  186.9 3.2 collective-permute-done
  190.1 0.9 multiply_reduce_fusion
  191.0 1.1 multiply_reduce_fusion.1
  192.0 0.9 multiply_reduce_fusion.2
  192.9 0.4 multiply_reduce_fusion.3
  194.6 0.7 stack.195
  195.3 0.7 stack.196
  195.9 0.7 stack.200
  196.6 0.7 stack.201
  197.3 0.7 stack.202
  197.9 0.7 stack.171
  198.6 0.7 stack.187
  199.2 0.7 stack.197
  199.9 0.7 stack.198
  200.6 0.7 stack.199
  201.2 5.7 stack.203
  206.9 1.5 broadcast_multiply_fusion
  208.5 475.4 %reduce-scatter.2.cloned.1.call-done = f32[32,1,256]{2,0,1:T(8,128)} async-done(((f32[32,64,256]{2,0,1:T(8,128)}), f32[32,1,256]{2,0,1:T(8,128)}) %reduce-scatter.2.cloned.1.call-update) | async-done | bytes 32784 | tf_op jit(solution)/shard_map/reduce_scatter | solution.py:95
  683.9 1.4 copy.17
  (105 shorter events, 6.9 us)
Async XLA Ops:
  6.5 677.3 %reduce-scatter.2.cloned.1.call-start = ((), (), s32[]{:S(2)}) async-start(), calls=%async_computation.1 | async-start | bytes 2129920 | tf_op jit(solution)/shard_map/reduce_scatter | solution.py:95
  9.7 5.1 copy-start.3
  9.7 5.1 copy-start.2
  9.7 5.1 copy-start.1
  16.3 2.2 copy-start
  23.3 4.6 collective-permute-start
  28.0 15.3 %collective-permute-start = (bf16[4,2,64,256]{3,2,0,1:T(8,128)(2,1)S(1)}, bf16[4,2,64,256]{3,2,0,1:T(8,128)(2,1)S(1)}, u32[]{:S(2)}, u32[]{:S(2)}) collective-permute-start(bf16[4,2,64,256]{3,2,0,1:T(8,128)(2,1)S(1)} %get-tuple-element.405), channel_id=1, source_target_pairs={{0,64},{64,128},{128,192},{192,256},{256,320},{320,384},{384,448},... | collective-permute-start | bytes 786440 | tf_op jit(solution)/shard_map/while/body/eval_jaxpr/ppermute | solution.py:14
  43.3 7.1 %collective-permute-start = (bf16[4,2,64,256]{3,2,0,1:T(8,128)(2,1)S(1)}, bf16[4,2,64,256]{3,2,0,1:T(8,128)(2,1)S(1)}, u32[]{:S(2)}, u32[]{:S(2)}) collective-permute-start(bf16[4,2,64,256]{3,2,0,1:T(8,128)(2,1)S(1)} %get-tuple-element.405), channel_id=1, source_target_pairs={{0,64},{64,128},{128,192},{192,256},{256,320},{320,384},{384,448},... | collective-permute-start | bytes 786440 | tf_op jit(solution)/shard_map/while/body/eval_jaxpr/ppermute | solution.py:14
  50.5 15.7 %collective-permute-start = (bf16[4,2,64,256]{3,2,0,1:T(8,128)(2,1)S(1)}, bf16[4,2,64,256]{3,2,0,1:T(8,128)(2,1)S(1)}, u32[]{:S(2)}, u32[]{:S(2)}) collective-permute-start(bf16[4,2,64,256]{3,2,0,1:T(8,128)(2,1)S(1)} %get-tuple-element.405), channel_id=1, source_target_pairs={{0,64},{64,128},{128,192},{192,256},{256,320},{320,384},{384,448},... | collective-permute-start | bytes 786440 | tf_op jit(solution)/shard_map/while/body/eval_jaxpr/ppermute | solution.py:14
  66.3 7.1 %collective-permute-start = (bf16[4,2,64,256]{3,2,0,1:T(8,128)(2,1)S(1)}, bf16[4,2,64,256]{3,2,0,1:T(8,128)(2,1)S(1)}, u32[]{:S(2)}, u32[]{:S(2)}) collective-permute-start(bf16[4,2,64,256]{3,2,0,1:T(8,128)(2,1)S(1)} %get-tuple-element.405), channel_id=1, source_target_pairs={{0,64},{64,128},{128,192},{192,256},{256,320},{320,384},{384,448},... | collective-permute-start | bytes 786440 | tf_op jit(solution)/shard_map/while/body/eval_jaxpr/ppermute | solution.py:14
  73.5 16.4 %collective-permute-start = (bf16[4,2,64,256]{3,2,0,1:T(8,128)(2,1)S(1)}, bf16[4,2,64,256]{3,2,0,1:T(8,128)(2,1)S(1)}, u32[]{:S(2)}, u32[]{:S(2)}) collective-permute-start(bf16[4,2,64,256]{3,2,0,1:T(8,128)(2,1)S(1)} %get-tuple-element.405), channel_id=1, source_target_pairs={{0,64},{64,128},{128,192},{192,256},{256,320},{320,384},{384,448},... | collective-permute-start | bytes 786440 | tf_op jit(solution)/shard_map/while/body/eval_jaxpr/ppermute | solution.py:14
  90.0 7.1 %collective-permute-start = (bf16[4,2,64,256]{3,2,0,1:T(8,128)(2,1)S(1)}, bf16[4,2,64,256]{3,2,0,1:T(8,128)(2,1)S(1)}, u32[]{:S(2)}, u32[]{:S(2)}) collective-permute-start(bf16[4,2,64,256]{3,2,0,1:T(8,128)(2,1)S(1)} %get-tuple-element.405), channel_id=1, source_target_pairs={{0,64},{64,128},{128,192},{192,256},{256,320},{320,384},{384,448},... | collective-permute-start | bytes 786440 | tf_op jit(solution)/shard_map/while/body/eval_jaxpr/ppermute | solution.py:14
  97.2 16.1 %collective-permute-start = (bf16[4,2,64,256]{3,2,0,1:T(8,128)(2,1)S(1)}, bf16[4,2,64,256]{3,2,0,1:T(8,128)(2,1)S(1)}, u32[]{:S(2)}, u32[]{:S(2)}) collective-permute-start(bf16[4,2,64,256]{3,2,0,1:T(8,128)(2,1)S(1)} %get-tuple-element.405), channel_id=1, source_target_pairs={{0,64},{64,128},{128,192},{192,256},{256,320},{320,384},{384,448},... | collective-permute-start | bytes 786440 | tf_op jit(solution)/shard_map/while/body/eval_jaxpr/ppermute | solution.py:14
  113.4 21.3 %collective-permute-start = (bf16[4,2,64,256]{3,2,0,1:T(8,128)(2,1)S(1)}, bf16[4,2,64,256]{3,2,0,1:T(8,128)(2,1)S(1)}, u32[]{:S(2)}, u32[]{:S(2)}) collective-permute-start(bf16[4,2,64,256]{3,2,0,1:T(8,128)(2,1)S(1)} %get-tuple-element.405), channel_id=1, source_target_pairs={{0,64},{64,128},{128,192},{192,256},{256,320},{320,384},{384,448},... | collective-permute-start | bytes 786440 | tf_op jit(solution)/shard_map/while/body/eval_jaxpr/ppermute | solution.py:14
  134.8 19.2 %collective-permute-start = (bf16[4,2,64,256]{3,2,0,1:T(8,128)(2,1)S(1)}, bf16[4,2,64,256]{3,2,0,1:T(8,128)(2,1)S(1)}, u32[]{:S(2)}, u32[]{:S(2)}) collective-permute-start(bf16[4,2,64,256]{3,2,0,1:T(8,128)(2,1)S(1)} %get-tuple-element.405), channel_id=1, source_target_pairs={{0,64},{64,128},{128,192},{192,256},{256,320},{320,384},{384,448},... | collective-permute-start | bytes 786440 | tf_op jit(solution)/shard_map/while/body/eval_jaxpr/ppermute | solution.py:14
  154.0 13.2 %collective-permute-start = (bf16[4,2,64,256]{3,2,0,1:T(8,128)(2,1)S(1)}, bf16[4,2,64,256]{3,2,0,1:T(8,128)(2,1)S(1)}, u32[]{:S(2)}, u32[]{:S(2)}) collective-permute-start(bf16[4,2,64,256]{3,2,0,1:T(8,128)(2,1)S(1)} %get-tuple-element.405), channel_id=1, source_target_pairs={{0,64},{64,128},{128,192},{192,256},{256,320},{320,384},{384,448},... | collective-permute-start | bytes 786440 | tf_op jit(solution)/shard_map/while/body/eval_jaxpr/ppermute | solution.py:14
  167.3 22.8 %collective-permute-start = (bf16[4,2,64,256]{3,2,0,1:T(8,128)(2,1)S(1)}, bf16[4,2,64,256]{3,2,0,1:T(8,128)(2,1)S(1)}, u32[]{:S(2)}, u32[]{:S(2)}) collective-permute-start(bf16[4,2,64,256]{3,2,0,1:T(8,128)(2,1)S(1)} %get-tuple-element.405), channel_id=1, source_target_pairs={{0,64},{64,128},{128,192},{192,256},{256,320},{320,384},{384,448},... | collective-permute-start | bytes 786440 | tf_op jit(solution)/shard_map/while/body/eval_jaxpr/ppermute | solution.py:14
Sparse Core Ops, SparseCore 0:
  208.6 475.1 reduce-scatter.1
where the time goes:
time: 697 us; the launch traced here: 692 us
  waiting for transfers between devices  519 us (74%)
  starting transfers between devices  121 us (17%)
  local copies, waits for them, and re-layouts  20.8 us (3%)
  between operations  13.7 us (2%)
  matrix products  9.95 us (1%)
    reduce_scatter x1, waiting for transfers between devices, body(): lax.psum_scatter(partial_value, 'freq', scatter_dimension=1, tiled=True)  475 us
    ppermute x12, starting transfers between devices, passed_along(): return lax.ppermute(block, axis, route)  121 us
    ppermute x12, waiting for transfers between devices, passed_along(): return lax.ppermute(block, axis, route)  43.7 us
  transfers between devices with their start and end apart: 13, of which 13 were waited for; matrix products, arithmetic and copies ran while one was open for 0% of the time, Pallas kernels for 0%

commit v1 on v0

v1 whole, which is shorter than its diff:
```python
import math

import jax
import jax.numpy as jnp
import numpy as np
from jax import lax
from jax.experimental import pallas as pl
from jax.experimental.pallas import tpu as pltpu
from jax.sharding import Mesh
from jax.sharding import PartitionSpec as P

H = 32
REACH = H // 2
NX = 64
NY = 256
HALF = 128
R = 4
TAPS = 25
MID = TAPS // 2
GROUP = 4

DEPTH = ("zh", "x")
FREQ = ("y", "zl", "core")


def tap_rows(table):
    first, second = table[:, 0], table[:, 1]

    def gap(n):
        return jnp.zeros((R, 1, n), jnp.float32)

    rows = []
    for a, b in ((first[:, 0:1], -first[:, 1:2]), (first[:, 1:2], first[:, 0:1])):
        rows.append(
            jnp.concatenate([a[..., MID:], gap(39), b, gap(39), a[..., :MID]], axis=-1)
        )
    rows_first = jnp.concatenate(rows, axis=1).reshape(R * 2, HALF)
    back = second[..., ::-1]
    rows_second = jnp.concatenate(
        [back[..., MID:], jnp.zeros((R, 2, NY - TAPS), jnp.float32), back[..., :MID]], axis=-1
    ).reshape(R * 2, NY)
    return rows_first, rows_second


def pick(masks, values):
    out = values[R - 1]
    for region in range(R - 2, -1, -1):
        out = jnp.where(masks[region], values[region], out)
    return out


def chain_kernel(count_ref, rows_first_ref, rows_second_ref, surface_ref, regions_ref, out_ref, band_first, band_second, state):
    def fan(row, height):
        wide = jnp.broadcast_to(row, (height, row.shape[-1]))
        return pltpu.roll(wide, 0, 1, stride=1, stride_axis=0)

    row_at = lax.broadcasted_iota(jnp.int32, (NX, HALF), 0)
    lane_at = lax.broadcasted_iota(jnp.int32, (NX, HALF), 1)
    near = jnp.abs((lane_at & (NX - 1)) - row_at) <= MID
    for block in range(R * 2):
        band = fan(rows_first_ref[block : block + 1, :], NX)
        band_first[block * NX : (block + 1) * NX, :] = jnp.where(near, band, 0.0).astype(jnp.bfloat16)

    row_at = lax.broadcasted_iota(jnp.int32, (NY, NY), 0)
    lane_at = lax.broadcasted_iota(jnp.int32, (NY, NY), 1)
    near = jnp.abs(lane_at - row_at) <= MID
    for region in range(R):
        for part in range(2):
            block = region * 2 + part
            band = fan(rows_second_ref[block : block + 1, :], NY)
            band = jnp.where(near, band, 0.0)
            plain = band.astype(jnp.bfloat16)
            for half in range(2):
                cut = plain[:, half * HALF : (half + 1) * HALF]

                def lanes(part_out):
                    start = ((part_out * 2 + half) * R + region) * HALF
                    return slice(start, start + HALF)

                if part == 0:
                    band_second[:NY, lanes(0)] = cut
                    band_second[NY:, lanes(1)] = cut
                else:
                    band_second[NY:, lanes(0)] = -cut
                    band_second[:NY, lanes(1)] = cut

    state[:NX, :] = surface_ref[0]
    state[NX:, :] = surface_ref[1]
    count = count_ref[0]

    def step(t, carry):
        region = regions_ref[t].astype(jnp.float32)
        masks = [region == float(r) for r in range(R - 1)]
        field = jnp.dot(band_first[...], state[...], preferred_element_type=jnp.float32)
        between = []
        for part in range(2):
            values = [field[(r * 2 + part) * NX : (r * 2 + part + 1) * NX] for r in range(R)]
            between.append(pick(masks, values).astype(jnp.bfloat16))
        between = jnp.concatenate(between, axis=1)
        slot = jnp.maximum(t - (count - GROUP), 0)
        for half in range(2):
            cut = [m[:, half * HALF : (half + 1) * HALF] for m in masks]
            for part in range(2):
                start = (part * 2 + half) * R * HALF
                wide = jnp.dot(
                    between,
                    band_second[:, start : start + R * HALF],
                    preferred_element_type=jnp.float32,
                )
                values = [wide[:, r * HALF : (r + 1) * HALF] for r in range(R)]
                leaving = pick(cut, values).astype(jnp.bfloat16)
                state[part * NX : (part + 1) * NX, half * HALF : (half + 1) * HALF] = leaving
                out_ref[slot * 2 + half, part] = leaving
        return carry

    lax.fori_loop(0, count, step, 0)


def image_kernel(scale, wave_ref, mine_ref, other_ref, core_ref, out_ref, wave, src):
    edge = jnp.zeros((4, 2, REACH, HALF), jnp.float32)
    mine = core_ref[0]
    for core in range(2):
        for ref in (wave, src):
            ref[core, :, :, :REACH, :] = edge
            ref[core, :, :, REACH + NX :, :] = edge
        for f in range(GROUP):
            wave[core, f, :, REACH : REACH + NX, :] = wave_ref[f * 2 + core].astype(jnp.float32)
    src[mine, :, :, REACH : REACH + NX, :] = mine_ref[...].astype(jnp.float32)
    src[1 - mine, :, :, REACH : REACH + NX, :] = other_ref[...].astype(jnp.float32)

    def row(x, carry):
        total = jnp.zeros((H, HALF), jnp.float32)
        for core in range(2):
            for f in range(GROUP):
                for part in range(2):
                    total = total + wave[core, f, part, pl.ds(x, H), :] * src[core, f, part, pl.ds(NX - 1 - x, H), :]
        out_ref[x] = (total * scale).astype(jnp.bfloat16)
        return carry

    lax.fori_loop(0, NX, row, 0)


def sum_kernel(part_ref, out_ref):
    groups = part_ref.shape[0] // 2
    for core in range(2):
        def add(i, total):
            return total + part_ref[2 * i + core].astype(jnp.float32)

        total = lax.fori_loop(0, groups, add, jnp.zeros((H, HALF), jnp.float32), unroll=True)
        out_ref[:, core * HALF : (core + 1) * HALF] = total


VMEM = pl.BlockSpec(memory_space=pltpu.VMEM)
SMEM = pl.BlockSpec(memory_space=pltpu.SMEM)


def body(surface, regions, table, source):
    zh = lax.axis_index("zh")
    mine_x = lax.axis_index("x")
    core = lax.axis_index("core")
    depths = lax.axis_size("zh") * lax.axis_size("x")

    local = regions[0].astype(jnp.bfloat16)
    all_regions = lax.all_to_all(
        jnp.broadcast_to(local[None], (depths, NX, NY)), DEPTH, 0, 0, tiled=True
    )

    flipped = source[0][:, :, ::-1, :]
    low, high = flipped[..., :HALF], flipped[..., HALF:]
    kept = jnp.where(core == 0, low, high)
    given = jnp.where(core == 0, high, low)
    other = lax.ppermute(given, "core", [(0, 1), (1, 0)])

    rows_first, rows_second = tap_rows(
        lax.dynamic_index_in_dim(table, mine_x, 0, keepdims=False).astype(jnp.float32)
    )
    entering = lax.dynamic_index_in_dim(surface, mine_x, 0, keepdims=False)
    count = ((zh + 1) * GROUP).astype(jnp.int32).reshape(1)

    waves = pl.pallas_call(
        chain_kernel,
        out_shape=jax.ShapeDtypeStruct((GROUP * 2, 2, NX, HALF), jnp.bfloat16),
        in_specs=[SMEM, VMEM, VMEM, VMEM, VMEM],
        out_specs=VMEM,
        scratch_shapes=[
            pltpu.VMEM((R * 2 * NX, 2 * NX), jnp.bfloat16),
            pltpu.VMEM((2 * NY, R * 2 * NY), jnp.bfloat16),
            pltpu.VMEM((2 * NX, NY), jnp.bfloat16),
        ],
        compiler_params=pltpu.CompilerParams(vmem_limit_bytes=24 << 20),
        cost_estimate=pl.CostEstimate(flops=4_000_000_000, bytes_accessed=4_000_000, transcendentals=0),
        name="chain",
    )(count, rows_first, rows_second, entering, all_regions)

    waves = lax.all_to_all(waves, ("x", "core"), 0, 0, tiled=True)

    scale = 1.0 / math.sqrt(surface.shape[0] * lax.axis_size(FREQ))
    partial_image = pl.pallas_call(
        lambda *refs: image_kernel(scale, *refs),
        out_shape=jax.ShapeDtypeStruct((NX, H, HALF), jnp.bfloat16),
        in_specs=[VMEM, VMEM, VMEM, SMEM],
        out_specs=VMEM,
        scratch_shapes=[
            pltpu.VMEM((2, GROUP, 2, NX + H, HALF), jnp.float32),
            pltpu.VMEM((2, GROUP, 2, NX + H, HALF), jnp.float32),
        ],
        compiler_params=pltpu.CompilerParams(vmem_limit_bytes=24 << 20),
        cost_estimate=pl.CostEstimate(flops=10_000_000, bytes_accessed=2_000_000, transcendentals=0),
        name="image",
    )(waves, kept, other, core.astype(jnp.int32).reshape(1))

    parts = lax.all_to_all(partial_image, FREQ, 0, 0, tiled=True)

    mine = pl.pallas_call(
        sum_kernel,
        out_shape=jax.ShapeDtypeStruct((H, NY), jnp.float32),
        in_specs=[VMEM],
        out_specs=VMEM,
        compiler_params=pltpu.CompilerParams(vmem_limit_bytes=24 << 20),
        name="total",
    )(parts)
    return mine[None, :, None, :]


def solution(mesh):
    wide = Mesh(np.asarray(mesh.devices).reshape(3, 4, 8, 4, 2), ("zh", "x", "y", "zl", "core"))
    in_specs = (
        P(FREQ, None, None, None),
        P(DEPTH, None, None),
        P(FREQ, None, None, None, None),
        P(DEPTH, FREQ, None, None, None),
    )
    out_specs = P(DEPTH, None, FREQ, None)
    return jax.shard_map(body, mesh=wide, in_specs=in_specs, out_specs=out_specs, check_vma=False)
```

time: 697 us -> 87 us (0.12)
  waiting for transfers between devices: 519 us -> 15.4 us
  starting transfers between devices: 121 us -> 28 us
  blocking collectives: 0 us -> 32.3 us
  local copies, waits for them, and re-layouts: 20.8 us -> 2.27 us
  between operations: 13.7 us -> 0.13 us
  matrix products: 9.95 us -> 0 us
    reduce_scatter x1 -> x0, waiting for transfers between devices: 475 us -> none  [body(): lax.psum_scatter(partial_value, 'freq', scatter_dimension=1, tiled=True)]
    ppermute x12 -> x1, starting transfers between devices: 121 us -> 2.03 us  [body(): other = lax.ppermute(given, 'core', [(0, 1), (1, 0)])]
    ppermute x12 -> x1, waiting for transfers between devices: 43.7 us -> 1.21 us  [body(): other = lax.ppermute(given, 'core', [(0, 1), (1, 0)])]
    all_to_all x0 -> x1, blocking collectives: none -> 32.3 us  [body(): parts = lax.all_to_all(partial_image, FREQ, 0, 0, tiled=True)]
    all_to_all x0 -> x2, starting transfers between devices: none -> 26 us  [the longest x1 17.1 us: body(): lax.all_to_all(jnp.broadcast_to(local[None], (depths, NX, NY)), DEPTH, 0,...]
    all_to_all x0 -> x2, waiting for transfers between devices: none -> 14.2 us  [the longest x1 10.9 us: body(): lax.all_to_all(jnp.broadcast_to(local[None], (depths, NX, NY)), DEPTH, 0,...]
    another operation x45 -> x1, local copies, waits for them, and re-layouts: 13.6 us -> 0.01 us  [the longest x33 13.4 us: offset_image(): return jnp.stack(images)]
    dot_general x34 -> x0, matrix products: 9.95 us -> none  [the longest x16 4.57 us: product(): jnp.einsum('bxk,byk->bxy', signal, band, preferred_element_type=jnp.float32)]
  transfers between devices with their start and end apart: 13 -> 3, of which waited for: 13 -> 3; matrix products, arithmetic and copies ran while one was open for 0% -> 2% of each run, Pallas kernels for 0% -> 0%
where the time goes in v1:
time: 87 us; the launch traced here: 86.6 us
  blocking collectives  32.3 us (37%)
  starting transfers between devices  28 us (32%)
  waiting for transfers between devices  15.4 us (18%)
  Pallas kernels  6.82 us (8%)
  local copies, waits for them, and re-layouts  2.27 us (3%)
  other arithmetic  1.7 us (2%)
    all_to_all x1, blocking collectives, body(): parts = lax.all_to_all(partial_image, FREQ, 0, 0, tiled=True)  32.3 us
    all_to_all x1, starting transfers between devices, body(): lax.all_to_all(jnp.broadcast_to(local[None], (depths, NX, NY)), DEPTH, 0,...  17.1 us
    all_to_all x1, waiting for transfers between devices, body(): lax.all_to_all(jnp.broadcast_to(local[None], (depths, NX, NY)), DEPTH, 0,...  10.9 us
    all_to_all x1, starting transfers between devices, body(): waves = lax.all_to_all(waves, ('x', 'core'), 0, 0, tiled=True)  8.9 us
    pallas_call x1, Pallas kernels, body(): pl.pallas_call(chain_kernel, out_shape=jax.ShapeDtypeStruct((GROUP * 2, 2...  4.22 us
    all_to_all x1, waiting for transfers between devices, body(): waves = lax.all_to_all(waves, ('x', 'core'), 0, 0, tiled=True)  3.25 us
    pallas_call x1, Pallas kernels, body(): pl.pallas_call(lambda *refs: image_kernel(scale, *refs), out_shape=jax.Sh...  2.52 us
    ppermute x1, starting transfers between devices, body(): other = lax.ppermute(given, 'core', [(0, 1), (1, 0)])  2.03 us
  transfers between devices with their start and end apart: 3, of which 3 were waited for; matrix products, arithmetic and copies ran while one was open for 2% of the time, Pallas kernels for 0%

profile of v1, /device:TPU:1, one launch (start us, length us, event | category | flops | bytes accessed | tf_op | source)
XLA Modules:
  0.0 86.6 jit_solution(6212006175738163529)
XLA Ops:
  0.0 0.0 copy-start
  0.0 0.9 %convert_bitcast_fusion = bf16[64,256]{1,0:T(8,128)(2,1)S(1)} fusion(s32[1,64,256]{2,1,0:T(8,128)} %param.5), kind=kLoop, calls=%fused_computation.3 | loop fusion | flops 16384 | bytes 98304 | tf_op jit(solution)/shard_map/broadcast_in_dim | solution.py:165
  0.9 0.8 broadcast_in_dim.16
  1.7 0.0 copy-start.1
  1.7 17.1 %all-to-all-start = ((bf16[12,64,256]{2,1,0:T(8,128)(2,1)}), bf16[12,64,256]{2,1,0:T(8,128)(2,1)S(1)}, u32[]{:S(2)}, u32[]{:S(2)}) async-start(bf16[12,64,256]{2,1,0:T(8,128)(2,1)} %broadcast_in_dim.16), calls=%async_computation | async-start | bytes 786432 | tf_op jit(solution)/shard_map/all_to_all | solution.py:164
  18.8 0.7 bitcast_convert_fusion
  19.5 0.1 slice.79
  19.6 0.1 slice.65
  19.7 0.1 slice.63
  19.8 0.1 pad.1.clone
  19.8 0.1 pad_maximum_fusion
  19.9 0.0 copy-done.1
  19.9 0.1 fusion
  20.0 0.1 slice.67
  20.1 0.1 slice.69
  20.2 0.1 fusion.2
  20.2 0.1 concatenate.12
  20.3 0.1 concatenate.13
  20.5 0.0 copy-done
  20.5 10.9 %all-to-all-done.regions_ref = bf16[12,64,256]{2,1,0:T(8,128)(2,1)S(1)} async-done(((bf16[12,64,256]{2,1,0:T(8,128)(2,1)}), bf16[12,64,256]{2,1,0:T(8,128)(2,1)S(1)}, u32[]{:S(2)}, u32[]{:S(2)}) %all-to-all-start) | async-done | bytes 393248 | tf_op jit(solution)/shard_map/all_to_all | solution.py:164
  31.4 4.2 %chain.1 = bf16[8,2,64,128]{3,2,1,0:T(8,128)(2,1)} custom-call(s32[1]{0:T(128)} %bitcast.count_ref, f32[8,128]{1,0:T(8,128)S(1)} %bitcast.18, f32[8,256]{1,0:T(8,128)S(1)} %reshape.16.rows_second_ref, bf16[2,64,256]{2,1,0:T(8,128)(2,1)S(1)} %dynamic-slice_bitcast_fusion.surface_ref, bf16[12,64,256]{2,1,0:T(8,128)(2,1)S(1)} %all-to-all-done.regions_ref), custom_call_target="tpu_custom_call" | custom-call | flops 4000000000 | bytes 4000000 | tf_op jit(solution)/shard_map/chain/pallas_call | solution.py:180
  35.6 8.9 %all-to-all-start.1 = ((bf16[8,2,64,128]{3,2,1,0:T(8,128)(2,1)}), bf16[8,2,64,128]{3,2,1,0:T(8,128)(2,1)S(1)}, u32[]{:S(2)}, u32[]{:S(2)}) async-start(bf16[8,2,64,128]{3,2,1,0:T(8,128)(2,1)} %chain.1), calls=%async_computation.1 | async-start | bytes 524288 | tf_op jit(solution)/shard_map/all_to_all | solution.py:195
  44.6 2.0 %collective-permute-start = (bf16[4,2,64,128]{3,2,1,0:T(8,128)(2,1)S(1)}, bf16[4,2,64,128]{3,2,1,0:T(8,128)(2,1)S(1)}, u32[]{:S(2)}, u32[]{:S(2)}) collective-permute-start(bf16[4,2,64,128]{3,2,1,0:T(8,128)(2,1)S(1)} %get-tuple-element.5), channel_id=1, source_target_pairs={{0,1},{1,0},{2,3},{3,2},{4,5},{5,4},{6,7},{7,6},{8,9},{9,8},{10,11... | collective-permute-start | bytes 393224 | tf_op jit(solution)/shard_map/ppermute | solution.py:172
  46.6 1.2 %collective-permute-done.refs_2_ = bf16[4,2,64,128]{3,2,1,0:T(8,128)(2,1)S(1)} collective-permute-done((bf16[4,2,64,128]{3,2,1,0:T(8,128)(2,1)S(1)}, bf16[4,2,64,128]{3,2,1,0:T(8,128)(2,1)S(1)}, u32[]{:S(2)}, u32[]{:S(2)}) %collective-permute-start) | collective-permute-done | bytes 131104 | tf_op jit(solution)/shard_map/ppermute | solution.py:172
  47.8 3.3 %all-to-all-done.1.refs_0_ = bf16[8,2,64,128]{3,2,1,0:T(8,128)(2,1)S(1)} async-done(((bf16[8,2,64,128]{3,2,1,0:T(8,128)(2,1)}), bf16[8,2,64,128]{3,2,1,0:T(8,128)(2,1)S(1)}, u32[]{:S(2)}, u32[]{:S(2)}) %all-to-all-start.1) | async-done | bytes 262176 | tf_op jit(solution)/shard_map/all_to_all | solution.py:195
  51.1 2.5 %image.1 = bf16[64,32,128]{2,1,0:T(8,128)(2,1)S(1)} custom-call(bf16[8,2,64,128]{3,2,1,0:T(8,128)(2,1)S(1)} %all-to-all-done.1.refs_0_, bf16[4,2,64,128]{3,2,1,0:T(8,128)(2,1)S(1)} %get-tuple-element.6.refs_1_, bf16[4,2,64,128]{3,2,1,0:T(8,128)(2,1)S(1)} %collective-permute-done.refs_2_, s32[1]{0:T(128)} %bitcast.9.refs_3_), custom_call_target="tpu_custom_call" | custom-call | flops 10000000 | bytes 2000000 | tf_op jit(solution)/shard_map/image/pallas_call | solution.py:198
  53.6 32.3 %all_to_all.15.part_ref = bf16[64,32,128]{2,1,0:T(8,128)(2,1)S(1)} all-to-all(bf16[64,32,128]{2,1,0:T(8,128)(2,1)S(1)} %image.1), channel_id=1, replica_groups=mesh['zh'=3,'x'=4,'y'=8,'zl'=4,'core'=2] {'y','zl','core'}, dimensions={0} | all-to-all | bytes 1048576 | tf_op jit(solution)/shard_map/all_to_all | solution.py:212
  85.8 0.1 total.1
  85.9 0.6 copy.5
  (9 shorter events, 0.1 us)
Async XLA Ops:
  0.0 20.5 %copy-start = (bf16[4,2,64,256]{3,2,1,0:T(8,128)(2,1)S(1)}, bf16[4,2,64,256]{3,2,1,0:T(8,128)(2,1)}, u32[]{:S(2)}) copy-start(bf16[4,2,64,256]{3,2,1,0:T(8,128)(2,1)} %param.4) | copy-start | bytes 786436
  1.7 18.3 %copy-start.1 = (bf16[1,4,2,64,256]{4,3,2,1,0:T(8,128)(2,1)S(1)}, bf16[1,4,2,64,256]{4,3,2,1,0:T(8,128)(2,1)}, u32[]{:S(2)}) copy-start(bf16[1,4,2,64,256]{4,3,2,1,0:T(8,128)(2,1)} %param.7) | copy-start | bytes 786436
  1.7 29.7 %all-to-all-start = ((bf16[12,64,256]{2,1,0:T(8,128)(2,1)}), bf16[12,64,256]{2,1,0:T(8,128)(2,1)S(1)}, u32[]{:S(2)}, u32[]{:S(2)}) async-start(bf16[12,64,256]{2,1,0:T(8,128)(2,1)} %broadcast_in_dim.16), calls=%async_computation | async-start | bytes 786432 | tf_op jit(solution)/shard_map/all_to_all | solution.py:164
  35.6 15.4 %all-to-all-start.1 = ((bf16[8,2,64,128]{3,2,1,0:T(8,128)(2,1)}), bf16[8,2,64,128]{3,2,1,0:T(8,128)(2,1)S(1)}, u32[]{:S(2)}, u32[]{:S(2)}) async-start(bf16[8,2,64,128]{3,2,1,0:T(8,128)(2,1)} %chain.1), calls=%async_computation.1 | async-start | bytes 524288 | tf_op jit(solution)/shard_map/all_to_all | solution.py:195
  44.6 3.2 %collective-permute-start = (bf16[4,2,64,128]{3,2,1,0:T(8,128)(2,1)S(1)}, bf16[4,2,64,128]{3,2,1,0:T(8,128)(2,1)S(1)}, u32[]{:S(2)}, u32[]{:S(2)}) collective-permute-start(bf16[4,2,64,128]{3,2,1,0:T(8,128)(2,1)S(1)} %get-tuple-element.5), channel_id=1, source_target_pairs={{0,1},{1,0},{2,3},{3,2},{4,5},{5,4},{6,7},{7,6},{8,9},{9,8},{10,11... | collective-permute-start | bytes 393224 | tf_op jit(solution)/shard_map/ppermute | solution.py:172

commit v2 on v1

v2 whole, which is shorter than its diff:
```python
import math

import jax
import jax.numpy as jnp
import numpy as np
from jax import lax
from jax.experimental import pallas as pl
from jax.experimental.pallas import tpu as pltpu
from jax.sharding import Mesh
from jax.sharding import PartitionSpec as P

H = 32
REACH = H // 2
NX = 64
NY = 256
LANES = 128
QUARTER = 64
R = 4
TAPS = 25
MID = TAPS // 2
GROUP = 4

AXES = ("zh", "x", "y", "zq", "zp", "core")
DEPTH = ("zh", "x")
FREQ = ("y", "zq", "zp", "core")
QUAD = ("zp", "core")


def tap_rows(table):
    first, second = table[:, 0], table[:, 1]

    def gap(n):
        return jnp.zeros((R, 1, n), jnp.float32)

    rows = []
    for a, b in ((first[:, 0:1], -first[:, 1:2]), (first[:, 1:2], first[:, 0:1])):
        rows.append(
            jnp.concatenate([a[..., MID:], gap(39), b, gap(39), a[..., :MID]], axis=-1)
        )
    rows_first = jnp.concatenate(rows, axis=1).reshape(R * 2, LANES)
    back = second[..., ::-1]
    rows_second = jnp.concatenate(
        [back[..., MID:], jnp.zeros((R, 2, LANES - TAPS), jnp.float32), back[..., :MID]], axis=-1
    ).reshape(R * 2, LANES)
    return rows_first, rows_second


def fan(row, height, shift):
    wide = jnp.broadcast_to(row, (height, row.shape[-1]))
    return pltpu.roll(wide, shift, 1, stride=1, stride_axis=0)


def bands_kernel(rows_first_ref, rows_second_ref, band_first, band_even, band_odd):
    row_at = lax.broadcasted_iota(jnp.int32, (NX, LANES), 0)
    lane_at = lax.broadcasted_iota(jnp.int32, (NX, LANES), 1)
    near = jnp.abs((lane_at & (NX - 1)) - row_at) <= MID
    for block in range(R * 2):
        band = fan(rows_first_ref[block : block + 1, :], NX, 0)
        band_first[block * NX : (block + 1) * NX, :] = jnp.where(near, band, 0.0).astype(jnp.bfloat16)

    left = lax.broadcasted_iota(jnp.int32, (LANES, LANES), 1) < QUARTER
    for region in range(R):
        tap_real = rows_second_ref[2 * region : 2 * region + 1, :]
        tap_imag = rows_second_ref[2 * region + 1 : 2 * region + 2, :]
        cols = slice(region * LANES, (region + 1) * LANES)
        for part, (to_real, to_imag) in enumerate(((tap_real, tap_imag), (-tap_imag, tap_real))):
            rows = slice(part * LANES, (part + 1) * LANES)
            real_band = fan(to_real, LANES, 0)
            imag_band = fan(to_imag, LANES, QUARTER)
            band_even[rows, cols] = jnp.where(left, real_band, imag_band).astype(jnp.bfloat16)
            band_odd[rows, cols] = jnp.where(left, imag_band, real_band).astype(jnp.bfloat16)


def pick(masks, values):
    out = values[R - 1]
    for region in range(R - 2, -1, -1):
        out = jnp.where(masks[region], values[region], out)
    return out


def chain_kernel(scalar_ref, band_first, band_even, band_odd, surface_ref, own_ref, swapped_ref, out_ref, state):
    state[:NX, :] = surface_ref[0]
    state[NX:, :] = surface_ref[1]
    core = scalar_ref[1]
    lane = lax.broadcasted_iota(jnp.int32, (NX, LANES), 1)
    left = lane < QUARTER
    low = lane < 96
    high = lane >= 32

    def split(values):
        return [values == float(r) for r in range(R - 1)]

    def step(t, slot):
        own = own_ref[t].astype(jnp.float32)
        swapped = swapped_ref[t].astype(jnp.float32)
        halves = [jnp.where(core == half, own, swapped) for half in range(2)]
        turned = [pltpu.roll(half, QUARTER, 1) for half in halves]
        full = split(jnp.concatenate(halves, axis=1))
        even_mask = split(jnp.concatenate([jnp.where(left, a, b) for a, b in zip(halves, turned)], axis=0))
        odd_mask = split(jnp.concatenate([jnp.where(left, b, a) for a, b in zip(halves, turned)], axis=0))

        field = jnp.dot(band_first[...], state[...], preferred_element_type=jnp.float32)
        even_in, odd_in = [], []
        for part in range(2):
            values = [field[(r * 2 + part) * NX : (r * 2 + part + 1) * NX] for r in range(R)]
            between = pick(full, values)
            a, b = between[:, :LANES], between[:, LANES:]
            even_in.append(jnp.concatenate([jnp.where(low, a, 0.0), jnp.where(low, b, a)], axis=0).astype(jnp.bfloat16))
            odd_in.append(jnp.concatenate([jnp.where(high, a, b), jnp.where(high, b, 0.0)], axis=0).astype(jnp.bfloat16))
        wide = jnp.dot(jnp.concatenate(even_in, axis=1), band_even[...], preferred_element_type=jnp.float32)
        even = pick(even_mask, [wide[:, r * LANES : (r + 1) * LANES] for r in range(R)])
        wide = jnp.dot(jnp.concatenate(odd_in, axis=1), band_odd[...], preferred_element_type=jnp.float32)
        odd = pick(odd_mask, [wide[:, r * LANES : (r + 1) * LANES] for r in range(R)])
        for half in range(2):
            rows = slice(half * NX, (half + 1) * NX)
            cols = slice(half * LANES, (half + 1) * LANES)
            e, o = even[rows], odd[rows]
            out_ref[slot * 4 + half * 2] = e.astype(jnp.bfloat16)
            out_ref[slot * 4 + half * 2 + 1] = o.astype(jnp.bfloat16)
            state[:NX, cols] = jnp.where(left, e, o).astype(jnp.bfloat16)
            state[NX:, cols] = pltpu.roll(jnp.where(left, o, e), QUARTER, 1).astype(jnp.bfloat16)

    def block(b, carry):
        for slot in range(GROUP):
            step(b * GROUP + slot, slot)
        return carry

    lax.fori_loop(0, scalar_ref[0], block, 0)


def pack_kernel(source_ref, out_ref):
    row_at = lax.broadcasted_iota(jnp.int32, (NX, NX), 0)
    col_at = lax.broadcasted_iota(jnp.int32, (NX, NX), 1)
    flip = (row_at + col_at == NX - 1).astype(jnp.bfloat16)
    left = lax.broadcasted_iota(jnp.int32, (NX, LANES), 1) < QUARTER
    for f in range(GROUP):
        real = jnp.dot(flip, source_ref[f, 0], preferred_element_type=jnp.float32)
        imag = jnp.dot(flip, source_ref[f, 1], preferred_element_type=jnp.float32)
        for half in range(2):
            cols = slice(half * LANES, (half + 1) * LANES)
            a = real[:, cols]
            b = pltpu.roll(imag[:, cols], QUARTER, 1)
            out_ref[half * 2, f] = jnp.where(left, a, b).astype(jnp.bfloat16)
            out_ref[half * 2 + 1, f] = jnp.where(left, b, a).astype(jnp.bfloat16)


def image_kernel(scale, wave_ref, source_ref, out_ref, wave, src):
    edge = jnp.zeros((4 * GROUP, REACH, LANES), jnp.float32)
    for ref in (wave, src):
        ref[:, :REACH, :] = edge
        ref[:, REACH + NX :, :] = edge
    for f in range(GROUP):
        for g in range(4):
            wave[f * 4 + g, REACH : REACH + NX, :] = wave_ref[f * 4 + g].astype(jnp.float32)
            src[f * 4 + g, REACH : REACH + NX, :] = source_ref[g, f].astype(jnp.float32)
    left = lax.broadcasted_iota(jnp.int32, (REACH, LANES), 1) < QUARTER

    def row(x, carry):
        total = jnp.zeros((H, LANES), jnp.float32)
        for i in range(4 * GROUP):
            total = total + wave[i, pl.ds(x, H), :] * src[i, pl.ds(NX - 1 - x, H), :]
        total = (total + pltpu.roll(total, QUARTER, 1)) * scale
        out_ref[x] = jnp.where(left, total[:REACH], total[REACH:]).astype(jnp.bfloat16)
        return carry

    lax.fori_loop(0, NX, row, 0, unroll=2)


def sum_kernel(part_ref, out_ref):
    groups = part_ref.shape[0] // 4
    left = lax.broadcasted_iota(jnp.int32, (REACH, LANES), 1) < QUARTER
    for half in range(2):
        totals = []
        for q in (2 * half, 2 * half + 1):
            total = part_ref[q].astype(jnp.float32)
            for i in range(1, groups):
                total = total + part_ref[4 * i + q].astype(jnp.float32)
            totals.append(total)
        a, b = totals
        cols = slice(half * LANES, (half + 1) * LANES)
        out_ref[:REACH, cols] = jnp.where(left, a, pltpu.roll(b, QUARTER, 1))
        out_ref[REACH:, cols] = jnp.where(left, pltpu.roll(a, QUARTER, 1), b)


VMEM = pl.BlockSpec(memory_space=pltpu.VMEM)
SMEM = pl.BlockSpec(memory_space=pltpu.SMEM)
PARAMS = pltpu.CompilerParams(vmem_limit_bytes=24 << 20)


def cost(flops, moved):
    return pl.CostEstimate(flops=flops, bytes_accessed=moved, transcendentals=0)


def body(surface, regions, table, source):
    zh = lax.axis_index("zh")
    mine_x = lax.axis_index("x")
    core = lax.axis_index("core")
    depths = lax.axis_size("zh") * lax.axis_size("x")
    swap = [(0, 1), (1, 0)]

    local = jnp.where(core == 0, regions[0, :, :LANES], regions[0, :, LANES:]).astype(jnp.bfloat16)
    own = lax.all_to_all(
        jnp.broadcast_to(local[None], (depths, NX, LANES)), DEPTH, 0, 0, tiled=True
    )
    swapped = lax.ppermute(own, "core", swap)

    packed = pl.pallas_call(
        pack_kernel,
        out_shape=jax.ShapeDtypeStruct((4, GROUP, NX, LANES), jnp.bfloat16),
        in_specs=[VMEM],
        out_specs=VMEM,
        compiler_params=PARAMS,
        cost_estimate=cost(20_000_000, 1_000_000),
        name="pack",
    )(source[0])
    sources = lax.all_to_all(packed, QUAD, 0, 0, tiled=True)

    rows_first, rows_second = tap_rows(
        lax.dynamic_index_in_dim(table, mine_x, 0, keepdims=False).astype(jnp.float32)
    )
    bands = pl.pallas_call(
        bands_kernel,
        out_shape=(
            jax.ShapeDtypeStruct((R * 2 * NX, LANES), jnp.bfloat16),
            jax.ShapeDtypeStruct((2 * LANES, R * LANES), jnp.bfloat16),
            jax.ShapeDtypeStruct((2 * LANES, R * LANES), jnp.bfloat16),
        ),
        in_specs=[VMEM] * 2,
        out_specs=(VMEM,) * 3,
        compiler_params=PARAMS,
        cost_estimate=cost(10_000_000, 1_000_000),
        name="bands",
    )(rows_first, rows_second)

    entering = lax.dynamic_index_in_dim(surface, mine_x, 0, keepdims=False)
    scalars = jnp.stack([zh + 1, core]).astype(jnp.int32)
    waves = pl.pallas_call(
        chain_kernel,
        out_shape=jax.ShapeDtypeStruct((GROUP * 4, NX, LANES), jnp.bfloat16),
        in_specs=[SMEM] + [VMEM] * 6,
        out_specs=VMEM,
        scratch_shapes=[pltpu.VMEM((2 * NX, NY), jnp.bfloat16)],
        compiler_params=PARAMS,
        cost_estimate=cost(4_000_000_000, 4_000_000),
        name="chain",
    )(scalars, *bands, entering, own, swapped)

    waves = lax.all_to_all(waves, ("x",) + QUAD, 0, 0, tiled=True)

    scale = 1.0 / math.sqrt(surface.shape[0] * lax.axis_size(FREQ))
    partial_image = pl.pallas_call(
        lambda *refs: image_kernel(scale, *refs),
        out_shape=jax.ShapeDtypeStruct((NX, REACH, LANES), jnp.bfloat16),
        in_specs=[VMEM, VMEM],
        out_specs=VMEM,
        scratch_shapes=[pltpu.VMEM((4 * GROUP, NX + H, LANES), jnp.float32)] * 2,
        compiler_params=PARAMS,
        cost_estimate=cost(10_000_000, 2_000_000),
        name="image",
    )(waves, sources)

    parts = lax.all_to_all(partial_image, FREQ, 0, 0, tiled=True)

    mine = pl.pallas_call(
        sum_kernel,
        out_shape=jax.ShapeDtypeStruct((H, NY), jnp.float32),
        in_specs=[VMEM],
        out_specs=VMEM,
        compiler_params=PARAMS,
        name="total",
    )(parts)
    return mine[None, :, None, :]


def solution(mesh):
    wide = Mesh(np.asarray(mesh.devices).reshape(3, 4, 8, 2, 2, 2), AXES)
    in_specs = (
        P(FREQ, None, None, None),
        P(DEPTH, None, None),
        P(FREQ, None, None, None, None),
        P(DEPTH, FREQ, None, None, None),
    )
    out_specs = P(DEPTH, None, FREQ, None)
    return jax.shard_map(body, mesh=wide, in_specs=in_specs, out_specs=out_specs, check_vma=False)
```

time: 87 us -> 83.7 us (0.962)
  waiting for transfers between devices: 15.4 us -> 8.31 us
  blocking collectives: 32.3 us -> 36.7 us
  starting transfers between devices: 28 us -> 25.4 us
  Pallas kernels: 6.82 us -> 9.04 us
    all_to_all x0 -> x1, blocking collectives: none -> 10.9 us  [body(): waves = lax.all_to_all(waves, ('x',) + QUAD, 0, 0, tiled=True)]
    all_to_all x2, waiting for transfers between devices: 14.2 us -> 7.03 us  [the longest x1 7.03 us: body(): lax.all_to_all(jnp.broadcast_to(local[None], (depths, NX, LANES)), DEPTH,...]
    all_to_all x1, blocking collectives: 32.3 us -> 25.9 us  [body(): parts = lax.all_to_all(partial_image, FREQ, 0, 0, tiled=True)]
    all_to_all x2, starting transfers between devices: 26 us -> 23.4 us  [the longest x1 17.1 us: body(): lax.all_to_all(jnp.broadcast_to(local[None], (depths, NX, LANES)), DEPTH,...]
    pallas_call x1, Pallas kernels: 2.52 us -> 4.86 us  [body(): pl.pallas_call(lambda *refs: image_kernel(scale, *refs), out_shape=jax.Sh...]
    pallas_call x1 -> x3, Pallas kernels: 4.22 us -> 4.07 us  [the longest x1 2.86 us: body(): pl.pallas_call(chain_kernel, out_shape=jax.ShapeDtypeStruct((GROUP * 4, N...]
  transfers between devices with their start and end apart: 3 -> 3, of which waited for: 3 -> 2; matrix products, arithmetic and copies ran while one was open for 2% -> 2% of each run, Pallas kernels for 0% -> 5%
where the time goes in v2:
time: 83.7 us; the launch traced here: 83.3 us
  blocking collectives  36.7 us (44%)
  starting transfers between devices  25.4 us (30%)
  Pallas kernels  9.04 us (11%)
  waiting for transfers between devices  8.31 us (10%)
  local copies, waits for them, and re-layouts  2.02 us (2%)
  other arithmetic  1.69 us (2%)
    all_to_all x1, blocking collectives, body(): parts = lax.all_to_all(partial_image, FREQ, 0, 0, tiled=True)  25.9 us
    all_to_all x1, starting transfers between devices, body(): lax.all_to_all(jnp.broadcast_to(local[None], (depths, NX, LANES)), DEPTH,...  17.1 us
    all_to_all x1, blocking collectives, body(): waves = lax.all_to_all(waves, ('x',) + QUAD, 0, 0, tiled=True)  10.9 us
    all_to_all x1, waiting for transfers between devices, body(): lax.all_to_all(jnp.broadcast_to(local[None], (depths, NX, LANES)), DEPTH,...  7.03 us
    all_to_all x1, starting transfers between devices, body(): sources = lax.all_to_all(packed, QUAD, 0, 0, tiled=True)  6.33 us
    pallas_call x1, Pallas kernels, body(): pl.pallas_call(lambda *refs: image_kernel(scale, *refs), out_shape=jax.Sh...  4.86 us
    pallas_call x1, Pallas kernels, body(): pl.pallas_call(chain_kernel, out_shape=jax.ShapeDtypeStruct((GROUP * 4, N...  2.86 us
    ppermute x1, starting transfers between devices, body(): swapped = lax.ppermute(own, 'core', swap)  1.95 us
  transfers between devices with their start and end apart: 3, of which 2 were waited for; matrix products, arithmetic and copies ran while one was open for 2% of the time, Pallas kernels for 5%

profile of v2, /device:TPU:1, one launch (start us, length us, event | category | flops | bytes accessed | tf_op | source)
XLA Modules:
  0.0 83.3 jit_solution(14273052842095752756)
XLA Ops:
  0.0 0.0 copy-start
  0.0 0.8 fusion
  0.8 0.7 broadcast_in_dim.16
  1.5 0.0 copy-start.1
  1.5 17.1 %all-to-all-start = ((bf16[12,64,128]{2,1,0:T(8,128)(2,1)}), bf16[12,64,128]{2,1,0:T(8,128)(2,1)S(1)}, u32[]{:S(2)}, u32[]{:S(2)}) async-start(bf16[12,64,128]{2,1,0:T(8,128)(2,1)} %broadcast_in_dim.16), calls=%async_computation | async-start | bytes 393216 | tf_op jit(solution)/shard_map/all_to_all | solution.py:202
  18.6 0.7 bitcast_convert_fusion
  19.4 0.1 slice.71
  19.4 0.1 slice.59
  19.5 0.1 slice.57
  19.6 0.1 pad.1.clone
  19.7 0.1 fusion.2
  19.8 0.1 concatenate.12
  19.9 0.1 concatenate.13
  20.0 0.1 pad_maximum_fusion.1
  20.1 0.2 bands.1
  20.3 0.0 copy-done.1
  20.3 1.0 %pack.1 = bf16[4,4,64,128]{3,2,1,0:T(8,128)(2,1)} custom-call(bf16[4,2,64,256]{3,2,1,0:T(8,128)(2,1)S(1)} %bitcast.18), custom_call_target="tpu_custom_call" | custom-call | flops 20000000 | bytes 1000000 | tf_op jit(solution)/shard_map/pack/pallas_call | solution.py:207
  21.3 7.0 %all-to-all-done.own_ref = bf16[12,64,128]{2,1,0:T(8,128)(2,1)S(1)} async-done(((bf16[12,64,128]{2,1,0:T(8,128)(2,1)}), bf16[12,64,128]{2,1,0:T(8,128)(2,1)S(1)}, u32[]{:S(2)}, u32[]{:S(2)}) %all-to-all-start) | async-done | bytes 196640 | tf_op jit(solution)/shard_map/all_to_all | solution.py:202
  28.4 6.3 %all-to-all-start.2 = ((bf16[4,4,64,128]{3,2,1,0:T(8,128)(2,1)}), bf16[4,4,64,128]{3,2,1,0:T(8,128)(2,1)S(1)}, u32[]{:S(2)}, u32[]{:S(2)}) async-start(bf16[4,4,64,128]{3,2,1,0:T(8,128)(2,1)} %pack.1), calls=%async_computation.2 | async-start | bytes 524288 | tf_op jit(solution)/shard_map/all_to_all | solution.py:216
  34.7 1.9 %collective-permute-start = (bf16[12,64,128]{2,1,0:T(8,128)(2,1)S(1)}, bf16[12,64,128]{2,1,0:T(8,128)(2,1)S(1)}, u32[]{:S(2)}, u32[]{:S(2)}) collective-permute-start(bf16[12,64,128]{2,1,0:T(8,128)(2,1)S(1)} %all-to-all-done.own_ref), channel_id=1, source_target_pairs={{0,1},{1,0},{2,3},{3,2},{4,5},{5,4},{6,7},{7,6},{8,9},{9,8},{10,11... | collective-permute-start | bytes 589832 | tf_op jit(solution)/shard_map/ppermute | solution.py:205
  36.6 0.1 pad_add_fusion.scalar_ref
  36.7 0.0 copy-done
  36.7 1.3 %collective-permute-done.swapped_ref = bf16[12,64,128]{2,1,0:T(8,128)(2,1)S(1)} collective-permute-done((bf16[12,64,128]{2,1,0:T(8,128)(2,1)S(1)}, bf16[12,64,128]{2,1,0:T(8,128)(2,1)S(1)}, u32[]{:S(2)}, u32[]{:S(2)}) %collective-permute-start) | collective-permute-done | bytes 196640 | tf_op jit(solution)/shard_map/ppermute | solution.py:205
  38.0 2.9 %chain.1 = bf16[16,64,128]{2,1,0:T(8,128)(2,1)S(1)} custom-call(s32[2]{0:T(128)S(1)} %pad_add_fusion.scalar_ref, bf16[512,128]{1,0:T(8,128)(2,1)S(1)} %get-tuple-element.8.band_first, bf16[256,512]{1,0:T(8,128)(2,1)S(1)} %get-tuple-element.9.band_even, bf16[256,512]{1,0:T(8,128)(2,1)S(1)} %get-tuple-element.10.band_odd, ...), custom_call_target="tpu_custom_call" | custom-call | flops 4000000000 | bytes 4000000 | tf_op jit(solution)/shard_map/chain/pallas_call | solution.py:237
  40.9 0.0 all-to-all-done.2.refs_1_
  40.9 10.9 %all_to_all.20.refs_0_ = bf16[16,64,128]{2,1,0:T(8,128)(2,1)S(1)} all-to-all(bf16[16,64,128]{2,1,0:T(8,128)(2,1)S(1)} %chain.1), channel_id=1, replica_groups=mesh['zh'=3,'x'=4,'y'=8,'zq'=2,'zp'=2,'core'=2] {'x','zp','core'}, dimensions={0} | all-to-all | bytes 524288 | tf_op jit(solution)/shard_map/all_to_all | solution.py:248
  51.8 4.9 %image.1 = bf16[64,16,128]{2,1,0:T(8,128)(2,1)S(1)} custom-call(bf16[16,64,128]{2,1,0:T(8,128)(2,1)S(1)} %all_to_all.20.refs_0_, bf16[4,4,64,128]{3,2,1,0:T(8,128)(2,1)S(1)} %all-to-all-done.2.refs_1_), custom_call_target="tpu_custom_call" | custom-call | flops 10000000 | bytes 2000000 | tf_op jit(solution)/shard_map/image/pallas_call | solution.py:251
  56.6 25.9 %all_to_all.21.part_ref = bf16[64,16,128]{2,1,0:T(8,128)(2,1)S(1)} all-to-all(bf16[64,16,128]{2,1,0:T(8,128)(2,1)S(1)} %image.1), channel_id=1, replica_groups=mesh['zh'=3,'x'=4,'y'=8,'zq'=2,'zp'=2,'core'=2] {'y','zq','zp','core'}, dimensions={0} | all-to-all | bytes 524288 | tf_op jit(solution)/shard_map/all_to_all | solution.py:262
  82.5 0.1 total.1
  82.6 0.6 copy.5
  (7 shorter events, 0.0 us)
Async XLA Ops:
  0.0 36.7 %copy-start = (bf16[4,2,64,256]{3,2,1,0:T(8,128)(2,1)S(1)}, bf16[4,2,64,256]{3,2,1,0:T(8,128)(2,1)}, u32[]{:S(2)}) copy-start(bf16[4,2,64,256]{3,2,1,0:T(8,128)(2,1)} %param.4) | copy-start | bytes 786436
  1.5 18.8 %copy-start.1 = (bf16[1,4,2,64,256]{4,3,2,1,0:T(8,128)(2,1)S(1)}, bf16[1,4,2,64,256]{4,3,2,1,0:T(8,128)(2,1)}, u32[]{:S(2)}) copy-start(bf16[1,4,2,64,256]{4,3,2,1,0:T(8,128)(2,1)} %param.7) | copy-start | bytes 786436
  1.5 26.8 %all-to-all-start = ((bf16[12,64,128]{2,1,0:T(8,128)(2,1)}), bf16[12,64,128]{2,1,0:T(8,128)(2,1)S(1)}, u32[]{:S(2)}, u32[]{:S(2)}) async-start(bf16[12,64,128]{2,1,0:T(8,128)(2,1)} %broadcast_in_dim.16), calls=%async_computation | async-start | bytes 393216 | tf_op jit(solution)/shard_map/all_to_all | solution.py:202
  28.4 12.5 %all-to-all-start.2 = ((bf16[4,4,64,128]{3,2,1,0:T(8,128)(2,1)}), bf16[4,4,64,128]{3,2,1,0:T(8,128)(2,1)S(1)}, u32[]{:S(2)}, u32[]{:S(2)}) async-start(bf16[4,4,64,128]{3,2,1,0:T(8,128)(2,1)} %pack.1), calls=%async_computation.2 | async-start | bytes 524288 | tf_op jit(solution)/shard_map/all_to_all | solution.py:216
  34.7 3.3 %collective-permute-start = (bf16[12,64,128]{2,1,0:T(8,128)(2,1)S(1)}, bf16[12,64,128]{2,1,0:T(8,128)(2,1)S(1)}, u32[]{:S(2)}, u32[]{:S(2)}) collective-permute-start(bf16[12,64,128]{2,1,0:T(8,128)(2,1)S(1)} %all-to-all-done.own_ref), channel_id=1, source_target_pairs={{0,1},{1,0},{2,3},{3,2},{4,5},{5,4},{6,7},{7,6},{8,9},{9,8},{10,11... | collective-permute-start | bytes 589832 | tf_op jit(solution)/shard_map/ppermute | solution.py:205

commit v3 on v2

--- a/solution.py
+++ b/solution.py
@@ -99,7 +99,11 @@
         even_mask = split(jnp.concatenate([jnp.where(left, a, b) for a, b in zip(halves, turned)], axis=0))
         odd_mask = split(jnp.concatenate([jnp.where(left, b, a) for a, b in zip(halves, turned)], axis=0))
 
-        field = jnp.dot(band_first[...], state[...], preferred_element_type=jnp.float32)
+        field = [
+            jnp.dot(band_first[rows], state[...], preferred_element_type=jnp.float32)
+            for rows in (slice(0, 4 * NX), slice(4 * NX, 8 * NX))
+        ]
+        field = jnp.concatenate(field, axis=0)
         even_in, odd_in = [], []
         for part in range(2):
             values = [field[(r * 2 + part) * NX : (r * 2 + part + 1) * NX] for r in range(R)]
@@ -128,7 +132,16 @@
     lax.fori_loop(0, scalar_ref[0], block, 0)
 
 
-def pack_kernel(source_ref, out_ref):
+def spread_kernel(core_ref, regions_ref, out_ref):
+    low = regions_ref[:, :LANES].astype(jnp.float32)
+    high = regions_ref[:, LANES:].astype(jnp.float32)
+    half = jnp.where(core_ref[0] == 0, low, high).astype(jnp.bfloat16)
+    for i in range(out_ref.shape[0]):
+        out_ref[i] = half
+
+
+def pack_kernel(quarter_ref, source_ref, *refs):
+    outs, packed = refs[:4], refs[4]
     row_at = lax.broadcasted_iota(jnp.int32, (NX, NX), 0)
     col_at = lax.broadcasted_iota(jnp.int32, (NX, NX), 1)
     flip = (row_at + col_at == NX - 1).astype(jnp.bfloat16)
@@ -140,30 +153,41 @@
             cols = slice(half * LANES, (half + 1) * LANES)
             a = real[:, cols]
             b = pltpu.roll(imag[:, cols], QUARTER, 1)
-            out_ref[half * 2, f] = jnp.where(left, a, b).astype(jnp.bfloat16)
-            out_ref[half * 2 + 1, f] = jnp.where(left, b, a).astype(jnp.bfloat16)
-
-
-def image_kernel(scale, wave_ref, source_ref, out_ref, wave, src):
+            packed[half * 2, f] = jnp.where(left, a, b).astype(jnp.bfloat16)
+            packed[half * 2 + 1, f] = jnp.where(left, b, a).astype(jnp.bfloat16)
+    for k in range(4):
+        outs[k][...] = packed[quarter_ref[0] ^ k]
+
+
+def image_kernel(scale, quarter_ref, wave_ref, *refs):
+    sources, out_ref, wave, src, totals = refs[:4], refs[4], refs[5], refs[6], refs[7]
     edge = jnp.zeros((4 * GROUP, REACH, LANES), jnp.float32)
     for ref in (wave, src):
         ref[:, :REACH, :] = edge
         ref[:, REACH + NX :, :] = edge
-    for f in range(GROUP):
-        for g in range(4):
-            wave[f * 4 + g, REACH : REACH + NX, :] = wave_ref[f * 4 + g].astype(jnp.float32)
-            src[f * 4 + g, REACH : REACH + NX, :] = source_ref[g, f].astype(jnp.float32)
-    left = lax.broadcasted_iota(jnp.int32, (REACH, LANES), 1) < QUARTER
+    for k in range(4):
+        group = (quarter_ref[0] ^ k) * GROUP
+        for f in range(GROUP):
+            wave[k * GROUP + f, REACH : REACH + NX, :] = wave_ref[f * 4 + k].astype(jnp.float32)
+            src[group + f, REACH : REACH + NX, :] = sources[k][f].astype(jnp.float32)
 
     def row(x, carry):
         total = jnp.zeros((H, LANES), jnp.float32)
         for i in range(4 * GROUP):
             total = total + wave[i, pl.ds(x, H), :] * src[i, pl.ds(NX - 1 - x, H), :]
+        totals[x] = total
+        return carry
+
+    lax.fori_loop(0, NX, row, 0, unroll=4)
+    left = lax.broadcasted_iota(jnp.int32, (REACH, LANES), 1) < QUARTER
+
+    def fold(x, carry):
+        total = totals[x]
         total = (total + pltpu.roll(total, QUARTER, 1)) * scale
         out_ref[x] = jnp.where(left, total[:REACH], total[REACH:]).astype(jnp.bfloat16)
         return carry
 
-    lax.fori_loop(0, NX, row, 0, unroll=2)
+    lax.fori_loop(0, NX, fold, 0, unroll=8)
 
 
 def sum_kernel(part_ref, out_ref):
@@ -178,8 +202,8 @@
             totals.append(total)
         a, b = totals
         cols = slice(half * LANES, (half + 1) * LANES)
-        out_ref[:REACH, cols] = jnp.where(left, a, pltpu.roll(b, QUARTER, 1))
-        out_ref[REACH:, cols] = jnp.where(left, pltpu.roll(a, QUARTER, 1), b)
+        out_ref[0, :REACH, 0, cols] = jnp.where(left, a, pltpu.roll(b, QUARTER, 1))
+        out_ref[0, REACH:, 0, cols] = jnp.where(left, pltpu.roll(a, QUARTER, 1), b)
 
 
 VMEM = pl.BlockSpec(memory_space=pltpu.VMEM)
@@ -198,22 +222,33 @@
     depths = lax.axis_size("zh") * lax.axis_size("x")
     swap = [(0, 1), (1, 0)]
 
-    local = jnp.where(core == 0, regions[0, :, :LANES], regions[0, :, LANES:]).astype(jnp.bfloat16)
-    own = lax.all_to_all(
-        jnp.broadcast_to(local[None], (depths, NX, LANES)), DEPTH, 0, 0, tiled=True
-    )
+    copies = pl.pallas_call(
+        spread_kernel,
+        out_shape=jax.ShapeDtypeStruct((depths, NX, LANES), jnp.bfloat16),
+        in_specs=[SMEM, VMEM],
+        out_specs=VMEM,
+        compiler_params=PARAMS,
+        cost_estimate=cost(1_000_000, 300_000),
+        name="spread",
+    )(core.astype(jnp.int32).reshape(1), regions[0])
+    own = lax.all_to_all(copies, DEPTH, 0, 0, tiled=True)
     swapped = lax.ppermute(own, "core", swap)
 
+    quarter = (lax.axis_index("zp") * 2 + core).astype(jnp.int32).reshape(1)
     packed = pl.pallas_call(
         pack_kernel,
-        out_shape=jax.ShapeDtypeStruct((4, GROUP, NX, LANES), jnp.bfloat16),
-        in_specs=[VMEM],
-        out_specs=VMEM,
+        out_shape=(jax.ShapeDtypeStruct((GROUP, NX, LANES), jnp.bfloat16),) * 4,
+        in_specs=[SMEM, VMEM],
+        out_specs=(VMEM,) * 4,
+        scratch_shapes=[pltpu.VMEM((4, GROUP, NX, LANES), jnp.bfloat16)],
         compiler_params=PARAMS,
         cost_estimate=cost(20_000_000, 1_000_000),
         name="pack",
-    )(source[0])
-    sources = lax.all_to_all(packed, QUAD, 0, 0, tiled=True)
+    )(quarter, source[0])
+    sources = [packed[0]] + [
+        lax.ppermute(packed[k], QUAD, [(i, i ^ k) for i in range(4)]) for k in (1, 2, 3)
+    ]
+    own, swapped, *sources = lax.optimization_barrier((own, swapped, *sources))
 
     rows_first, rows_second = tap_rows(
         lax.dynamic_index_in_dim(table, mine_x, 0, keepdims=False).astype(jnp.float32)
@@ -251,25 +286,25 @@
     partial_image = pl.pallas_call(
         lambda *refs: image_kernel(scale, *refs),
         out_shape=jax.ShapeDtypeStruct((NX, REACH, LANES), jnp.bfloat16),
-        in_specs=[VMEM, VMEM],
+        in_specs=[SMEM] + [VMEM] * 5,
         out_specs=VMEM,
-        scratch_shapes=[pltpu.VMEM((4 * GROUP, NX + H, LANES), jnp.float32)] * 2,
+        scratch_shapes=[pltpu.VMEM((4 * GROUP, NX + H, LANES), jnp.float32)] * 2
+        + [pltpu.VMEM((NX, H, LANES), jnp.float32)],
         compiler_params=PARAMS,
         cost_estimate=cost(10_000_000, 2_000_000),
         name="image",
-    )(waves, sources)
+    )(quarter, waves, *sources)
 
     parts = lax.all_to_all(partial_image, FREQ, 0, 0, tiled=True)
 
-    mine = pl.pallas_call(
+    return pl.pallas_call(
         sum_kernel,
-        out_shape=jax.ShapeDtypeStruct((H, NY), jnp.float32),
+        out_shape=jax.ShapeDtypeStruct((1, H, 1, NY), jnp.float32),
         in_specs=[VMEM],
         out_specs=VMEM,
         compiler_params=PARAMS,
         name="total",
     )(parts)
-    return mine[None, :, None, :]
 
 
 def solution(mesh):

time: 83.7 us -> 78.2 us (0.934)
  waiting for transfers between devices: 8.31 us -> 0.94 us
  starting transfers between devices: 25.4 us -> 29.6 us
  Pallas kernels: 9.04 us -> 7.39 us
    ppermute x0 -> x3, starting transfers between devices: none -> 8.33 us  [body(): lax.ppermute(packed[k], QUAD, [(i, i ^ k) for i in range(4)])]
    all_to_all x2 -> x1, waiting for transfers between devices: 7.03 us -> 0.01 us  [body(): own = lax.all_to_all(copies, DEPTH, 0, 0, tiled=True)]
    all_to_all x2 -> x1, starting transfers between devices: 23.4 us -> 17.1 us  [body(): own = lax.all_to_all(copies, DEPTH, 0, 0, tiled=True)]
    ppermute x1, starting transfers between devices: 1.95 us -> 4.19 us  [body(): swapped = lax.ppermute(own, 'core', swap)]
    pallas_call x1, Pallas kernels: 4.86 us -> 2.99 us  [body(): pl.pallas_call(lambda *refs: image_kernel(scale, *refs), out_shape=jax.Sh...]
    broadcast_in_dim x2 -> x0, local copies, waits for them, and re-layouts: 1.36 us -> none  [the longest x1 0.71 us: body(): jnp.broadcast_to(local[None], (depths, NX, LANES))]
    unnamed x4 -> x6, local copies, waits for them, and re-layouts: 0.01 us -> 0.89 us
    pallas_call x2 -> x3, Pallas kernels: 1.1 us -> 1.73 us  [the longest x1 0.73 us: body(): pl.pallas_call(sum_kernel, out_shape=jax.ShapeDtypeStruct((1, H, 1, NY),...]
  transfers between devices with their start and end apart: 3 -> 5, of which waited for: 2 -> 1; matrix products, arithmetic and copies ran while one was open for 2% -> 2% of each run, Pallas kernels for 5% -> 1%
where the time goes in v3:
time: 78.2 us; the launch traced here: 77.7 us
  blocking collectives  37.2 us (48%)
  starting transfers between devices  29.6 us (38%)
  Pallas kernels  7.39 us (9%)
  local copies, waits for them, and re-layouts  1.55 us (2%)
  waiting for transfers between devices  0.94 us (1%)
  other arithmetic  0.87 us (1%)
    all_to_all x1, blocking collectives, body(): parts = lax.all_to_all(partial_image, FREQ, 0, 0, tiled=True)  26.1 us
    all_to_all x1, starting transfers between devices, body(): own = lax.all_to_all(copies, DEPTH, 0, 0, tiled=True)  17.1 us
    all_to_all x1, blocking collectives, body(): waves = lax.all_to_all(waves, ('x',) + QUAD, 0, 0, tiled=True)  11.1 us
    ppermute x3, starting transfers between devices, body(): lax.ppermute(packed[k], QUAD, [(i, i ^ k) for i in range(4)])  8.33 us
    ppermute x1, starting transfers between devices, body(): swapped = lax.ppermute(own, 'core', swap)  4.19 us
    pallas_call x1, Pallas kernels, body(): pl.pallas_call(lambda *refs: image_kernel(scale, *refs), out_shape=jax.Sh...  2.99 us
    pallas_call x1, Pallas kernels, body(): pl.pallas_call(chain_kernel, out_shape=jax.ShapeDtypeStruct((GROUP * 4, N...  2.45 us
  transfers between devices with their start and end apart: 5, of which 1 were waited for; matrix products, arithmetic and copies ran while one was open for 2% of the time, Pallas kernels for 1%

profile of v3, /device:TPU:1, one launch (start us, length us, event | category | flops | bytes accessed | tf_op | source)
XLA Modules:
  0.0 77.7 jit_solution(11412951112654835217)
XLA Ops:
  0.0 0.0 copy-start
  0.0 0.0 copy-start.2
  0.0 0.9 %copy-done.2 = s32[1,64,256]{2,1,0:T(8,128)S(1)} copy-done((s32[1,64,256]{2,1,0:T(8,128)S(1)}, s32[1,64,256]{2,1,0:T(8,128)}, u32[]{:S(2)}) %copy-start.2) | copy-done | bytes 65560
  0.9 0.7 spread.1
  1.6 0.0 copy-start.1
  1.6 17.1 %all-to-all-start = ((bf16[12,64,128]{2,1,0:T(8,128)(2,1)}), bf16[12,64,128]{2,1,0:T(8,128)(2,1)S(1)}, u32[]{:S(2)}, u32[]{:S(2)}) async-start(bf16[12,64,128]{2,1,0:T(8,128)(2,1)} %spread.1), calls=%async_computation | async-start | bytes 393216 | tf_op jit(solution)/shard_map/all_to_all | solution.py:234
  18.7 0.0 copy-done.1
  18.7 0.3 pack.1
  19.0 2.9 %collective-permute-start.1 = (bf16[4,64,128]{2,1,0:T(8,128)(2,1)S(1)}, bf16[4,64,128]{2,1,0:T(8,128)(2,1)S(1)}, u32[]{:S(2)}, u32[]{:S(2)}) collective-permute-start(bf16[4,64,128]{2,1,0:T(8,128)(2,1)S(1)} %get-tuple-element.22), channel_id=1, source_target_pairs={{0,1},{1,0},{2,3},{3,2},{4,5},{5,4},{6,7},{7,6},{8,9},{9,8},{10,11... | collective-permute-start | bytes 196616 | tf_op jit(solution)/shard_map/ppermute | solution.py:249
  21.9 3.1 %collective-permute-start.2 = (bf16[4,64,128]{2,1,0:T(8,128)(2,1)S(1)}, bf16[4,64,128]{2,1,0:T(8,128)(2,1)S(1)}, u32[]{:S(2)}, u32[]{:S(2)}) collective-permute-start(bf16[4,64,128]{2,1,0:T(8,128)(2,1)S(1)} %get-tuple-element.23), channel_id=1, source_target_pairs={{0,2},{1,3},{2,0},{3,1},{4,6},{5,7},{6,4},{7,5},{8,10},{9,11},{10,... | collective-permute-start | bytes 196616 | tf_op jit(solution)/shard_map/ppermute | solution.py:249
  25.0 2.3 %collective-permute-start.3 = (bf16[4,64,128]{2,1,0:T(8,128)(2,1)S(1)}, bf16[4,64,128]{2,1,0:T(8,128)(2,1)S(1)}, u32[]{:S(2)}, u32[]{:S(2)}) collective-permute-start(bf16[4,64,128]{2,1,0:T(8,128)(2,1)S(1)} %get-tuple-element.24), channel_id=1, source_target_pairs={{0,3},{1,2},{2,1},{3,0},{4,7},{5,6},{6,5},{7,4},{8,11},{9,10},{10,... | collective-permute-start | bytes 196616 | tf_op jit(solution)/shard_map/ppermute | solution.py:249
  27.4 0.7 bitcast_convert_fusion
  28.1 0.1 slice.63
  28.2 0.1 slice.51
  28.3 0.1 slice.53
  28.4 0.1 pad.1.clone
  28.5 0.1 fusion.1
  28.5 0.1 concatenate.13
  28.6 0.1 concatenate.12
  28.8 0.1 pad_maximum_fusion.1
  28.8 0.2 bands.1
  29.1 0.0 all-to-all-done.own_ref
  29.1 4.2 %collective-permute-start = (bf16[12,64,128]{2,1,0:T(8,128)(2,1)S(1)}, bf16[12,64,128]{2,1,0:T(8,128)(2,1)S(1)}, u32[]{:S(2)}, u32[]{:S(2)}) collective-permute-start(bf16[12,64,128]{2,1,0:T(8,128)(2,1)S(1)} %all-to-all-done.own_ref), channel_id=1, source_target_pairs={{0,1},{1,0},{2,3},{3,2},{4,5},{5,4},{6,7},{7,6},{8,9},{9,8},{10,11... | collective-permute-start | bytes 589832 | tf_op jit(solution)/shard_map/ppermute | solution.py:235
  33.3 0.0 copy-done
  33.3 0.1 pad_add_fusion.scalar_ref
  33.4 0.0 collective-permute-done.1.refs_3_
  33.4 0.0 collective-permute-done.2.refs_4_
  33.4 0.0 collective-permute-done.3.refs_5_
  33.4 0.9 %collective-permute-done.swapped_ref = bf16[12,64,128]{2,1,0:T(8,128)(2,1)S(1)} collective-permute-done((bf16[12,64,128]{2,1,0:T(8,128)(2,1)S(1)}, bf16[12,64,128]{2,1,0:T(8,128)(2,1)S(1)}, u32[]{:S(2)}, u32[]{:S(2)}) %collective-permute-start) | collective-permute-done | bytes 196640 | tf_op jit(solution)/shard_map/ppermute | solution.py:235
  34.3 2.4 %chain.1 = bf16[16,64,128]{2,1,0:T(8,128)(2,1)S(1)} custom-call(s32[2]{0:T(128)S(1)} %pad_add_fusion.scalar_ref, bf16[512,128]{1,0:T(8,128)(2,1)S(1)} %get-tuple-element.18.band_first, bf16[256,512]{1,0:T(8,128)(2,1)S(1)} %get-tuple-element.19.band_even, bf16[256,512]{1,0:T(8,128)(2,1)S(1)} %get-tuple-element.20.band_odd, ...), custom_call_target="tpu_custom_call" | custom-call | flops 4000000000 | bytes 4000000 | tf_op jit(solution)/shard_map/chain/pallas_call | solution.py:272
  36.8 11.1 %all_to_all.15.refs_1_ = bf16[16,64,128]{2,1,0:T(8,128)(2,1)S(1)} all-to-all(bf16[16,64,128]{2,1,0:T(8,128)(2,1)S(1)} %chain.1), channel_id=1, replica_groups=mesh['zh'=3,'x'=4,'y'=8,'zq'=2,'zp'=2,'core'=2] {'x','zp','core'}, dimensions={0} | all-to-all | bytes 524288 | tf_op jit(solution)/shard_map/all_to_all | solution.py:283
  47.9 3.0 %image.1 = bf16[64,16,128]{2,1,0:T(8,128)(2,1)S(1)} custom-call(s32[1]{0:T(128)} %bitcast.quarter_ref.refs_0_, bf16[16,64,128]{2,1,0:T(8,128)(2,1)S(1)} %all_to_all.15.refs_1_, bf16[4,64,128]{2,1,0:T(8,128)(2,1)S(1)} %get-tuple-element.27.refs_2_, bf16[4,64,128]{2,1,0:T(8,128)(2,1)S(1)} %collective-permute-done.1.refs_3_, ...), custom_call_target="tpu_custom_call" | custom-call | flops 10000000 | bytes 2000000 | tf_op jit(solution)/shard_map/image/pallas_call | solution.py:286
  50.9 26.1 %all_to_all.16.part_ref = bf16[64,16,128]{2,1,0:T(8,128)(2,1)S(1)} all-to-all(bf16[64,16,128]{2,1,0:T(8,128)(2,1)S(1)} %image.1), channel_id=1, replica_groups=mesh['zh'=3,'x'=4,'y'=8,'zq'=2,'zp'=2,'core'=2] {'y','zq','zp','core'}, dimensions={0} | all-to-all | bytes 524288 | tf_op jit(solution)/shard_map/all_to_all | solution.py:298
  77.0 0.7 total.1
  (7 shorter events, 0.0 us)
Async XLA Ops:
  0.0 33.3 %copy-start = (bf16[4,2,64,256]{3,2,1,0:T(8,128)(2,1)S(1)}, bf16[4,2,64,256]{3,2,1,0:T(8,128)(2,1)}, u32[]{:S(2)}) copy-start(bf16[4,2,64,256]{3,2,1,0:T(8,128)(2,1)} %param.4) | copy-start | bytes 786436
  0.0 0.9 %copy-start.2 = (s32[1,64,256]{2,1,0:T(8,128)S(1)}, s32[1,64,256]{2,1,0:T(8,128)}, u32[]{:S(2)}) copy-start(s32[1,64,256]{2,1,0:T(8,128)} %param.5) | copy-start | bytes 196612
  1.6 17.1 %copy-start.1 = (bf16[1,4,2,64,256]{4,3,2,1,0:T(8,128)(2,1)S(1)}, bf16[1,4,2,64,256]{4,3,2,1,0:T(8,128)(2,1)}, u32[]{:S(2)}) copy-start(bf16[1,4,2,64,256]{4,3,2,1,0:T(8,128)(2,1)} %param.7) | copy-start | bytes 786436
  1.6 27.5 %all-to-all-start = ((bf16[12,64,128]{2,1,0:T(8,128)(2,1)}), bf16[12,64,128]{2,1,0:T(8,128)(2,1)S(1)}, u32[]{:S(2)}, u32[]{:S(2)}) async-start(bf16[12,64,128]{2,1,0:T(8,128)(2,1)} %spread.1), calls=%async_computation | async-start | bytes 393216 | tf_op jit(solution)/shard_map/all_to_all | solution.py:234
  19.0 14.4 %collective-permute-start.1 = (bf16[4,64,128]{2,1,0:T(8,128)(2,1)S(1)}, bf16[4,64,128]{2,1,0:T(8,128)(2,1)S(1)}, u32[]{:S(2)}, u32[]{:S(2)}) collective-permute-start(bf16[4,64,128]{2,1,0:T(8,128)(2,1)S(1)} %get-tuple-element.22), channel_id=1, source_target_pairs={{0,1},{1,0},{2,3},{3,2},{4,5},{5,4},{6,7},{7,6},{8,9},{9,8},{10,11... | collective-permute-start | bytes 196616 | tf_op jit(solution)/shard_map/ppermute | solution.py:249
  21.9 11.5 %collective-permute-start.2 = (bf16[4,64,128]{2,1,0:T(8,128)(2,1)S(1)}, bf16[4,64,128]{2,1,0:T(8,128)(2,1)S(1)}, u32[]{:S(2)}, u32[]{:S(2)}) collective-permute-start(bf16[4,64,128]{2,1,0:T(8,128)(2,1)S(1)} %get-tuple-element.23), channel_id=1, source_target_pairs={{0,2},{1,3},{2,0},{3,1},{4,6},{5,7},{6,4},{7,5},{8,10},{9,11},{10,... | collective-permute-start | bytes 196616 | tf_op jit(solution)/shard_map/ppermute | solution.py:249
  25.0 8.4 %collective-permute-start.3 = (bf16[4,64,128]{2,1,0:T(8,128)(2,1)S(1)}, bf16[4,64,128]{2,1,0:T(8,128)(2,1)S(1)}, u32[]{:S(2)}, u32[]{:S(2)}) collective-permute-start(bf16[4,64,128]{2,1,0:T(8,128)(2,1)S(1)} %get-tuple-element.24), channel_id=1, source_target_pairs={{0,3},{1,2},{2,1},{3,0},{4,7},{5,6},{6,5},{7,4},{8,11},{9,10},{10,... | collective-permute-start | bytes 196616 | tf_op jit(solution)/shard_map/ppermute | solution.py:249
  29.1 5.2 %collective-permute-start = (bf16[12,64,128]{2,1,0:T(8,128)(2,1)S(1)}, bf16[12,64,128]{2,1,0:T(8,128)(2,1)S(1)}, u32[]{:S(2)}, u32[]{:S(2)}) collective-permute-start(bf16[12,64,128]{2,1,0:T(8,128)(2,1)S(1)} %all-to-all-done.own_ref), channel_id=1, source_target_pairs={{0,1},{1,0},{2,3},{3,2},{4,5},{5,4},{6,7},{7,6},{8,9},{9,8},{10,11... | collective-permute-start | bytes 589832 | tf_op jit(solution)/shard_map/ppermute | solution.py:235

commit v4 on v3

--- a/solution.py
+++ b/solution.py
@@ -78,10 +78,10 @@
     return out
 
 
-def chain_kernel(scalar_ref, band_first, band_even, band_odd, surface_ref, own_ref, swapped_ref, out_ref, state):
+def chain_kernel(scalar_ref, band_first, band_even, band_odd, surface_ref, regions_ref, out_ref, state):
     state[:NX, :] = surface_ref[0]
     state[NX:, :] = surface_ref[1]
-    core = scalar_ref[1]
+    blocks = scalar_ref[0]
     lane = lax.broadcasted_iota(jnp.int32, (NX, LANES), 1)
     left = lane < QUARTER
     low = lane < 96
@@ -90,12 +90,11 @@
     def split(values):
         return [values == float(r) for r in range(R - 1)]
 
-    def step(t, slot):
-        own = own_ref[t].astype(jnp.float32)
-        swapped = swapped_ref[t].astype(jnp.float32)
-        halves = [jnp.where(core == half, own, swapped) for half in range(2)]
+    def step(b, slot):
+        region = regions_ref[slot, blocks - 1 - b].astype(jnp.float32)
+        halves = [region[:, :LANES], region[:, LANES:]]
         turned = [pltpu.roll(half, QUARTER, 1) for half in halves]
-        full = split(jnp.concatenate(halves, axis=1))
+        full = split(region)
         even_mask = split(jnp.concatenate([jnp.where(left, a, b) for a, b in zip(halves, turned)], axis=0))
         odd_mask = split(jnp.concatenate([jnp.where(left, b, a) for a, b in zip(halves, turned)], axis=0))
 
@@ -126,18 +125,17 @@
 
     def block(b, carry):
         for slot in range(GROUP):
-            step(b * GROUP + slot, slot)
+            step(b, slot)
         return carry
 
-    lax.fori_loop(0, scalar_ref[0], block, 0)
-
-
-def spread_kernel(core_ref, regions_ref, out_ref):
-    low = regions_ref[:, :LANES].astype(jnp.float32)
-    high = regions_ref[:, LANES:].astype(jnp.float32)
-    half = jnp.where(core_ref[0] == 0, low, high).astype(jnp.bfloat16)
+    lax.fori_loop(0, blocks, block, 0)
+
+
+def spread_kernel(*refs):
+    out_ref = refs[-1]
     for i in range(out_ref.shape[0]):
-        out_ref[i] = half
+        for slot, ref in enumerate(refs[:-1]):
+            out_ref[i, slot] = ref[...]
 
 
 def pack_kernel(quarter_ref, source_ref, *refs):
@@ -219,20 +217,22 @@
     zh = lax.axis_index("zh")
     mine_x = lax.axis_index("x")
     core = lax.axis_index("core")
-    depths = lax.axis_size("zh") * lax.axis_size("x")
-    swap = [(0, 1), (1, 0)]
-
+    blocks = lax.axis_size("zh")
+    local = regions[0].astype(jnp.bfloat16)
+    earlier = [
+        lax.ppermute(local, "zh", [(i, i + k) for i in range(blocks - k)]) for k in range(1, blocks)
+    ]
     copies = pl.pallas_call(
         spread_kernel,
-        out_shape=jax.ShapeDtypeStruct((depths, NX, LANES), jnp.bfloat16),
-        in_specs=[SMEM, VMEM],
+        out_shape=jax.ShapeDtypeStruct((GROUP, blocks, NX, NY), jnp.bfloat16),
+        in_specs=[VMEM] * blocks,
         out_specs=VMEM,
         compiler_params=PARAMS,
-        cost_estimate=cost(1_000_000, 300_000),
+        cost_estimate=cost(1_000_000, 500_000),
         name="spread",
-    )(core.astype(jnp.int32).reshape(1), regions[0])
-    own = lax.all_to_all(copies, DEPTH, 0, 0, tiled=True)
-    swapped = lax.ppermute(own, "core", swap)
+    )(local, *earlier)
+    copies, local_source = lax.optimization_barrier((copies, source[0]))
+    all_regions = lax.all_to_all(copies, "x", 0, 0, tiled=True)
 
     quarter = (lax.axis_index("zp") * 2 + core).astype(jnp.int32).reshape(1)
     packed = pl.pallas_call(
@@ -244,11 +244,12 @@
         compiler_params=PARAMS,
         cost_estimate=cost(20_000_000, 1_000_000),
         name="pack",
-    )(quarter, source[0])
+    )(quarter, local_source)
     sources = [packed[0]] + [
         lax.ppermute(packed[k], QUAD, [(i, i ^ k) for i in range(4)]) for k in (1, 2, 3)
     ]
-    own, swapped, *sources = lax.optimization_barrier((own, swapped, *sources))
+    all_regions, *early = lax.optimization_barrier((all_regions, *sources[:3]))
+    sources[:3] = early
 
     rows_first, rows_second = tap_rows(
         lax.dynamic_index_in_dim(table, mine_x, 0, keepdims=False).astype(jnp.float32)
@@ -268,17 +269,17 @@
     )(rows_first, rows_second)
 
     entering = lax.dynamic_index_in_dim(surface, mine_x, 0, keepdims=False)
-    scalars = jnp.stack([zh + 1, core]).astype(jnp.int32)
+    count = (zh + 1).astype(jnp.int32).reshape(1)
     waves = pl.pallas_call(
         chain_kernel,
         out_shape=jax.ShapeDtypeStruct((GROUP * 4, NX, LANES), jnp.bfloat16),
-        in_specs=[SMEM] + [VMEM] * 6,
+        in_specs=[SMEM] + [VMEM] * 5,
         out_specs=VMEM,
         scratch_shapes=[pltpu.VMEM((2 * NX, NY), jnp.bfloat16)],
         compiler_params=PARAMS,
         cost_estimate=cost(4_000_000_000, 4_000_000),
         name="chain",
-    )(scalars, *bands, entering, own, swapped)
+    )(count, *bands, entering, all_regions)
 
     waves = lax.all_to_all(waves, ("x",) + QUAD, 0, 0, tiled=True)
 

time: 78.2 us -> 79.1 us (1.012)
  blocking collectives: 37.2 us -> 25.2 us
  starting transfers between devices: 29.6 us -> 37.4 us
  waiting for transfers between devices: 0.94 us -> 5.9 us
  local copies, waits for them, and re-layouts: 1.55 us -> 0.67 us
  other arithmetic: 0.87 us -> 1.68 us
    ppermute x1 -> x2, starting transfers between devices: 4.19 us -> 16.4 us  [body(): lax.ppermute(local, 'zh', [(i, i + k) for i in range(blocks - k)])]
    all_to_all x1 -> x0, blocking collectives: 11.1 us -> none  [body(): waves = lax.all_to_all(waves, ('x',) + QUAD, 0, 0, tiled=True)]
    all_to_all x1 -> x2, starting transfers between devices: 17.1 us -> 10.9 us  [the longest x1 6.74 us: body(): waves = lax.all_to_all(waves, ('x',) + QUAD, 0, 0, tiled=True)]
    ppermute x3, waiting for transfers between devices: 0.01 us -> 5.47 us  [body(): lax.ppermute(packed[k], QUAD, [(i, i ^ k) for i in range(4)])]
    ppermute x3, starting transfers between devices: 8.33 us -> 10.1 us  [body(): lax.ppermute(packed[k], QUAD, [(i, i ^ k) for i in range(4)])]
    all_to_all x1, blocking collectives: 26.1 us -> 25.2 us  [body(): parts = lax.all_to_all(partial_image, FREQ, 0, 0, tiled=True)]
    ppermute x1 -> x2, waiting for transfers between devices: 0.93 us -> 0.01 us  [body(): lax.ppermute(local, 'zh', [(i, i + k) for i in range(blocks - k)])]
    convert_element_type x0 -> x1, other arithmetic: none -> 0.89 us  [body(): local = regions[0].astype(jnp.bfloat16)]
  transfers between devices with their start and end apart: 5 -> 7, of which waited for: 1 -> 3; matrix products, arithmetic and copies ran while one was open for 2% -> 2% of each run, Pallas kernels for 1% -> 1%
where the time goes in v4:
time: 79.1 us; the launch traced here: 78.6 us
  starting transfers between devices  37.4 us (47%)
  blocking collectives  25.2 us (32%)
  Pallas kernels  7.64 us (10%)
  waiting for transfers between devices  5.9 us (7%)
  other arithmetic  1.68 us (2%)
    all_to_all x1, blocking collectives, body(): parts = lax.all_to_all(partial_image, FREQ, 0, 0, tiled=True)  25.2 us
    ppermute x2, starting transfers between devices, body(): lax.ppermute(local, 'zh', [(i, i + k) for i in range(blocks - k)])  16.4 us
    ppermute x3, starting transfers between devices, body(): lax.ppermute(packed[k], QUAD, [(i, i ^ k) for i in range(4)])  10.1 us
    all_to_all x1, starting transfers between devices, body(): waves = lax.all_to_all(waves, ('x',) + QUAD, 0, 0, tiled=True)  6.74 us
    ppermute x3, waiting for transfers between devices, body(): lax.ppermute(packed[k], QUAD, [(i, i ^ k) for i in range(4)])  5.47 us
    all_to_all x1, starting transfers between devices, body(): all_regions = lax.all_to_all(copies, 'x', 0, 0, tiled=True)  4.14 us
    pallas_call x1, Pallas kernels, body(): pl.pallas_call(lambda *refs: image_kernel(scale, *refs), out_shape=jax.Sh...  2.99 us
    pallas_call x1, Pallas kernels, body(): pl.pallas_call(chain_kernel, out_shape=jax.ShapeDtypeStruct((GROUP * 4, N...  2.61 us
  transfers between devices with their start and end apart: 7, of which 3 were waited for; matrix products, arithmetic and copies ran while one was open for 2% of the time, Pallas kernels for 1%

profile of v4, /device:TPU:1, one launch (start us, length us, event | category | flops | bytes accessed | tf_op | source)
XLA Modules:
  0.0 78.6 jit_solution(588361347849041842)
XLA Ops:
  0.0 0.0 copy-start
  0.0 0.9 %convert_bitcast_fusion.refs_0_ = bf16[64,256]{1,0:T(8,128)(2,1)S(1)} fusion(s32[1,64,256]{2,1,0:T(8,128)} %param.5), kind=kLoop, calls=%fused_computation.1 | loop fusion | flops 16384 | bytes 98304 | tf_op jit(solution)/shard_map/convert_element_type | solution.py:221
  0.9 15.1 %collective-permute-start.1 = (bf16[64,256]{1,0:T(8,128)(2,1)S(1)}, bf16[64,256]{1,0:T(8,128)(2,1)S(1)}, u32[]{:S(2)}, u32[]{:S(2)}) collective-permute-start(bf16[64,256]{1,0:T(8,128)(2,1)S(1)} %convert_bitcast_fusion.refs_0_), channel_id=1, source_target_pairs={{0,512},{1,513},{2,514},{3,515},{4,516},{5,517},{6,518},{7,519},{8... | collective-permute-start | bytes 98312 | tf_op jit(solution)/shard_map/ppermute | solution.py:223
  16.0 1.3 %collective-permute-start = (bf16[64,256]{1,0:T(8,128)(2,1)S(1)}, bf16[64,256]{1,0:T(8,128)(2,1)S(1)}, u32[]{:S(2)}, u32[]{:S(2)}) collective-permute-start(bf16[64,256]{1,0:T(8,128)(2,1)S(1)} %convert_bitcast_fusion.refs_0_), channel_id=1, source_target_pairs={{0,256},{256,512},{1,257},{257,513},{2,258},{258,514},{3,259},{259... | collective-permute-start | bytes 98312 | tf_op jit(solution)/shard_map/ppermute | solution.py:223
  17.3 0.7 bitcast_convert_fusion
  18.0 0.1 fusion.1
  18.1 0.1 concatenate.13
  18.2 0.1 concatenate.12
  18.3 0.1 slice.63
  18.4 0.1 slice.51
  18.5 0.1 slice.53
  18.6 0.1 pad.1.clone
  18.7 0.0 collective-permute-done.1.refs_2_
  18.7 0.0 collective-permute-done.refs_1_
  18.7 0.8 %spread.1 = bf16[4,3,64,256]{3,2,1,0:T(8,128)(2,1)} custom-call(bf16[64,256]{1,0:T(8,128)(2,1)S(1)} %convert_bitcast_fusion.refs_0_, bf16[64,256]{1,0:T(8,128)(2,1)S(1)} %collective-permute-done.refs_1_, bf16[64,256]{1,0:T(8,128)(2,1)S(1)} %collective-permute-done.1.refs_2_), custom_call_target="tpu_custom_call" | custom-call | flops 1000000 | bytes 500000 | tf_op jit(solution)/shard_map/spread/pallas_call | solution.py:225
  19.5 0.0 copy-start.1
  19.5 4.1 %all-to-all-start = ((bf16[4,3,64,256]{3,2,1,0:T(8,128)(2,1)}), bf16[4,3,64,256]{3,2,1,0:T(8,128)(2,1)S(1)}, u32[]{:S(2)}, u32[]{:S(2)}) async-start(bf16[4,3,64,256]{3,2,1,0:T(8,128)(2,1)} %spread.1), calls=%async_computation | async-start | bytes 786432 | tf_op jit(solution)/shard_map/all_to_all | solution.py:235
  23.6 0.1 pad_maximum_fusion.1
  23.7 0.2 bands.1
  23.9 0.0 copy-done.1
  23.9 0.3 pack.1
  24.2 3.3 %collective-permute-start.2 = (bf16[4,64,128]{2,1,0:T(8,128)(2,1)S(1)}, bf16[4,64,128]{2,1,0:T(8,128)(2,1)S(1)}, u32[]{:S(2)}, u32[]{:S(2)}) collective-permute-start(bf16[4,64,128]{2,1,0:T(8,128)(2,1)S(1)} %get-tuple-element.24), channel_id=1, source_target_pairs={{0,1},{1,0},{2,3},{3,2},{4,5},{5,4},{6,7},{7,6},{8,9},{9,8},{10,11... | collective-permute-start | bytes 196616 | tf_op jit(solution)/shard_map/ppermute | solution.py:249
  27.6 3.3 %collective-permute-start.3 = (bf16[4,64,128]{2,1,0:T(8,128)(2,1)S(1)}, bf16[4,64,128]{2,1,0:T(8,128)(2,1)S(1)}, u32[]{:S(2)}, u32[]{:S(2)}) collective-permute-start(bf16[4,64,128]{2,1,0:T(8,128)(2,1)S(1)} %get-tuple-element.25), channel_id=1, source_target_pairs={{0,2},{1,3},{2,0},{3,1},{4,6},{5,7},{6,4},{7,5},{8,10},{9,11},{10,... | collective-permute-start | bytes 196616 | tf_op jit(solution)/shard_map/ppermute | solution.py:249
  30.9 0.0 copy-done
  30.9 0.0 collective-permute-done.2.refs_3_
  30.9 2.3 %collective-permute-done.3.refs_4_ = bf16[4,64,128]{2,1,0:T(8,128)(2,1)S(1)} collective-permute-done((bf16[4,64,128]{2,1,0:T(8,128)(2,1)S(1)}, bf16[4,64,128]{2,1,0:T(8,128)(2,1)S(1)}, u32[]{:S(2)}, u32[]{:S(2)}) %collective-permute-start.3) | collective-permute-done | bytes 65568 | tf_op jit(solution)/shard_map/ppermute | solution.py:249
  33.2 0.0 all-to-all-done.regions_ref
  33.2 2.6 %chain.1 = bf16[16,64,128]{2,1,0:T(8,128)(2,1)} custom-call(s32[1]{0:T(128)} %bitcast.1.scalar_ref, bf16[512,128]{1,0:T(8,128)(2,1)S(1)} %get-tuple-element.18.band_first, bf16[256,512]{1,0:T(8,128)(2,1)S(1)} %get-tuple-element.19.band_even, bf16[256,512]{1,0:T(8,128)(2,1)S(1)} %get-tuple-element.20.band_odd, ...), custom_call_target="tpu_custom_call" | custom-call | flops 4000000000 | bytes 4000000 | tf_op jit(solution)/shard_map/chain/pallas_call | solution.py:273
  35.8 6.7 %all-to-all-start.1 = ((bf16[16,64,128]{2,1,0:T(8,128)(2,1)}), bf16[16,64,128]{2,1,0:T(8,128)(2,1)S(1)}, u32[]{:S(2)}, u32[]{:S(2)}) async-start(bf16[16,64,128]{2,1,0:T(8,128)(2,1)} %chain.1), calls=%async_computation.1 | async-start | bytes 524288 | tf_op jit(solution)/shard_map/all_to_all | solution.py:284
  42.5 3.5 %collective-permute-start.4 = (bf16[4,64,128]{2,1,0:T(8,128)(2,1)S(1)}, bf16[4,64,128]{2,1,0:T(8,128)(2,1)S(1)}, u32[]{:S(2)}, u32[]{:S(2)}) collective-permute-start(bf16[4,64,128]{2,1,0:T(8,128)(2,1)S(1)} %get-tuple-element.30), channel_id=1, source_target_pairs={{0,3},{1,2},{2,1},{3,0},{4,7},{5,6},{6,5},{7,4},{8,11},{9,10},{10,... | collective-permute-start | bytes 196616 | tf_op jit(solution)/shard_map/ppermute | solution.py:249
  46.1 3.2 %collective-permute-done.4.refs_5_ = bf16[4,64,128]{2,1,0:T(8,128)(2,1)S(1)} collective-permute-done((bf16[4,64,128]{2,1,0:T(8,128)(2,1)S(1)}, bf16[4,64,128]{2,1,0:T(8,128)(2,1)S(1)}, u32[]{:S(2)}, u32[]{:S(2)}) %collective-permute-start.4) | collective-permute-done | bytes 65568 | tf_op jit(solution)/shard_map/ppermute | solution.py:249
  49.3 0.4 all-to-all-done.1.refs_1_
  49.7 3.0 %image.1 = bf16[64,16,128]{2,1,0:T(8,128)(2,1)S(1)} custom-call(s32[1]{0:T(128)} %bitcast.quarter_ref.refs_0_, bf16[16,64,128]{2,1,0:T(8,128)(2,1)S(1)} %all-to-all-done.1.refs_1_, bf16[4,64,128]{2,1,0:T(8,128)(2,1)S(1)} %get-tuple-element.27.refs_2_, bf16[4,64,128]{2,1,0:T(8,128)(2,1)S(1)} %collective-permute-done.2.refs_3_, ...), custom_call_target="tpu_custom_call" | custom-call | flops 10000000 | bytes 2000000 | tf_op jit(solution)/shard_map/image/pallas_call | solution.py:287
  52.7 25.2 %all_to_all.15.part_ref = bf16[64,16,128]{2,1,0:T(8,128)(2,1)S(1)} all-to-all(bf16[64,16,128]{2,1,0:T(8,128)(2,1)S(1)} %image.1), channel_id=1, replica_groups=mesh['zh'=3,'x'=4,'y'=8,'zq'=2,'zp'=2,'core'=2] {'y','zq','zp','core'}, dimensions={0} | all-to-all | bytes 524288 | tf_op jit(solution)/shard_map/all_to_all | solution.py:299
  77.9 0.7 total.1
  (7 shorter events, 0.0 us)
Async XLA Ops:
  0.0 30.9 %copy-start = (bf16[4,2,64,256]{3,2,1,0:T(8,128)(2,1)S(1)}, bf16[4,2,64,256]{3,2,1,0:T(8,128)(2,1)}, u32[]{:S(2)}) copy-start(bf16[4,2,64,256]{3,2,1,0:T(8,128)(2,1)} %param.4) | copy-start | bytes 786436
  0.9 17.8 %collective-permute-start.1 = (bf16[64,256]{1,0:T(8,128)(2,1)S(1)}, bf16[64,256]{1,0:T(8,128)(2,1)S(1)}, u32[]{:S(2)}, u32[]{:S(2)}) collective-permute-start(bf16[64,256]{1,0:T(8,128)(2,1)S(1)} %convert_bitcast_fusion.refs_0_), channel_id=1, source_target_pairs={{0,512},{1,513},{2,514},{3,515},{4,516},{5,517},{6,518},{7,519},{8... | collective-permute-start | bytes 98312 | tf_op jit(solution)/shard_map/ppermute | solution.py:223
  16.0 2.7 %collective-permute-start = (bf16[64,256]{1,0:T(8,128)(2,1)S(1)}, bf16[64,256]{1,0:T(8,128)(2,1)S(1)}, u32[]{:S(2)}, u32[]{:S(2)}) collective-permute-start(bf16[64,256]{1,0:T(8,128)(2,1)S(1)} %convert_bitcast_fusion.refs_0_), channel_id=1, source_target_pairs={{0,256},{256,512},{1,257},{257,513},{2,258},{258,514},{3,259},{259... | collective-permute-start | bytes 98312 | tf_op jit(solution)/shard_map/ppermute | solution.py:223
  19.5 4.4 %copy-start.1 = (bf16[1,4,2,64,256]{4,3,2,1,0:T(8,128)(2,1)S(1)}, bf16[1,4,2,64,256]{4,3,2,1,0:T(8,128)(2,1)}, u32[]{:S(2)}) copy-start(bf16[1,4,2,64,256]{4,3,2,1,0:T(8,128)(2,1)} %param.7) | copy-start | bytes 786436
  19.5 13.7 %all-to-all-start = ((bf16[4,3,64,256]{3,2,1,0:T(8,128)(2,1)}), bf16[4,3,64,256]{3,2,1,0:T(8,128)(2,1)S(1)}, u32[]{:S(2)}, u32[]{:S(2)}) async-start(bf16[4,3,64,256]{3,2,1,0:T(8,128)(2,1)} %spread.1), calls=%async_computation | async-start | bytes 786432 | tf_op jit(solution)/shard_map/all_to_all | solution.py:235
  24.2 6.7 %collective-permute-start.2 = (bf16[4,64,128]{2,1,0:T(8,128)(2,1)S(1)}, bf16[4,64,128]{2,1,0:T(8,128)(2,1)S(1)}, u32[]{:S(2)}, u32[]{:S(2)}) collective-permute-start(bf16[4,64,128]{2,1,0:T(8,128)(2,1)S(1)} %get-tuple-element.24), channel_id=1, source_target_pairs={{0,1},{1,0},{2,3},{3,2},{4,5},{5,4},{6,7},{7,6},{8,9},{9,8},{10,11... | collective-permute-start | bytes 196616 | tf_op jit(solution)/shard_map/ppermute | solution.py:249
  27.6 5.6 %collective-permute-start.3 = (bf16[4,64,128]{2,1,0:T(8,128)(2,1)S(1)}, bf16[4,64,128]{2,1,0:T(8,128)(2,1)S(1)}, u32[]{:S(2)}, u32[]{:S(2)}) collective-permute-start(bf16[4,64,128]{2,1,0:T(8,128)(2,1)S(1)} %get-tuple-element.25), channel_id=1, source_target_pairs={{0,2},{1,3},{2,0},{3,1},{4,6},{5,7},{6,4},{7,5},{8,10},{9,11},{10,... | collective-permute-start | bytes 196616 | tf_op jit(solution)/shard_map/ppermute | solution.py:249
  35.8 13.9 %all-to-all-start.1 = ((bf16[16,64,128]{2,1,0:T(8,128)(2,1)}), bf16[16,64,128]{2,1,0:T(8,128)(2,1)S(1)}, u32[]{:S(2)}, u32[]{:S(2)}) async-start(bf16[16,64,128]{2,1,0:T(8,128)(2,1)} %chain.1), calls=%async_computation.1 | async-start | bytes 524288 | tf_op jit(solution)/shard_map/all_to_all | solution.py:284
  42.5 6.8 %collective-permute-start.4 = (bf16[4,64,128]{2,1,0:T(8,128)(2,1)S(1)}, bf16[4,64,128]{2,1,0:T(8,128)(2,1)S(1)}, u32[]{:S(2)}, u32[]{:S(2)}) collective-permute-start(bf16[4,64,128]{2,1,0:T(8,128)(2,1)S(1)} %get-tuple-element.30), channel_id=1, source_target_pairs={{0,3},{1,2},{2,1},{3,0},{4,7},{5,6},{6,5},{7,4},{8,11},{9,10},{10,... | collective-permute-start | bytes 196616 | tf_op jit(solution)/shard_map/ppermute | solution.py:249

commit v5 on v4

--- a/solution.py
+++ b/solution.py
@@ -139,7 +139,7 @@
 
 
 def pack_kernel(quarter_ref, source_ref, *refs):
-    outs, packed = refs[:4], refs[4]
+    own_ref, core_ref, chip_ref, packed = refs
     row_at = lax.broadcasted_iota(jnp.int32, (NX, NX), 0)
     col_at = lax.broadcasted_iota(jnp.int32, (NX, NX), 1)
     flip = (row_at + col_at == NX - 1).astype(jnp.bfloat16)
@@ -153,12 +153,15 @@
             b = pltpu.roll(imag[:, cols], QUARTER, 1)
             packed[half * 2, f] = jnp.where(left, a, b).astype(jnp.bfloat16)
             packed[half * 2 + 1, f] = jnp.where(left, b, a).astype(jnp.bfloat16)
-    for k in range(4):
-        outs[k][...] = packed[quarter_ref[0] ^ k]
-
-
-def image_kernel(scale, quarter_ref, wave_ref, *refs):
-    sources, out_ref, wave, src, totals = refs[:4], refs[4], refs[5], refs[6], refs[7]
+    mine = quarter_ref[0]
+    own_ref[...] = packed[mine]
+    core_ref[0] = packed[mine ^ 1]
+    core_ref[1] = packed[mine ^ 3]
+    chip_ref[0] = packed[mine ^ 2]
+
+
+def image_kernel(scale, quarter_ref, wave_ref, own_ref, core_ref, chip_ref, out_ref, wave, src, totals):
+    sources = [own_ref, core_ref.at[0], chip_ref.at[0], chip_ref.at[1]]
     edge = jnp.zeros((4 * GROUP, REACH, LANES), jnp.float32)
     for ref in (wave, src):
         ref[:, :REACH, :] = edge
@@ -222,6 +225,21 @@
     earlier = [
         lax.ppermute(local, "zh", [(i, i + k) for i in range(blocks - k)]) for k in range(1, blocks)
     ]
+    quarter = (lax.axis_index("zp") * 2 + core).astype(jnp.int32).reshape(1)
+    four = jax.ShapeDtypeStruct((GROUP, NX, LANES), jnp.bfloat16)
+    pair = jax.ShapeDtypeStruct((2, GROUP, NX, LANES), jnp.bfloat16)
+    one = jax.ShapeDtypeStruct((1, GROUP, NX, LANES), jnp.bfloat16)
+    packed, to_core, to_chip = pl.pallas_call(
+        pack_kernel,
+        out_shape=(four, pair, one),
+        in_specs=[SMEM, VMEM],
+        out_specs=(VMEM,) * 3,
+        scratch_shapes=[pltpu.VMEM((4, GROUP, NX, LANES), jnp.bfloat16)],
+        compiler_params=PARAMS,
+        cost_estimate=cost(20_000_000, 1_000_000),
+        name="pack",
+    )(quarter, source[0])
+    from_core = lax.ppermute(to_core, "core", [(0, 1), (1, 0)])
     copies = pl.pallas_call(
         spread_kernel,
         out_shape=jax.ShapeDtypeStruct((GROUP, blocks, NX, NY), jnp.bfloat16),
@@ -231,25 +249,11 @@
         cost_estimate=cost(1_000_000, 500_000),
         name="spread",
     )(local, *earlier)
-    copies, local_source = lax.optimization_barrier((copies, source[0]))
+    copies, from_core = lax.optimization_barrier((copies, from_core))
+    from_chip = lax.ppermute(
+        jnp.concatenate([to_chip, from_core[1:]], axis=0), "zp", [(0, 1), (1, 0)]
+    )
     all_regions = lax.all_to_all(copies, "x", 0, 0, tiled=True)
-
-    quarter = (lax.axis_index("zp") * 2 + core).astype(jnp.int32).reshape(1)
-    packed = pl.pallas_call(
-        pack_kernel,
-        out_shape=(jax.ShapeDtypeStruct((GROUP, NX, LANES), jnp.bfloat16),) * 4,
-        in_specs=[SMEM, VMEM],
-        out_specs=(VMEM,) * 4,
-        scratch_shapes=[pltpu.VMEM((4, GROUP, NX, LANES), jnp.bfloat16)],
-        compiler_params=PARAMS,
-        cost_estimate=cost(20_000_000, 1_000_000),
-        name="pack",
-    )(quarter, local_source)
-    sources = [packed[0]] + [
-        lax.ppermute(packed[k], QUAD, [(i, i ^ k) for i in range(4)]) for k in (1, 2, 3)
-    ]
-    all_regions, *early = lax.optimization_barrier((all_regions, *sources[:3]))
-    sources[:3] = early
 
     rows_first, rows_second = tap_rows(
         lax.dynamic_index_in_dim(table, mine_x, 0, keepdims=False).astype(jnp.float32)
@@ -277,24 +281,25 @@
         out_specs=VMEM,
         scratch_shapes=[pltpu.VMEM((2 * NX, NY), jnp.bfloat16)],
         compiler_params=PARAMS,
-        cost_estimate=cost(4_000_000_000, 4_000_000),
+        cost_estimate=cost(1_000_000, 100_000),
         name="chain",
     )(count, *bands, entering, all_regions)
 
+    waves, from_chip = lax.optimization_barrier((waves, from_chip))
     waves = lax.all_to_all(waves, ("x",) + QUAD, 0, 0, tiled=True)
 
     scale = 1.0 / math.sqrt(surface.shape[0] * lax.axis_size(FREQ))
     partial_image = pl.pallas_call(
         lambda *refs: image_kernel(scale, *refs),
         out_shape=jax.ShapeDtypeStruct((NX, REACH, LANES), jnp.bfloat16),
-        in_specs=[SMEM] + [VMEM] * 5,
+        in_specs=[SMEM] + [VMEM] * 4,
         out_specs=VMEM,
         scratch_shapes=[pltpu.VMEM((4 * GROUP, NX + H, LANES), jnp.float32)] * 2
         + [pltpu.VMEM((NX, H, LANES), jnp.float32)],
         compiler_params=PARAMS,
         cost_estimate=cost(10_000_000, 2_000_000),
         name="image",
-    )(quarter, waves, *sources)
+    )(quarter, waves, packed, from_core, from_chip)
 
     parts = lax.all_to_all(partial_image, FREQ, 0, 0, tiled=True)
 

time: 79.1 us -> 77 us (0.973)
  starting transfers between devices: 37.4 us -> 26.4 us
  blocking collectives: 25.2 us -> 35.3 us
  waiting for transfers between devices: 5.9 us -> 4.5 us
  local copies, waits for them, and re-layouts: 0.67 us -> 1.62 us
    all_to_all x0 -> x1, blocking collectives: none -> 11.4 us  [body(): waves = lax.all_to_all(waves, ('x',) + QUAD, 0, 0, tiled=True)]
    all_to_all x1 -> x0, starting transfers between devices: 6.74 us -> none  [body(): waves = lax.all_to_all(waves, ('x',) + QUAD, 0, 0, tiled=True)]
    ppermute x3 -> x2, waiting for transfers between devices: 5.47 us -> 0.01 us  [the longest x1 0.01 us: body(): from_core = lax.ppermute(to_core, 'core', [(0, 1), (1, 0)])]
    all_to_all x1, waiting for transfers between devices: 0.01 us -> 4.49 us  [body(): all_regions = lax.all_to_all(copies, 'x', 0, 0, tiled=True)]
    ppermute x3 -> x2, starting transfers between devices: 10.1 us -> 5.98 us  [the longest x1 3.11 us: body(): lax.ppermute(jnp.concatenate([to_chip, from_core[1:]], axis=0), 'zp', [(0...]
    all_to_all x1, blocking collectives: 25.2 us -> 23.9 us  [body(): parts = lax.all_to_all(partial_image, FREQ, 0, 0, tiled=True)]
    unnamed x4, local copies, waits for them, and re-layouts: 0.01 us -> 0.95 us
  transfers between devices with their start and end apart: 7 -> 5, of which waited for: 3 -> 1; matrix products, arithmetic and copies ran while one was open for 2% -> 2% of each run, Pallas kernels for 1% -> 4%
where the time goes in v5:
time: 77 us; the launch traced here: 76.6 us
  blocking collectives  35.3 us (46%)
  starting transfers between devices  26.4 us (34%)
  Pallas kernels  6.91 us (9%)
  waiting for transfers between devices  4.5 us (6%)
  other arithmetic  1.69 us (2%)
  local copies, waits for them, and re-layouts  1.62 us (2%)
    all_to_all x1, blocking collectives, body(): parts = lax.all_to_all(partial_image, FREQ, 0, 0, tiled=True)  23.9 us
    ppermute x2, starting transfers between devices, body(): lax.ppermute(local, 'zh', [(i, i + k) for i in range(blocks - k)])  16.4 us
    all_to_all x1, blocking collectives, body(): waves = lax.all_to_all(waves, ('x',) + QUAD, 0, 0, tiled=True)  11.4 us
    all_to_all x1, waiting for transfers between devices, body(): all_regions = lax.all_to_all(copies, 'x', 0, 0, tiled=True)  4.49 us
    all_to_all x1, starting transfers between devices, body(): all_regions = lax.all_to_all(copies, 'x', 0, 0, tiled=True)  4.01 us
    ppermute x1, starting transfers between devices, body(): lax.ppermute(jnp.concatenate([to_chip, from_core[1:]], axis=0), 'zp', [(0...  3.11 us
    pallas_call x1, Pallas kernels, body(): pl.pallas_call(lambda *refs: image_kernel(scale, *refs), out_shape=jax.Sh...  2.99 us
    ppermute x1, starting transfers between devices, body(): from_core = lax.ppermute(to_core, 'core', [(0, 1), (1, 0)])  2.87 us
  transfers between devices with their start and end apart: 5, of which 1 were waited for; matrix products, arithmetic and copies ran while one was open for 2% of the time, Pallas kernels for 4%

profile of v5, /device:TPU:1, one launch (start us, length us, event | category | flops | bytes accessed | tf_op | source)
XLA Modules:
  0.0 76.6 jit_solution(12721382234252554924)
XLA Ops:
  0.0 0.0 copy-start
  0.0 0.9 %convert_bitcast_fusion.refs_0_ = bf16[64,256]{1,0:T(8,128)(2,1)S(1)} fusion(s32[1,64,256]{2,1,0:T(8,128)} %param.5), kind=kLoop, calls=%fused_computation.2 | loop fusion | flops 16384 | bytes 98304 | tf_op jit(solution)/shard_map/convert_element_type | solution.py:224
  0.9 15.1 %collective-permute-start.1 = (bf16[64,256]{1,0:T(8,128)(2,1)S(1)}, bf16[64,256]{1,0:T(8,128)(2,1)S(1)}, u32[]{:S(2)}, u32[]{:S(2)}) collective-permute-start(bf16[64,256]{1,0:T(8,128)(2,1)S(1)} %convert_bitcast_fusion.refs_0_), channel_id=1, source_target_pairs={{0,512},{1,513},{2,514},{3,515},{4,516},{5,517},{6,518},{7,519},{8... | collective-permute-start | bytes 98312 | tf_op jit(solution)/shard_map/ppermute | solution.py:226
  16.0 1.3 %collective-permute-start = (bf16[64,256]{1,0:T(8,128)(2,1)S(1)}, bf16[64,256]{1,0:T(8,128)(2,1)S(1)}, u32[]{:S(2)}, u32[]{:S(2)}) collective-permute-start(bf16[64,256]{1,0:T(8,128)(2,1)S(1)} %convert_bitcast_fusion.refs_0_), channel_id=1, source_target_pairs={{0,256},{256,512},{1,257},{257,513},{2,258},{258,514},{3,259},{259... | collective-permute-start | bytes 98312 | tf_op jit(solution)/shard_map/ppermute | solution.py:226
  17.3 0.0 copy-start.1
  17.3 0.9 %copy-done.1 = bf16[1,4,2,64,256]{4,3,2,1,0:T(8,128)(2,1)S(1)} copy-done((bf16[1,4,2,64,256]{4,3,2,1,0:T(8,128)(2,1)S(1)}, bf16[1,4,2,64,256]{4,3,2,1,0:T(8,128)(2,1)}, u32[]{:S(2)}) %copy-start.1) | copy-done | bytes 262168
  18.2 0.3 pack.1
  18.5 2.9 %collective-permute-start.2 = (bf16[2,4,64,128]{3,2,1,0:T(8,128)(2,1)S(1)}, bf16[2,4,64,128]{3,2,1,0:T(8,128)(2,1)S(1)}, u32[]{:S(2)}, u32[]{:S(2)}) collective-permute-start(bf16[2,4,64,128]{3,2,1,0:T(8,128)(2,1)S(1)} %get-tuple-element.18), channel_id=1, source_target_pairs={{0,1},{1,0},{2,3},{3,2},{4,5},{5,4},{6,7},{7,6},{8,9},{9,8},{10,11... | collective-permute-start | bytes 393224 | tf_op jit(solution)/shard_map/ppermute | solution.py:242
  21.4 0.7 bitcast_convert_fusion
  22.1 0.1 fusion.1
  22.2 0.1 slice.67
  22.3 0.1 slice.54
  22.4 0.1 slice.56
  22.5 0.1 pad.3.clone
  22.6 0.1 pad_maximum_fusion.2
  22.6 0.1 concatenate.16
  22.8 0.1 concatenate.15
  22.9 0.0 collective-permute-done.1.refs_2_
  22.9 0.0 collective-permute-done.refs_1_
  22.9 0.8 %spread.1 = bf16[4,3,64,256]{3,2,1,0:T(8,128)(2,1)} custom-call(bf16[64,256]{1,0:T(8,128)(2,1)S(1)} %convert_bitcast_fusion.refs_0_, bf16[64,256]{1,0:T(8,128)(2,1)S(1)} %collective-permute-done.refs_1_, bf16[64,256]{1,0:T(8,128)(2,1)S(1)} %collective-permute-done.1.refs_2_), custom_call_target="tpu_custom_call" | custom-call | flops 1000000 | bytes 500000 | tf_op jit(solution)/shard_map/spread/pallas_call | solution.py:243
  23.7 0.0 collective-permute-done.2.refs_3_
  23.7 4.0 %all-to-all-start = ((bf16[4,3,64,256]{3,2,1,0:T(8,128)(2,1)}), bf16[4,3,64,256]{3,2,1,0:T(8,128)(2,1)S(1)}, u32[]{:S(2)}, u32[]{:S(2)}) async-start(bf16[4,3,64,256]{3,2,1,0:T(8,128)(2,1)} %spread.1), calls=%async_computation | async-start | bytes 786432 | tf_op jit(solution)/shard_map/all_to_all | solution.py:256
  27.7 3.1 %collective-permute-start.3 = (bf16[2,4,64,128]{3,2,1,0:T(8,128)(2,1)S(1)}, bf16[2,4,64,128]{3,2,1,0:T(8,128)(2,1)S(1)}, u32[]{:S(2)}, u32[]{:S(2)}) collective-permute-start(bf16[2,4,64,128]{3,2,1,0:T(8,128)(2,1)S(1)} %pad_maximum_fusion), channel_id=1, source_target_pairs={{0,2},{2,0},{1,3},{3,1},{4,6},{6,4},{5,7},{7,5},{8,10},{10,8},{9,1... | collective-permute-start | bytes 393224 | tf_op jit(solution)/shard_map/ppermute | solution.py:253
  30.9 0.2 bands.1
  31.1 0.0 copy-done
  31.1 4.5 %all-to-all-done.regions_ref = bf16[4,3,64,256]{3,2,1,0:T(8,128)(2,1)S(1)} async-done(((bf16[4,3,64,256]{3,2,1,0:T(8,128)(2,1)}), bf16[4,3,64,256]{3,2,1,0:T(8,128)(2,1)S(1)}, u32[]{:S(2)}, u32[]{:S(2)}) %all-to-all-start) | async-done | bytes 393248 | tf_op jit(solution)/shard_map/all_to_all | solution.py:256
  35.6 1.9 %chain.1 = bf16[16,64,128]{2,1,0:T(8,128)(2,1)S(1)} custom-call(s32[1]{0:T(128)} %bitcast.1.scalar_ref, bf16[512,128]{1,0:T(8,128)(2,1)S(1)} %get-tuple-element.15.band_first, bf16[256,512]{1,0:T(8,128)(2,1)S(1)} %get-tuple-element.16.band_even, bf16[256,512]{1,0:T(8,128)(2,1)S(1)} %get-tuple-element.17.band_odd, ...), custom_call_target="tpu_custom_call" | custom-call | flops 1000000 | bytes 100000 | tf_op jit(solution)/shard_map/chain/pallas_call | solution.py:277
  37.5 0.0 collective-permute-done.3.refs_4_
  37.5 11.4 %all_to_all.15.refs_1_ = bf16[16,64,128]{2,1,0:T(8,128)(2,1)S(1)} all-to-all(bf16[16,64,128]{2,1,0:T(8,128)(2,1)S(1)} %chain.1), channel_id=1, replica_groups=mesh['zh'=3,'x'=4,'y'=8,'zq'=2,'zp'=2,'core'=2] {'x','zp','core'}, dimensions={0} | all-to-all | bytes 524288 | tf_op jit(solution)/shard_map/all_to_all | solution.py:289
  49.0 3.0 %image.1 = bf16[64,16,128]{2,1,0:T(8,128)(2,1)S(1)} custom-call(s32[1]{0:T(128)} %bitcast.quarter_ref.refs_0_, bf16[16,64,128]{2,1,0:T(8,128)(2,1)S(1)} %all_to_all.15.refs_1_, bf16[4,64,128]{2,1,0:T(8,128)(2,1)S(1)} %get-tuple-element.23.refs_2_, bf16[2,4,64,128]{3,2,1,0:T(8,128)(2,1)S(1)} %collective-permute-done.2.refs_3_, ...), custom_call_target="tpu_custom_call" | custom-call | flops 10000000 | bytes 2000000 | tf_op jit(solution)/shard_map/image/pallas_call | solution.py:292
  52.0 23.9 %all_to_all.16.part_ref = bf16[64,16,128]{2,1,0:T(8,128)(2,1)S(1)} all-to-all(bf16[64,16,128]{2,1,0:T(8,128)(2,1)S(1)} %image.1), channel_id=1, replica_groups=mesh['zh'=3,'x'=4,'y'=8,'zq'=2,'zp'=2,'core'=2] {'y','zq','zp','core'}, dimensions={0} | all-to-all | bytes 524288 | tf_op jit(solution)/shard_map/all_to_all | solution.py:304
  75.8 0.7 total.1
  (9 shorter events, 0.1 us)
Async XLA Ops:
  0.0 31.1 %copy-start = (bf16[4,2,64,256]{3,2,1,0:T(8,128)(2,1)S(1)}, bf16[4,2,64,256]{3,2,1,0:T(8,128)(2,1)}, u32[]{:S(2)}) copy-start(bf16[4,2,64,256]{3,2,1,0:T(8,128)(2,1)} %param.4) | copy-start | bytes 786436
  0.9 22.0 %collective-permute-start.1 = (bf16[64,256]{1,0:T(8,128)(2,1)S(1)}, bf16[64,256]{1,0:T(8,128)(2,1)S(1)}, u32[]{:S(2)}, u32[]{:S(2)}) collective-permute-start(bf16[64,256]{1,0:T(8,128)(2,1)S(1)} %convert_bitcast_fusion.refs_0_), channel_id=1, source_target_pairs={{0,512},{1,513},{2,514},{3,515},{4,516},{5,517},{6,518},{7,519},{8... | collective-permute-start | bytes 98312 | tf_op jit(solution)/shard_map/ppermute | solution.py:226
  16.0 6.9 %collective-permute-start = (bf16[64,256]{1,0:T(8,128)(2,1)S(1)}, bf16[64,256]{1,0:T(8,128)(2,1)S(1)}, u32[]{:S(2)}, u32[]{:S(2)}) collective-permute-start(bf16[64,256]{1,0:T(8,128)(2,1)S(1)} %convert_bitcast_fusion.refs_0_), channel_id=1, source_target_pairs={{0,256},{256,512},{1,257},{257,513},{2,258},{258,514},{3,259},{259... | collective-permute-start | bytes 98312 | tf_op jit(solution)/shard_map/ppermute | solution.py:226
  17.3 1.0 %copy-start.1 = (bf16[1,4,2,64,256]{4,3,2,1,0:T(8,128)(2,1)S(1)}, bf16[1,4,2,64,256]{4,3,2,1,0:T(8,128)(2,1)}, u32[]{:S(2)}) copy-start(bf16[1,4,2,64,256]{4,3,2,1,0:T(8,128)(2,1)} %param.7) | copy-start | bytes 786436
  18.5 5.1 %collective-permute-start.2 = (bf16[2,4,64,128]{3,2,1,0:T(8,128)(2,1)S(1)}, bf16[2,4,64,128]{3,2,1,0:T(8,128)(2,1)S(1)}, u32[]{:S(2)}, u32[]{:S(2)}) collective-permute-start(bf16[2,4,64,128]{3,2,1,0:T(8,128)(2,1)S(1)} %get-tuple-element.18), channel_id=1, source_target_pairs={{0,1},{1,0},{2,3},{3,2},{4,5},{5,4},{6,7},{7,6},{8,9},{9,8},{10,11... | collective-permute-start | bytes 393224 | tf_op jit(solution)/shard_map/ppermute | solution.py:242
  23.7 11.9 %all-to-all-start = ((bf16[4,3,64,256]{3,2,1,0:T(8,128)(2,1)}), bf16[4,3,64,256]{3,2,1,0:T(8,128)(2,1)S(1)}, u32[]{:S(2)}, u32[]{:S(2)}) async-start(bf16[4,3,64,256]{3,2,1,0:T(8,128)(2,1)} %spread.1), calls=%async_computation | async-start | bytes 786432 | tf_op jit(solution)/shard_map/all_to_all | solution.py:256
  27.7 9.8 %collective-permute-start.3 = (bf16[2,4,64,128]{3,2,1,0:T(8,128)(2,1)S(1)}, bf16[2,4,64,128]{3,2,1,0:T(8,128)(2,1)S(1)}, u32[]{:S(2)}, u32[]{:S(2)}) collective-permute-start(bf16[2,4,64,128]{3,2,1,0:T(8,128)(2,1)S(1)} %pad_maximum_fusion), channel_id=1, source_target_pairs={{0,2},{2,0},{1,3},{3,1},{4,6},{6,4},{5,7},{7,5},{8,10},{10,8},{9,1... | collective-permute-start | bytes 393224 | tf_op jit(solution)/shard_map/ppermute | solution.py:253

commit v6 on v5

--- a/solution.py
+++ b/solution.py
@@ -26,22 +26,35 @@
 QUAD = ("zp", "core")
 
 
-def tap_rows(table):
-    first, second = table[:, 0], table[:, 1]
-
-    def gap(n):
-        return jnp.zeros((R, 1, n), jnp.float32)
-
-    rows = []
-    for a, b in ((first[:, 0:1], -first[:, 1:2]), (first[:, 1:2], first[:, 0:1])):
-        rows.append(
-            jnp.concatenate([a[..., MID:], gap(39), b, gap(39), a[..., :MID]], axis=-1)
-        )
-    rows_first = jnp.concatenate(rows, axis=1).reshape(R * 2, LANES)
-    back = second[..., ::-1]
-    rows_second = jnp.concatenate(
-        [back[..., MID:], jnp.zeros((R, 2, LANES - TAPS), jnp.float32), back[..., :MID]], axis=-1
-    ).reshape(R * 2, LANES)
+def onehot(shape, fit, value=1.0):
+    row_at = lax.broadcasted_iota(jnp.int32, shape, 0)
+    col_at = lax.broadcasted_iota(jnp.int32, shape, 1)
+    return jnp.where(fit(row_at, col_at), value, 0.0).astype(jnp.bfloat16)
+
+
+def exact(a, b):
+    return jnp.dot(a, b, preferred_element_type=jnp.float32)
+
+
+def tap_rows(taps):
+    many = R * 2
+
+    def row(pass_at, part):
+        return lambda i, j: j == (i >> 1) * 4 + pass_at * 2 + part(i & 1)
+
+    def lanes(shift, sign=1):
+        return onehot((LANES, LANES), lambda k, n: k == ((sign * n + shift) & (LANES - 1)))
+
+    def chosen(fit):
+        return exact(fit, taps).astype(jnp.bfloat16)
+
+    shape = (many, 2 * many)
+    straight = chosen(onehot(shape, row(0, lambda p: p)))
+    row_at = lax.broadcasted_iota(jnp.int32, (many, LANES), 0)
+    crossed = exact(chosen(onehot(shape, row(0, lambda p: 1 - p))), lanes(-(QUARTER - MID)))
+    crossed = jnp.where((row_at & 1) == 0, -crossed, crossed)
+    rows_first = exact(straight, lanes(MID)) + crossed
+    rows_second = exact(chosen(onehot(shape, row(1, lambda p: p))), lanes(MID, -1))
     return rows_first, rows_second
 
 
@@ -50,18 +63,20 @@
     return pltpu.roll(wide, shift, 1, stride=1, stride_axis=0)
 
 
-def bands_kernel(rows_first_ref, rows_second_ref, band_first, band_even, band_odd):
+def bands_kernel(index_ref, table_ref, band_first, band_even, band_odd):
+    taps = table_ref[pl.ds(pl.multiple_of(index_ref[0] * 16, 16), 16), :]
+    rows_first, rows_second = tap_rows(taps)
     row_at = lax.broadcasted_iota(jnp.int32, (NX, LANES), 0)
     lane_at = lax.broadcasted_iota(jnp.int32, (NX, LANES), 1)
     near = jnp.abs((lane_at & (NX - 1)) - row_at) <= MID
     for block in range(R * 2):
-        band = fan(rows_first_ref[block : block + 1, :], NX, 0)
+        band = fan(rows_first[block : block + 1, :], NX, 0)
         band_first[block * NX : (block + 1) * NX, :] = jnp.where(near, band, 0.0).astype(jnp.bfloat16)
 
     left = lax.broadcasted_iota(jnp.int32, (LANES, LANES), 1) < QUARTER
     for region in range(R):
-        tap_real = rows_second_ref[2 * region : 2 * region + 1, :]
-        tap_imag = rows_second_ref[2 * region + 1 : 2 * region + 2, :]
+        tap_real = rows_second[2 * region : 2 * region + 1, :]
+        tap_imag = rows_second[2 * region + 1 : 2 * region + 2, :]
         cols = slice(region * LANES, (region + 1) * LANES)
         for part, (to_real, to_imag) in enumerate(((tap_real, tap_imag), (-tap_imag, tap_real))):
             rows = slice(part * LANES, (part + 1) * LANES)
@@ -79,8 +94,8 @@
 
 
 def chain_kernel(scalar_ref, band_first, band_even, band_odd, surface_ref, regions_ref, out_ref, state):
-    state[:NX, :] = surface_ref[0]
-    state[NX:, :] = surface_ref[1]
+    state[:NX, :] = surface_ref[scalar_ref[1], 0]
+    state[NX:, :] = surface_ref[scalar_ref[1], 1]
     blocks = scalar_ref[0]
     lane = lax.broadcasted_iota(jnp.int32, (NX, LANES), 1)
     left = lane < QUARTER
@@ -172,14 +187,27 @@
             wave[k * GROUP + f, REACH : REACH + NX, :] = wave_ref[f * 4 + k].astype(jnp.float32)
             src[group + f, REACH : REACH + NX, :] = sources[k][f].astype(jnp.float32)
 
-    def row(x, carry):
-        total = jnp.zeros((H, LANES), jnp.float32)
+    tall, deep = NX // 8, H // 8
+    inside = range(1, tall + deep - 2)
+
+    def rows_from(start, carry):
+        sums = {}
         for i in range(4 * GROUP):
-            total = total + wave[i, pl.ds(x, H), :] * src[i, pl.ds(NX - 1 - x, H), :]
-        totals[x] = total
+            waves = {j: wave[i, pl.ds(start + 8 * j, 8), :] for j in inside}
+            sources = {j: src[i, pl.ds(7 - start + 8 * j, 8), :] for j in inside}
+            for m in range(tall):
+                for n in range(deep):
+                    j, k = m + n, tall - 1 - m + n
+                    if j in inside and k in inside:
+                        term = waves[j] * sources[k]
+                        sums[m, n] = sums[m, n] + term if i else term
+        for m in range(tall):
+            for n in range(deep):
+                value = sums.get((m, n))
+                totals[start + 8 * m, 8 * n : 8 * n + 8, :] = jnp.zeros((8, LANES), jnp.float32) if value is None else value
         return carry
 
-    lax.fori_loop(0, NX, row, 0, unroll=4)
+    lax.fori_loop(0, 8, rows_from, 0)
     left = lax.broadcasted_iota(jnp.int32, (REACH, LANES), 1) < QUARTER
 
     def fold(x, carry):
@@ -221,7 +249,7 @@
     mine_x = lax.axis_index("x")
     core = lax.axis_index("core")
     blocks = lax.axis_size("zh")
-    local = regions[0].astype(jnp.bfloat16)
+    local, local_source = lax.optimization_barrier((regions[0].astype(jnp.bfloat16), source[0]))
     earlier = [
         lax.ppermute(local, "zh", [(i, i + k) for i in range(blocks - k)]) for k in range(1, blocks)
     ]
@@ -238,8 +266,7 @@
         compiler_params=PARAMS,
         cost_estimate=cost(20_000_000, 1_000_000),
         name="pack",
-    )(quarter, source[0])
-    from_core = lax.ppermute(to_core, "core", [(0, 1), (1, 0)])
+    )(quarter, local_source)
     copies = pl.pallas_call(
         spread_kernel,
         out_shape=jax.ShapeDtypeStruct((GROUP, blocks, NX, NY), jnp.bfloat16),
@@ -249,15 +276,14 @@
         cost_estimate=cost(1_000_000, 500_000),
         name="spread",
     )(local, *earlier)
-    copies, from_core = lax.optimization_barrier((copies, from_core))
+    copies, to_core, table = lax.optimization_barrier((copies, to_core, table))
+    from_core = lax.ppermute(to_core, "core", [(0, 1), (1, 0)])
     from_chip = lax.ppermute(
         jnp.concatenate([to_chip, from_core[1:]], axis=0), "zp", [(0, 1), (1, 0)]
     )
     all_regions = lax.all_to_all(copies, "x", 0, 0, tiled=True)
 
-    rows_first, rows_second = tap_rows(
-        lax.dynamic_index_in_dim(table, mine_x, 0, keepdims=False).astype(jnp.float32)
-    )
+    padded = jnp.pad(table.reshape(GROUP * R * 4, TAPS), ((0, 0), (0, LANES - TAPS)))
     bands = pl.pallas_call(
         bands_kernel,
         out_shape=(
@@ -265,15 +291,14 @@
             jax.ShapeDtypeStruct((2 * LANES, R * LANES), jnp.bfloat16),
             jax.ShapeDtypeStruct((2 * LANES, R * LANES), jnp.bfloat16),
         ),
-        in_specs=[VMEM] * 2,
+        in_specs=[SMEM, VMEM],
         out_specs=(VMEM,) * 3,
         compiler_params=PARAMS,
         cost_estimate=cost(10_000_000, 1_000_000),
         name="bands",
-    )(rows_first, rows_second)
-
-    entering = lax.dynamic_index_in_dim(surface, mine_x, 0, keepdims=False)
-    count = (zh + 1).astype(jnp.int32).reshape(1)
+    )(mine_x.astype(jnp.int32).reshape(1), padded)
+
+    scalars = jnp.stack([zh + 1, mine_x]).astype(jnp.int32)
     waves = pl.pallas_call(
         chain_kernel,
         out_shape=jax.ShapeDtypeStruct((GROUP * 4, NX, LANES), jnp.bfloat16),
@@ -281,9 +306,9 @@
         out_specs=VMEM,
         scratch_shapes=[pltpu.VMEM((2 * NX, NY), jnp.bfloat16)],
         compiler_params=PARAMS,
-        cost_estimate=cost(1_000_000, 100_000),
+        cost_estimate=cost(4_000_000_000, 4_000_000),
         name="chain",
-    )(count, *bands, entering, all_regions)
+    )(scalars, *bands, surface, all_regions)
 
     waves, from_chip = lax.optimization_barrier((waves, from_chip))
     waves = lax.all_to_all(waves, ("x",) + QUAD, 0, 0, tiled=True)

time: 77 us -> 77.5 us (level)
  blocking collectives: 35.3 us -> 38.9 us
  waiting for transfers between devices: 4.5 us -> 1.13 us
  starting transfers between devices: 26.4 us -> 27.4 us
    all_to_all x1, waiting for transfers between devices: 4.49 us -> 0.01 us  [body(): all_regions = lax.all_to_all(copies, 'x', 0, 0, tiled=True)]
    all_to_all x1, blocking collectives: 11.4 us -> 14.1 us  [body(): waves = lax.all_to_all(waves, ('x',) + QUAD, 0, 0, tiled=True)]
    all_to_all x1, blocking collectives: 23.9 us -> 24.8 us  [body(): parts = lax.all_to_all(partial_image, FREQ, 0, 0, tiled=True)]
    ppermute x1, waiting for transfers between devices: 0.01 us -> 0.81 us  [body(): lax.ppermute(jnp.concatenate([to_chip, from_core[1:]], axis=0), 'zp', [(0...]
    convert_element_type x2 -> x1, other arithmetic: 1.58 us -> 0.85 us  [body(): regions[0].astype(jnp.bfloat16)]
  transfers between devices with their start and end apart: 5 -> 5, of which waited for: 1 -> 2; matrix products, arithmetic and copies ran while one was open for 2% -> 0% of each run, Pallas kernels for 4% -> 4%
where the time goes in v6:
time: 77.5 us; the launch traced here: 77.1 us
  blocking collectives  38.9 us (50%)
  starting transfers between devices  27.4 us (35%)
  Pallas kernels  7.63 us (10%)
  waiting for transfers between devices  1.13 us (1%)
  local copies, waits for them, and re-layouts  0.96 us (1%)
  other arithmetic  0.94 us (1%)
    all_to_all x1, blocking collectives, body(): parts = lax.all_to_all(partial_image, FREQ, 0, 0, tiled=True)  24.8 us
    ppermute x2, starting transfers between devices, body(): lax.ppermute(local, 'zh', [(i, i + k) for i in range(blocks - k)])  16.4 us
    all_to_all x1, blocking collectives, body(): waves = lax.all_to_all(waves, ('x',) + QUAD, 0, 0, tiled=True)  14.1 us
    all_to_all x1, starting transfers between devices, body(): all_regions = lax.all_to_all(copies, 'x', 0, 0, tiled=True)  4.14 us
    ppermute x1, starting transfers between devices, body(): from_core = lax.ppermute(to_core, 'core', [(0, 1), (1, 0)])  3.56 us
    ppermute x1, starting transfers between devices, body(): lax.ppermute(jnp.concatenate([to_chip, from_core[1:]], axis=0), 'zp', [(0...  3.31 us
    pallas_call x1, Pallas kernels, body(): pl.pallas_call(lambda *refs: image_kernel(scale, *refs), out_shape=jax.Sh...  2.81 us
    pallas_call x1, Pallas kernels, body(): pl.pallas_call(chain_kernel, out_shape=jax.ShapeDtypeStruct((GROUP * 4, N...  2.47 us
  transfers between devices with their start and end apart: 5, of which 2 were waited for; matrix products, arithmetic and copies ran while one was open for 0% of the time, Pallas kernels for 4%

profile of v6, /device:TPU:1, one launch (start us, length us, event | category | flops | bytes accessed | tf_op | source)
XLA Modules:
  0.0 77.1 jit_solution(7805661329608029032)
XLA Ops:
  0.0 0.8 %convert_bitcast_fusion.refs_0_ = bf16[64,256]{1,0:T(8,128)(2,1)S(1)} fusion(s32[1,64,256]{2,1,0:T(8,128)} %param.5), kind=kLoop, calls=%fused_computation.1 | loop fusion | flops 16384 | bytes 98304 | tf_op jit(solution)/shard_map/convert_element_type | solution.py:252
  0.8 15.1 %collective-permute-start.1 = (bf16[64,256]{1,0:T(8,128)(2,1)S(1)}, bf16[64,256]{1,0:T(8,128)(2,1)S(1)}, u32[]{:S(2)}, u32[]{:S(2)}) collective-permute-start(bf16[64,256]{1,0:T(8,128)(2,1)S(1)} %convert_bitcast_fusion.refs_0_), channel_id=1, source_target_pairs={{0,512},{1,513},{2,514},{3,515},{4,516},{5,517},{6,518},{7,519},{8... | collective-permute-start | bytes 98312 | tf_op jit(solution)/shard_map/ppermute | solution.py:254
  15.9 1.3 %collective-permute-start = (bf16[64,256]{1,0:T(8,128)(2,1)S(1)}, bf16[64,256]{1,0:T(8,128)(2,1)S(1)}, u32[]{:S(2)}, u32[]{:S(2)}) collective-permute-start(bf16[64,256]{1,0:T(8,128)(2,1)S(1)} %convert_bitcast_fusion.refs_0_), channel_id=1, source_target_pairs={{0,256},{256,512},{1,257},{257,513},{2,258},{258,514},{3,259},{259... | collective-permute-start | bytes 98312 | tf_op jit(solution)/shard_map/ppermute | solution.py:254
  17.2 0.0 copy-start
  17.3 0.9 %copy-done = bf16[1,4,2,64,256]{4,3,2,1,0:T(8,128)(2,1)S(1)} copy-done((bf16[1,4,2,64,256]{4,3,2,1,0:T(8,128)(2,1)S(1)}, bf16[1,4,2,64,256]{4,3,2,1,0:T(8,128)(2,1)}, u32[]{:S(2)}) %copy-start) | copy-done | bytes 262168
  18.2 0.3 pack.1
  18.5 0.0 collective-permute-done.1.refs_2_
  18.5 0.0 collective-permute-done.refs_1_
  18.5 0.8 %spread.1 = bf16[4,3,64,256]{3,2,1,0:T(8,128)(2,1)} custom-call(bf16[64,256]{1,0:T(8,128)(2,1)S(1)} %convert_bitcast_fusion.refs_0_, bf16[64,256]{1,0:T(8,128)(2,1)S(1)} %collective-permute-done.refs_1_, bf16[64,256]{1,0:T(8,128)(2,1)S(1)} %collective-permute-done.1.refs_2_), custom_call_target="tpu_custom_call" | custom-call | flops 1000000 | bytes 500000 | tf_op jit(solution)/shard_map/spread/pallas_call | solution.py:270
  19.3 0.0 copy-start.2
  19.3 4.1 %all-to-all-start = ((bf16[4,3,64,256]{3,2,1,0:T(8,128)(2,1)}), bf16[4,3,64,256]{3,2,1,0:T(8,128)(2,1)S(1)}, u32[]{:S(2)}, u32[]{:S(2)}) async-start(bf16[4,3,64,256]{3,2,1,0:T(8,128)(2,1)} %spread.1), calls=%async_computation | async-start | bytes 786432 | tf_op jit(solution)/shard_map/all_to_all | solution.py:284
  23.4 0.0 copy-start.1
  23.4 3.6 %collective-permute-start.2 = (bf16[2,4,64,128]{3,2,1,0:T(8,128)(2,1)S(1)}, bf16[2,4,64,128]{3,2,1,0:T(8,128)(2,1)S(1)}, u32[]{:S(2)}, u32[]{:S(2)}) collective-permute-start(bf16[2,4,64,128]{3,2,1,0:T(8,128)(2,1)S(1)} %get-tuple-element.27), channel_id=1, source_target_pairs={{0,1},{1,0},{2,3},{3,2},{4,5},{5,4},{6,7},{7,6},{8,9},{9,8},{10,11... | collective-permute-start | bytes 393224 | tf_op jit(solution)/shard_map/ppermute | solution.py:280
  27.0 0.1 pad_add_fusion.scalar_ref
  27.1 0.0 copy-done.2
  27.1 0.5 bands.1
  27.7 0.3 collective-permute-done.2.refs_3_
  28.0 3.3 %collective-permute-start.3 = (bf16[2,4,64,128]{3,2,1,0:T(8,128)(2,1)S(1)}, bf16[2,4,64,128]{3,2,1,0:T(8,128)(2,1)S(1)}, u32[]{:S(2)}, u32[]{:S(2)}) collective-permute-start(bf16[2,4,64,128]{3,2,1,0:T(8,128)(2,1)S(1)} %pad_maximum_fusion), channel_id=1, source_target_pairs={{0,2},{2,0},{1,3},{3,1},{4,6},{6,4},{5,7},{7,5},{8,10},{10,8},{9,1... | collective-permute-start | bytes 393224 | tf_op jit(solution)/shard_map/ppermute | solution.py:281
  31.3 0.0 all-to-all-done.regions_ref
  31.3 0.0 copy-done.1
  31.3 2.5 %chain.1 = bf16[16,64,128]{2,1,0:T(8,128)(2,1)S(1)} custom-call(s32[2]{0:T(128)S(1)} %pad_add_fusion.scalar_ref, bf16[512,128]{1,0:T(8,128)(2,1)S(1)} %get-tuple-element.22.band_first, bf16[256,512]{1,0:T(8,128)(2,1)S(1)} %get-tuple-element.23.band_even, bf16[256,512]{1,0:T(8,128)(2,1)S(1)} %get-tuple-element.24.band_odd, ...), custom_call_target="tpu_custom_call" | custom-call | flops 4000000000 | bytes 4000000 | tf_op jit(solution)/shard_map/chain/pallas_call | solution.py:302
  33.8 0.8 %collective-permute-done.3.refs_4_ = bf16[2,4,64,128]{3,2,1,0:T(8,128)(2,1)S(1)} collective-permute-done((bf16[2,4,64,128]{3,2,1,0:T(8,128)(2,1)S(1)}, bf16[2,4,64,128]{3,2,1,0:T(8,128)(2,1)S(1)}, u32[]{:S(2)}, u32[]{:S(2)}) %collective-permute-start.3) | collective-permute-done | bytes 131104 | tf_op jit(solution)/shard_map/ppermute | solution.py:281
  34.6 14.1 %all_to_all.15.refs_1_ = bf16[16,64,128]{2,1,0:T(8,128)(2,1)S(1)} all-to-all(bf16[16,64,128]{2,1,0:T(8,128)(2,1)S(1)} %chain.1), channel_id=1, replica_groups=mesh['zh'=3,'x'=4,'y'=8,'zq'=2,'zp'=2,'core'=2] {'x','zp','core'}, dimensions={0} | all-to-all | bytes 524288 | tf_op jit(solution)/shard_map/all_to_all | solution.py:314
  48.7 2.8 %image.1 = bf16[64,16,128]{2,1,0:T(8,128)(2,1)S(1)} custom-call(s32[1]{0:T(128)} %bitcast.quarter_ref.refs_0_, bf16[16,64,128]{2,1,0:T(8,128)(2,1)S(1)} %all_to_all.15.refs_1_, bf16[4,64,128]{2,1,0:T(8,128)(2,1)S(1)} %get-tuple-element.29.refs_2_, bf16[2,4,64,128]{3,2,1,0:T(8,128)(2,1)S(1)} %collective-permute-done.2.refs_3_, ...), custom_call_target="tpu_custom_call" | custom-call | flops 10000000 | bytes 2000000 | tf_op jit(solution)/shard_map/image/pallas_call | solution.py:317
  51.5 24.8 %all_to_all.16.part_ref = bf16[64,16,128]{2,1,0:T(8,128)(2,1)S(1)} all-to-all(bf16[64,16,128]{2,1,0:T(8,128)(2,1)S(1)} %image.1), channel_id=1, replica_groups=mesh['zh'=3,'x'=4,'y'=8,'zq'=2,'zp'=2,'core'=2] {'y','zq','zp','core'}, dimensions={0} | all-to-all | bytes 524288 | tf_op jit(solution)/shard_map/all_to_all | solution.py:329
  76.3 0.7 total.1
  (3 shorter events, 0.0 us)
Async XLA Ops:
  0.8 17.7 %collective-permute-start.1 = (bf16[64,256]{1,0:T(8,128)(2,1)S(1)}, bf16[64,256]{1,0:T(8,128)(2,1)S(1)}, u32[]{:S(2)}, u32[]{:S(2)}) collective-permute-start(bf16[64,256]{1,0:T(8,128)(2,1)S(1)} %convert_bitcast_fusion.refs_0_), channel_id=1, source_target_pairs={{0,512},{1,513},{2,514},{3,515},{4,516},{5,517},{6,518},{7,519},{8... | collective-permute-start | bytes 98312 | tf_op jit(solution)/shard_map/ppermute | solution.py:254
  15.9 2.6 %collective-permute-start = (bf16[64,256]{1,0:T(8,128)(2,1)S(1)}, bf16[64,256]{1,0:T(8,128)(2,1)S(1)}, u32[]{:S(2)}, u32[]{:S(2)}) collective-permute-start(bf16[64,256]{1,0:T(8,128)(2,1)S(1)} %convert_bitcast_fusion.refs_0_), channel_id=1, source_target_pairs={{0,256},{256,512},{1,257},{257,513},{2,258},{258,514},{3,259},{259... | collective-permute-start | bytes 98312 | tf_op jit(solution)/shard_map/ppermute | solution.py:254
  17.2 1.0 %copy-start = (bf16[1,4,2,64,256]{4,3,2,1,0:T(8,128)(2,1)S(1)}, bf16[1,4,2,64,256]{4,3,2,1,0:T(8,128)(2,1)}, u32[]{:S(2)}) copy-start(bf16[1,4,2,64,256]{4,3,2,1,0:T(8,128)(2,1)} %param.7) | copy-start | bytes 786436
  19.3 7.8 %copy-start.2 = (bf16[4,4,2,2,25]{4,3,2,1,0:T(2,128)(2,1)S(1)}, bf16[4,4,2,2,25]{4,3,2,1,0:T(2,128)(2,1)}, u32[]{:S(2)}) copy-start(bf16[4,4,2,2,25]{4,3,2,1,0:T(2,128)(2,1)} %param.6) | copy-start | bytes 9604
  19.3 12.0 %all-to-all-start = ((bf16[4,3,64,256]{3,2,1,0:T(8,128)(2,1)}), bf16[4,3,64,256]{3,2,1,0:T(8,128)(2,1)S(1)}, u32[]{:S(2)}, u32[]{:S(2)}) async-start(bf16[4,3,64,256]{3,2,1,0:T(8,128)(2,1)} %spread.1), calls=%async_computation | async-start | bytes 786432 | tf_op jit(solution)/shard_map/all_to_all | solution.py:284
  23.4 7.9 %copy-start.1 = (bf16[4,2,64,256]{3,2,1,0:T(8,128)(2,1)S(1)}, bf16[4,2,64,256]{3,2,1,0:T(8,128)(2,1)}, u32[]{:S(2)}) copy-start(bf16[4,2,64,256]{3,2,1,0:T(8,128)(2,1)} %surface_ref.1) | copy-start | bytes 786436
  23.4 4.5 %collective-permute-start.2 = (bf16[2,4,64,128]{3,2,1,0:T(8,128)(2,1)S(1)}, bf16[2,4,64,128]{3,2,1,0:T(8,128)(2,1)S(1)}, u32[]{:S(2)}, u32[]{:S(2)}) collective-permute-start(bf16[2,4,64,128]{3,2,1,0:T(8,128)(2,1)S(1)} %get-tuple-element.27), channel_id=1, source_target_pairs={{0,1},{1,0},{2,3},{3,2},{4,5},{5,4},{6,7},{7,6},{8,9},{9,8},{10,11... | collective-permute-start | bytes 393224 | tf_op jit(solution)/shard_map/ppermute | solution.py:280
  28.0 6.6 %collective-permute-start.3 = (bf16[2,4,64,128]{3,2,1,0:T(8,128)(2,1)S(1)}, bf16[2,4,64,128]{3,2,1,0:T(8,128)(2,1)S(1)}, u32[]{:S(2)}, u32[]{:S(2)}) collective-permute-start(bf16[2,4,64,128]{3,2,1,0:T(8,128)(2,1)S(1)} %pad_maximum_fusion), channel_id=1, source_target_pairs={{0,2},{2,0},{1,3},{3,1},{4,6},{6,4},{5,7},{7,5},{8,10},{10,8},{9,1... | collective-permute-start | bytes 393224 | tf_op jit(solution)/shard_map/ppermute | solution.py:281

commit v7 on v6

--- a/solution.py
+++ b/solution.py
@@ -93,7 +93,10 @@
     return out
 
 
-def chain_kernel(scalar_ref, band_first, band_even, band_odd, surface_ref, regions_ref, out_ref, state):
+def chain_kernel(scalar_ref, band_first, band_even, band_odd, surface_ref, *refs):
+    columns, out_ref, state, regions_ref = refs[:GROUP], refs[GROUP], refs[GROUP + 1], refs[GROUP + 2]
+    for k in range(GROUP):
+        regions_ref[scalar_ref[1] ^ k] = columns[k][...]
     state[:NX, :] = surface_ref[scalar_ref[1], 0]
     state[NX:, :] = surface_ref[scalar_ref[1], 1]
     blocks = scalar_ref[0]
@@ -146,11 +149,19 @@
     lax.fori_loop(0, blocks, block, 0)
 
 
-def spread_kernel(*refs):
-    out_ref = refs[-1]
-    for i in range(out_ref.shape[0]):
-        for slot, ref in enumerate(refs[:-1]):
-            out_ref[i, slot] = ref[...]
+def stack_kernel(zh_ref, local_ref, near_ref, far_ref, out_ref):
+    last = zh_ref[0] == 2
+    out_ref[0] = local_ref[...]
+
+    @pl.when(last)
+    def _():
+        out_ref[1] = far_ref[0]
+        out_ref[2] = far_ref[1]
+
+    @pl.when(jnp.logical_not(last))
+    def _():
+        out_ref[1] = near_ref[...]
+        out_ref[2] = near_ref[...]
 
 
 def pack_kernel(quarter_ref, source_ref, *refs):
@@ -250,9 +261,8 @@
     core = lax.axis_index("core")
     blocks = lax.axis_size("zh")
     local, local_source = lax.optimization_barrier((regions[0].astype(jnp.bfloat16), source[0]))
-    earlier = [
-        lax.ppermute(local, "zh", [(i, i + k) for i in range(blocks - k)]) for k in range(1, blocks)
-    ]
+    near = lax.ppermute(local, "zh", [(0, 1)])
+    far = lax.ppermute(jnp.stack([local, near]), "zh", [(1, 2)])
     quarter = (lax.axis_index("zp") * 2 + core).astype(jnp.int32).reshape(1)
     four = jax.ShapeDtypeStruct((GROUP, NX, LANES), jnp.bfloat16)
     pair = jax.ShapeDtypeStruct((2, GROUP, NX, LANES), jnp.bfloat16)
@@ -267,21 +277,23 @@
         cost_estimate=cost(20_000_000, 1_000_000),
         name="pack",
     )(quarter, local_source)
-    copies = pl.pallas_call(
-        spread_kernel,
-        out_shape=jax.ShapeDtypeStruct((GROUP, blocks, NX, NY), jnp.bfloat16),
-        in_specs=[VMEM] * blocks,
+    column = pl.pallas_call(
+        stack_kernel,
+        out_shape=jax.ShapeDtypeStruct((blocks, NX, NY), jnp.bfloat16),
+        in_specs=[SMEM] + [VMEM] * 3,
         out_specs=VMEM,
         compiler_params=PARAMS,
         cost_estimate=cost(1_000_000, 500_000),
-        name="spread",
-    )(local, *earlier)
-    copies, to_core, table = lax.optimization_barrier((copies, to_core, table))
+        name="stack",
+    )(zh.astype(jnp.int32).reshape(1), local, near, far)
     from_core = lax.ppermute(to_core, "core", [(0, 1), (1, 0)])
+    column, from_core, table = lax.optimization_barrier((column, from_core, table))
     from_chip = lax.ppermute(
         jnp.concatenate([to_chip, from_core[1:]], axis=0), "zp", [(0, 1), (1, 0)]
     )
-    all_regions = lax.all_to_all(copies, "x", 0, 0, tiled=True)
+    columns = [column] + [
+        lax.ppermute(column, "x", [(i, i ^ k) for i in range(GROUP)]) for k in range(1, GROUP)
+    ]
 
     padded = jnp.pad(table.reshape(GROUP * R * 4, TAPS), ((0, 0), (0, LANES - TAPS)))
     bands = pl.pallas_call(
@@ -302,13 +314,16 @@
     waves = pl.pallas_call(
         chain_kernel,
         out_shape=jax.ShapeDtypeStruct((GROUP * 4, NX, LANES), jnp.bfloat16),
-        in_specs=[SMEM] + [VMEM] * 5,
+        in_specs=[SMEM] + [VMEM] * (4 + GROUP),
         out_specs=VMEM,
-        scratch_shapes=[pltpu.VMEM((2 * NX, NY), jnp.bfloat16)],
+        scratch_shapes=[
+            pltpu.VMEM((2 * NX, NY), jnp.bfloat16),
+            pltpu.VMEM((GROUP, blocks, NX, NY), jnp.bfloat16),
+        ],
         compiler_params=PARAMS,
         cost_estimate=cost(4_000_000_000, 4_000_000),
         name="chain",
-    )(scalars, *bands, surface, all_regions)
+    )(scalars, *bands, surface, *columns)
 
     waves, from_chip = lax.optimization_barrier((waves, from_chip))
     waves = lax.all_to_all(waves, ("x",) + QUAD, 0, 0, tiled=True)

time: 77.5 us -> 79.8 us (1.030)
  the two profiles are of different devices: /device:TPU:1 before, /device:TPU:513 now
where the time goes in v7:
time: 79.8 us; the launch traced here: 79.3 us
  blocking collectives  39.1 us (49%)
  starting transfers between devices  19.2 us (24%)
  Pallas kernels  10.8 us (14%)
  waiting for transfers between devices  8.15 us (10%)
  local copies, waits for them, and re-layouts  0.97 us (1%)
  other arithmetic  0.95 us (1%)
    all_to_all x1, blocking collectives, body(): parts = lax.all_to_all(partial_image, FREQ, 0, 0, tiled=True)  26.4 us
    all_to_all x1, blocking collectives, body(): waves = lax.all_to_all(waves, ('x',) + QUAD, 0, 0, tiled=True)  12.8 us
    ppermute x3, starting transfers between devices, body(): lax.ppermute(column, 'x', [(i, i ^ k) for i in range(GROUP)])  9.72 us
    ppermute x1, waiting for transfers between devices, body(): far = lax.ppermute(jnp.stack([local, near]), 'zh', [(1, 2)])  8.14 us
    pallas_call x1, Pallas kernels, body(): pl.pallas_call(chain_kernel, out_shape=jax.ShapeDtypeStruct((GROUP * 4, N...  6.38 us
    ppermute x1, starting transfers between devices, body(): lax.ppermute(jnp.concatenate([to_chip, from_core[1:]], axis=0), 'zp', [(0...  4.92 us
    pallas_call x1, Pallas kernels, body(): pl.pallas_call(lambda *refs: image_kernel(scale, *refs), out_shape=jax.Sh...  2.81 us
    ppermute x1, starting transfers between devices, body(): from_core = lax.ppermute(to_core, 'core', [(0, 1), (1, 0)])  2.58 us
  transfers between devices with their start and end apart: 7, of which 1 were waited for; matrix products, arithmetic and copies ran while one was open for 0% of the time, Pallas kernels for 9%

profile of v7, /device:TPU:513, one launch (start us, length us, event | category | flops | bytes accessed | tf_op | source)
XLA Modules:
  0.0 79.3 jit_solution(11956825792371559164)
XLA Ops:
  0.0 0.8 %convert_bitcast_fusion.local_ref = bf16[64,256]{1,0:T(8,128)(2,1)S(1)} fusion(s32[1,64,256]{2,1,0:T(8,128)} %param.5), kind=kLoop, calls=%fused_computation.2 | loop fusion | flops 16384 | bytes 98304 | tf_op jit(solution)/shard_map/convert_element_type | solution.py:263
  0.8 0.7 collective-permute-start
  1.5 0.0 copy-start
  1.5 0.9 %copy-done = bf16[1,4,2,64,256]{4,3,2,1,0:T(8,128)(2,1)S(1)} copy-done((bf16[1,4,2,64,256]{4,3,2,1,0:T(8,128)(2,1)S(1)}, bf16[1,4,2,64,256]{4,3,2,1,0:T(8,128)(2,1)}, u32[]{:S(2)}) %copy-start) | copy-done | bytes 262168
  2.5 0.3 pack.1
  2.8 2.6 %collective-permute-start.2 = (bf16[2,4,64,128]{3,2,1,0:T(8,128)(2,1)S(1)}, bf16[2,4,64,128]{3,2,1,0:T(8,128)(2,1)S(1)}, u32[]{:S(2)}, u32[]{:S(2)}) collective-permute-start(bf16[2,4,64,128]{3,2,1,0:T(8,128)(2,1)S(1)} %get-tuple-element.20), channel_id=1, source_target_pairs={{0,1},{1,0},{2,3},{3,2},{4,5},{5,4},{6,7},{7,6},{8,9},{9,8},{10,11... | collective-permute-start | bytes 393224 | tf_op jit(solution)/shard_map/ppermute | solution.py:289
  5.4 0.0 collective-permute-done.near_ref
  5.4 1.3 %collective-permute-start.1 = (bf16[2,64,256]{2,1,0:T(8,128)(2,1)S(1)}, bf16[2,64,256]{2,1,0:T(8,128)(2,1)S(1)}, u32[]{:S(2)}, u32[]{:S(2)}) collective-permute-start(bf16[2,64,256]{2,1,0:T(8,128)(2,1)S(1)} %pad_maximum_fusion.1), channel_id=1, source_target_pairs={{256,512},{257,513},{258,514},{259,515},{260,516},{261,517},{262,5... | collective-permute-start | bytes 196616 | tf_op jit(solution)/shard_map/ppermute | solution.py:265
  6.7 0.1 pad_add_fusion.scalar_ref
  6.8 8.1 %collective-permute-done.1.far_ref = bf16[2,64,256]{2,1,0:T(8,128)(2,1)S(1)} collective-permute-done((bf16[2,64,256]{2,1,0:T(8,128)(2,1)S(1)}, bf16[2,64,256]{2,1,0:T(8,128)(2,1)S(1)}, u32[]{:S(2)}, u32[]{:S(2)}) %collective-permute-start.1) | collective-permute-done | bytes 65568 | tf_op jit(solution)/shard_map/ppermute | solution.py:265
  14.9 0.0 copy-start.1
  14.9 0.0 collective-permute-done.2.refs_3_
  15.0 3.2 %collective-permute-start.3 = (bf16[3,64,256]{2,1,0:T(8,128)(2,1)S(1)}, bf16[3,64,256]{2,1,0:T(8,128)(2,1)S(1)}, u32[]{:S(2)}, u32[]{:S(2)}) collective-permute-start(bf16[3,64,256]{2,1,0:T(8,128)(2,1)S(1)} %stack.25.refs_0_), channel_id=1, source_target_pairs={{0,64},{64,0},{128,192},{192,128},{1,65},{65,1},{129,193},{193,129... | collective-permute-start | bytes 294920 | tf_op jit(solution)/shard_map/ppermute | solution.py:295
  18.2 4.4 %collective-permute-start.4 = (bf16[3,64,256]{2,1,0:T(8,128)(2,1)S(1)}, bf16[3,64,256]{2,1,0:T(8,128)(2,1)S(1)}, u32[]{:S(2)}, u32[]{:S(2)}) collective-permute-start(bf16[3,64,256]{2,1,0:T(8,128)(2,1)S(1)} %stack.25.refs_0_), channel_id=1, source_target_pairs={{0,128},{64,192},{128,0},{192,64},{1,129},{65,193},{129,1},{193,65... | collective-permute-start | bytes 294920 | tf_op jit(solution)/shard_map/ppermute | solution.py:295
  22.6 2.1 %collective-permute-start.5 = (bf16[3,64,256]{2,1,0:T(8,128)(2,1)S(1)}, bf16[3,64,256]{2,1,0:T(8,128)(2,1)S(1)}, u32[]{:S(2)}, u32[]{:S(2)}) collective-permute-start(bf16[3,64,256]{2,1,0:T(8,128)(2,1)S(1)} %stack.25.refs_0_), channel_id=1, source_target_pairs={{0,192},{64,128},{128,64},{192,0},{1,193},{65,129},{129,65},{193,1... | collective-permute-start | bytes 294920 | tf_op jit(solution)/shard_map/ppermute | solution.py:295
  24.7 0.0 copy-start.2
  24.7 4.9 %collective-permute-start.6 = (bf16[2,4,64,128]{3,2,1,0:T(8,128)(2,1)S(1)}, bf16[2,4,64,128]{3,2,1,0:T(8,128)(2,1)S(1)}, u32[]{:S(2)}, u32[]{:S(2)}) collective-permute-start(bf16[2,4,64,128]{3,2,1,0:T(8,128)(2,1)S(1)} %pad_maximum_fusion), channel_id=1, source_target_pairs={{0,2},{2,0},{1,3},{3,1},{4,6},{6,4},{5,7},{7,5},{8,10},{10,8},{9,1... | collective-permute-start | bytes 393224 | tf_op jit(solution)/shard_map/ppermute | solution.py:291
  29.7 0.0 copy-done.2
  29.7 0.5 bands.1
  30.2 0.0 collective-permute-done.3.refs_1_
  30.3 0.0 collective-permute-done.4.refs_2_
  30.3 0.0 collective-permute-done.5.refs_3_
  30.3 0.0 copy-done.1
  30.3 6.4 %chain.1 = bf16[16,64,128]{2,1,0:T(8,128)(2,1)S(1)} custom-call(s32[2]{0:T(128)S(1)} %pad_add_fusion.scalar_ref, bf16[512,128]{1,0:T(8,128)(2,1)S(1)} %get-tuple-element.22.band_first, bf16[256,512]{1,0:T(8,128)(2,1)S(1)} %get-tuple-element.23.band_even, bf16[256,512]{1,0:T(8,128)(2,1)S(1)} %get-tuple-element.24.band_odd, ...), custom_call_target="tpu_custom_call" | custom-call | flops 4000000000 | bytes 4000000 | tf_op jit(solution)/shard_map/chain/pallas_call | solution.py:314
  36.7 0.0 collective-permute-done.6.refs_4_
  36.7 12.8 %all_to_all.10.refs_1_ = bf16[16,64,128]{2,1,0:T(8,128)(2,1)S(1)} all-to-all(bf16[16,64,128]{2,1,0:T(8,128)(2,1)S(1)} %chain.1), channel_id=1, replica_groups=mesh['zh'=3,'x'=4,'y'=8,'zq'=2,'zp'=2,'core'=2] {'x','zp','core'}, dimensions={0} | all-to-all | bytes 524288 | tf_op jit(solution)/shard_map/all_to_all | solution.py:329
  49.4 2.8 %image.1 = bf16[64,16,128]{2,1,0:T(8,128)(2,1)S(1)} custom-call(s32[1]{0:T(128)} %bitcast.quarter_ref.refs_0_, bf16[16,64,128]{2,1,0:T(8,128)(2,1)S(1)} %all_to_all.10.refs_1_, bf16[4,64,128]{2,1,0:T(8,128)(2,1)S(1)} %get-tuple-element.29.refs_2_, bf16[2,4,64,128]{3,2,1,0:T(8,128)(2,1)S(1)} %collective-permute-done.2.refs_3_, ...), custom_call_target="tpu_custom_call" | custom-call | flops 10000000 | bytes 2000000 | tf_op jit(solution)/shard_map/image/pallas_call | solution.py:332
  52.2 26.4 %all_to_all.11.part_ref = bf16[64,16,128]{2,1,0:T(8,128)(2,1)S(1)} all-to-all(bf16[64,16,128]{2,1,0:T(8,128)(2,1)S(1)} %image.1), channel_id=1, replica_groups=mesh['zh'=3,'x'=4,'y'=8,'zq'=2,'zp'=2,'core'=2] {'y','zq','zp','core'}, dimensions={0} | all-to-all | bytes 524288 | tf_op jit(solution)/shard_map/all_to_all | solution.py:344
  78.6 0.7 total.1
  (5 shorter events, 0.0 us)
Async XLA Ops:
  0.8 4.5 %collective-permute-start = (bf16[64,256]{1,0:T(8,128)(2,1)S(1)}, bf16[64,256]{1,0:T(8,128)(2,1)S(1)}, u32[]{:S(2)}, u32[]{:S(2)}) collective-permute-start(bf16[64,256]{1,0:T(8,128)(2,1)S(1)} %convert_bitcast_fusion.local_ref), channel_id=1, source_target_pairs={{0,256},{1,257},{2,258},{3,259},{4,260},{5,261},{6,262},{7,263},{8... | collective-permute-start | bytes 98312 | tf_op jit(solution)/shard_map/ppermute | solution.py:264
  1.5 1.0 %copy-start = (bf16[1,4,2,64,256]{4,3,2,1,0:T(8,128)(2,1)S(1)}, bf16[1,4,2,64,256]{4,3,2,1,0:T(8,128)(2,1)}, u32[]{:S(2)}) copy-start(bf16[1,4,2,64,256]{4,3,2,1,0:T(8,128)(2,1)} %param.7) | copy-start | bytes 786436
  2.8 12.2 %collective-permute-start.2 = (bf16[2,4,64,128]{3,2,1,0:T(8,128)(2,1)S(1)}, bf16[2,4,64,128]{3,2,1,0:T(8,128)(2,1)S(1)}, u32[]{:S(2)}, u32[]{:S(2)}) collective-permute-start(bf16[2,4,64,128]{3,2,1,0:T(8,128)(2,1)S(1)} %get-tuple-element.20), channel_id=1, source_target_pairs={{0,1},{1,0},{2,3},{3,2},{4,5},{5,4},{6,7},{7,6},{8,9},{9,8},{10,11... | collective-permute-start | bytes 393224 | tf_op jit(solution)/shard_map/ppermute | solution.py:289
  5.4 9.5 %collective-permute-start.1 = (bf16[2,64,256]{2,1,0:T(8,128)(2,1)S(1)}, bf16[2,64,256]{2,1,0:T(8,128)(2,1)S(1)}, u32[]{:S(2)}, u32[]{:S(2)}) collective-permute-start(bf16[2,64,256]{2,1,0:T(8,128)(2,1)S(1)} %pad_maximum_fusion.1), channel_id=1, source_target_pairs={{256,512},{257,513},{258,514},{259,515},{260,516},{261,517},{262,5... | collective-permute-start | bytes 196616 | tf_op jit(solution)/shard_map/ppermute | solution.py:265
  14.9 15.3 %copy-start.1 = (bf16[4,2,64,256]{3,2,1,0:T(8,128)(2,1)S(1)}, bf16[4,2,64,256]{3,2,1,0:T(8,128)(2,1)}, u32[]{:S(2)}) copy-start(bf16[4,2,64,256]{3,2,1,0:T(8,128)(2,1)} %surface_ref.1) | copy-start | bytes 786436
  15.0 15.3 %collective-permute-start.3 = (bf16[3,64,256]{2,1,0:T(8,128)(2,1)S(1)}, bf16[3,64,256]{2,1,0:T(8,128)(2,1)S(1)}, u32[]{:S(2)}, u32[]{:S(2)}) collective-permute-start(bf16[3,64,256]{2,1,0:T(8,128)(2,1)S(1)} %stack.25.refs_0_), channel_id=1, source_target_pairs={{0,64},{64,0},{128,192},{192,128},{1,65},{65,1},{129,193},{193,129... | collective-permute-start | bytes 294920 | tf_op jit(solution)/shard_map/ppermute | solution.py:295
  18.2 12.1 %collective-permute-start.4 = (bf16[3,64,256]{2,1,0:T(8,128)(2,1)S(1)}, bf16[3,64,256]{2,1,0:T(8,128)(2,1)S(1)}, u32[]{:S(2)}, u32[]{:S(2)}) collective-permute-start(bf16[3,64,256]{2,1,0:T(8,128)(2,1)S(1)} %stack.25.refs_0_), channel_id=1, source_target_pairs={{0,128},{64,192},{128,0},{192,64},{1,129},{65,193},{129,1},{193,65... | collective-permute-start | bytes 294920 | tf_op jit(solution)/shard_map/ppermute | solution.py:295
  22.6 7.7 %collective-permute-start.5 = (bf16[3,64,256]{2,1,0:T(8,128)(2,1)S(1)}, bf16[3,64,256]{2,1,0:T(8,128)(2,1)S(1)}, u32[]{:S(2)}, u32[]{:S(2)}) collective-permute-start(bf16[3,64,256]{2,1,0:T(8,128)(2,1)S(1)} %stack.25.refs_0_), channel_id=1, source_target_pairs={{0,192},{64,128},{128,64},{192,0},{1,193},{65,129},{129,65},{193,1... | collective-permute-start | bytes 294920 | tf_op jit(solution)/shard_map/ppermute | solution.py:295
  24.7 5.0 %copy-start.2 = (bf16[4,4,2,2,25]{4,3,2,1,0:T(2,128)(2,1)S(1)}, bf16[4,4,2,2,25]{4,3,2,1,0:T(2,128)(2,1)}, u32[]{:S(2)}) copy-start(bf16[4,4,2,2,25]{4,3,2,1,0:T(2,128)(2,1)} %param.6) | copy-start | bytes 9604
  24.7 11.9 %collective-permute-start.6 = (bf16[2,4,64,128]{3,2,1,0:T(8,128)(2,1)S(1)}, bf16[2,4,64,128]{3,2,1,0:T(8,128)(2,1)S(1)}, u32[]{:S(2)}, u32[]{:S(2)}) collective-permute-start(bf16[2,4,64,128]{3,2,1,0:T(8,128)(2,1)S(1)} %pad_maximum_fusion), channel_id=1, source_target_pairs={{0,2},{2,0},{1,3},{3,1},{4,6},{6,4},{5,7},{7,5},{8,10},{10,8},{9,1... | collective-permute-start | bytes 393224 | tf_op jit(solution)/shard_map/ppermute | solution.py:291

commit v8 on v6

--- a/solution.py
+++ b/solution.py
@@ -93,10 +93,22 @@
     return out
 
 
-def chain_kernel(scalar_ref, band_first, band_even, band_odd, surface_ref, regions_ref, out_ref, state):
-    state[:NX, :] = surface_ref[scalar_ref[1], 0]
-    state[NX:, :] = surface_ref[scalar_ref[1], 1]
-    blocks = scalar_ref[0]
+def chain_kernel(turn_ref, band_first, band_even, band_odd, entering_ref, regions_ref, *refs):
+    out_ref, state = refs[-2:]
+    active = turn_ref[0] == 1
+
+    @pl.when(active)
+    def _():
+        run_steps(band_first, band_even, band_odd, entering_ref, regions_ref, out_ref, state)
+
+    @pl.when(jnp.logical_not(active))
+    def _():
+        out_ref[...] = refs[0][...] if len(refs) == 3 else jnp.zeros_like(out_ref)
+        state[...] = jnp.zeros_like(state)
+
+
+def run_steps(band_first, band_even, band_odd, entering_ref, regions_ref, out_ref, state):
+    state[...] = entering_ref[...]
     lane = lax.broadcasted_iota(jnp.int32, (NX, LANES), 1)
     left = lane < QUARTER
     low = lane < 96
@@ -105,8 +117,8 @@
     def split(values):
         return [values == float(r) for r in range(R - 1)]
 
-    def step(b, slot):
-        region = regions_ref[slot, blocks - 1 - b].astype(jnp.float32)
+    for slot in range(GROUP):
+        region = regions_ref[slot].astype(jnp.float32)
         halves = [region[:, :LANES], region[:, LANES:]]
         turned = [pltpu.roll(half, QUARTER, 1) for half in halves]
         full = split(region)
@@ -138,20 +150,6 @@
             state[:NX, cols] = jnp.where(left, e, o).astype(jnp.bfloat16)
             state[NX:, cols] = pltpu.roll(jnp.where(left, o, e), QUARTER, 1).astype(jnp.bfloat16)
 
-    def block(b, carry):
-        for slot in range(GROUP):
-            step(b, slot)
-        return carry
-
-    lax.fori_loop(0, blocks, block, 0)
-
-
-def spread_kernel(*refs):
-    out_ref = refs[-1]
-    for i in range(out_ref.shape[0]):
-        for slot, ref in enumerate(refs[:-1]):
-            out_ref[i, slot] = ref[...]
-
 
 def pack_kernel(quarter_ref, source_ref, *refs):
     own_ref, core_ref, chip_ref, packed = refs
@@ -249,10 +247,10 @@
     mine_x = lax.axis_index("x")
     core = lax.axis_index("core")
     blocks = lax.axis_size("zh")
-    local, local_source = lax.optimization_barrier((regions[0].astype(jnp.bfloat16), source[0]))
-    earlier = [
-        lax.ppermute(local, "zh", [(i, i + k) for i in range(blocks - k)]) for k in range(1, blocks)
-    ]
+    local = regions[0].astype(jnp.bfloat16)
+    copies = jnp.broadcast_to(local[None], (GROUP, NX, NY))
+    copies, local_source, table = lax.optimization_barrier((copies, source[0], table))
+    all_regions = lax.all_to_all(copies, "x", 0, 0, tiled=True)
     quarter = (lax.axis_index("zp") * 2 + core).astype(jnp.int32).reshape(1)
     four = jax.ShapeDtypeStruct((GROUP, NX, LANES), jnp.bfloat16)
     pair = jax.ShapeDtypeStruct((2, GROUP, NX, LANES), jnp.bfloat16)
@@ -267,21 +265,10 @@
         cost_estimate=cost(20_000_000, 1_000_000),
         name="pack",
     )(quarter, local_source)
-    copies = pl.pallas_call(
-        spread_kernel,
-        out_shape=jax.ShapeDtypeStruct((GROUP, blocks, NX, NY), jnp.bfloat16),
-        in_specs=[VMEM] * blocks,
-        out_specs=VMEM,
-        compiler_params=PARAMS,
-        cost_estimate=cost(1_000_000, 500_000),
-        name="spread",
-    )(local, *earlier)
-    copies, to_core, table = lax.optimization_barrier((copies, to_core, table))
     from_core = lax.ppermute(to_core, "core", [(0, 1), (1, 0)])
     from_chip = lax.ppermute(
         jnp.concatenate([to_chip, from_core[1:]], axis=0), "zp", [(0, 1), (1, 0)]
     )
-    all_regions = lax.all_to_all(copies, "x", 0, 0, tiled=True)
 
     padded = jnp.pad(table.reshape(GROUP * R * 4, TAPS), ((0, 0), (0, LANES - TAPS)))
     bands = pl.pallas_call(
@@ -298,17 +285,24 @@
         name="bands",
     )(mine_x.astype(jnp.int32).reshape(1), padded)
 
-    scalars = jnp.stack([zh + 1, mine_x]).astype(jnp.int32)
-    waves = pl.pallas_call(
-        chain_kernel,
-        out_shape=jax.ShapeDtypeStruct((GROUP * 4, NX, LANES), jnp.bfloat16),
-        in_specs=[SMEM] + [VMEM] * 5,
-        out_specs=VMEM,
-        scratch_shapes=[pltpu.VMEM((2 * NX, NY), jnp.bfloat16)],
-        compiler_params=PARAMS,
-        cost_estimate=cost(4_000_000_000, 4_000_000),
-        name="chain",
-    )(scalars, *bands, surface, all_regions)
+    entering = lax.dynamic_index_in_dim(surface, mine_x, 0, keepdims=False).reshape(2 * NX, NY)
+    before = ()
+    for block in range(blocks):
+        waves, leaving = pl.pallas_call(
+            chain_kernel,
+            out_shape=(
+                jax.ShapeDtypeStruct((GROUP * 4, NX, LANES), jnp.bfloat16),
+                jax.ShapeDtypeStruct((2 * NX, NY), jnp.bfloat16),
+            ),
+            in_specs=[SMEM] + [VMEM] * (5 + len(before)),
+            out_specs=(VMEM,) * 2,
+            compiler_params=PARAMS,
+            cost_estimate=cost(300_000_000, 4_000_000),
+            name="chain",
+        )((zh == block).astype(jnp.int32).reshape(1), *bands, entering, all_regions, *before)
+        before = (waves,)
+        if block + 1 < blocks:
+            entering = lax.ppermute(leaving, "zh", [(block, block + 1)])
 
     waves, from_chip = lax.optimization_barrier((waves, from_chip))
     waves = lax.all_to_all(waves, ("x",) + QUAD, 0, 0, tiled=True)

time: 77.5 us -> 72.1 us (0.930)
  starting transfers between devices: 27.4 us -> 22.1 us
    ppermute x2, starting transfers between devices: 16.4 us -> 2.38 us  [body(): entering = lax.ppermute(leaving, 'zh', [(block, block + 1)])]
    ppermute x1, starting transfers between devices: 3.56 us -> 10.9 us  [body(): from_core = lax.ppermute(to_core, 'core', [(0, 1), (1, 0)])]
    unnamed x6, local copies, waits for them, and re-layouts: 0.95 us -> 0.01 us
    broadcast_in_dim x0 -> x1, other arithmetic: none -> 0.9 us  [body(): copies = jnp.broadcast_to(local[None], (GROUP, NX, NY))]
    convert_element_type x1 -> x0, other arithmetic: 0.85 us -> none  [body(): regions[0].astype(jnp.bfloat16)]
    pallas_call x2 -> x3, Pallas kernels: 3.25 us -> 2.59 us  [body(): pl.pallas_call(chain_kernel, out_shape=(jax.ShapeDtypeStruct((GROUP * 4,...]
  transfers between devices with their start and end apart: 5 -> 5, of which waited for: 2 -> 1; matrix products, arithmetic and copies ran while one was open for 0% -> 0% of each run, Pallas kernels for 4% -> 5%
where the time goes in v8:
time: 72.1 us; the launch traced here: 71.4 us
  blocking collectives  39.5 us (55%)
  starting transfers between devices  22.1 us (31%)
  Pallas kernels  6.98 us (10%)
  waiting for transfers between devices  0.96 us (1%)
  other arithmetic  0.92 us (1%)
    all_to_all x1, blocking collectives, body(): parts = lax.all_to_all(partial_image, FREQ, 0, 0, tiled=True)  25.4 us
    all_to_all x1, blocking collectives, body(): waves = lax.all_to_all(waves, ('x',) + QUAD, 0, 0, tiled=True)  14.1 us
    ppermute x1, starting transfers between devices, body(): from_core = lax.ppermute(to_core, 'core', [(0, 1), (1, 0)])  10.9 us
    all_to_all x1, starting transfers between devices, body(): all_regions = lax.all_to_all(copies, 'x', 0, 0, tiled=True)  4.84 us
    ppermute x1, starting transfers between devices, body(): lax.ppermute(jnp.concatenate([to_chip, from_core[1:]], axis=0), 'zp', [(0...  4 us
    pallas_call x1, Pallas kernels, body(): pl.pallas_call(lambda *refs: image_kernel(scale, *refs), out_shape=jax.Sh...  2.81 us
    pallas_call x3, Pallas kernels, body(): pl.pallas_call(chain_kernel, out_shape=(jax.ShapeDtypeStruct((GROUP * 4,...  2.59 us
    ppermute x2, starting transfers between devices, body(): entering = lax.ppermute(leaving, 'zh', [(block, block + 1)])  2.38 us
  transfers between devices with their start and end apart: 5, of which 1 were waited for; matrix products, arithmetic and copies ran while one was open for 0% of the time, Pallas kernels for 5%

profile of v8, /device:TPU:1, one launch (start us, length us, event | category | flops | bytes accessed | tf_op | source)
XLA Modules:
  0.0 71.4 jit_solution(9709271504593715019)
XLA Ops:
  0.0 0.0 copy-start
  0.0 0.0 copy-start.1
  0.0 0.9 %convert_bitcast_fusion = bf16[64,256]{1,0:T(8,128)(2,1)S(1)} fusion(s32[1,64,256]{2,1,0:T(8,128)} %param.5), kind=kLoop, calls=%fused_computation.1 | loop fusion | flops 16384 | bytes 98304 | tf_op jit(solution)/shard_map/broadcast_in_dim | solution.py:251
  0.9 0.7 broadcast_in_dim.9
  1.6 4.8 %all-to-all-start = ((bf16[4,64,256]{2,1,0:T(8,128)(2,1)}), bf16[4,64,256]{2,1,0:T(8,128)(2,1)S(1)}, u32[]{:S(2)}, u32[]{:S(2)}) async-start(bf16[4,64,256]{2,1,0:T(8,128)(2,1)} %broadcast_in_dim.9), calls=%async_computation | async-start | bytes 262144 | tf_op jit(solution)/shard_map/all_to_all | solution.py:253
  6.4 0.0 copy-done.1
  6.4 0.3 pack.1
  6.7 0.0 copy-start.2
  6.7 10.9 %collective-permute-start.2 = (bf16[2,4,64,128]{3,2,1,0:T(8,128)(2,1)S(1)}, bf16[2,4,64,128]{3,2,1,0:T(8,128)(2,1)S(1)}, u32[]{:S(2)}, u32[]{:S(2)}) collective-permute-start(bf16[2,4,64,128]{3,2,1,0:T(8,128)(2,1)S(1)} %get-tuple-element.33), channel_id=1, source_target_pairs={{0,1},{1,0},{2,3},{3,2},{4,5},{5,4},{6,7},{7,6},{8,9},{9,8},{10,11... | collective-permute-start | bytes 393224 | tf_op jit(solution)/shard_map/ppermute | solution.py:268
  17.7 0.0 copy-done.2
  17.7 0.5 bands.1
  18.2 0.0 copy-done
  18.3 0.0 all-to-all-done.regions_ref
  18.3 1.9 %chain.3 = (bf16[16,64,128]{2,1,0:T(8,128)(2,1)S(1)}, bf16[128,256]{1,0:T(8,128)(2,1)S(1)}) custom-call(s32[1]{0:T(128)} %bitcast.7.turn_ref, bf16[512,128]{1,0:T(8,128)(2,1)S(1)} %get-tuple-element.22.band_first, bf16[256,512]{1,0:T(8,128)(2,1)S(1)} %get-tuple-element.23.band_even, bf16[256,512]{1,0:T(8,128)(2,1)S(1)} %get-tuple-element.24.band_odd, ...), custom_call_target="tpu_custom_call" | custom-call | flops 300000000 | bytes 4000000 | tf_op jit(solution)/shard_map/chain/pallas_call | solution.py:291
  20.2 1.7 %collective-permute-start = (bf16[128,256]{1,0:T(8,128)(2,1)S(1)}, bf16[128,256]{1,0:T(8,128)(2,1)S(1)}, u32[]{:S(2)}, u32[]{:S(2)}) collective-permute-start(bf16[128,256]{1,0:T(8,128)(2,1)S(1)} %get-tuple-element.26), channel_id=1, source_target_pairs={{0,256},{1,257},{2,258},{3,259},{4,260},{5,261},{6,262},{7,263},{8... | collective-permute-start | bytes 196616 | tf_op jit(solution)/shard_map/ppermute | solution.py:305
  21.9 0.0 collective-permute-done.2.refs_3_
  22.0 4.0 %collective-permute-start.3 = (bf16[2,4,64,128]{3,2,1,0:T(8,128)(2,1)S(1)}, bf16[2,4,64,128]{3,2,1,0:T(8,128)(2,1)S(1)}, u32[]{:S(2)}, u32[]{:S(2)}) collective-permute-start(bf16[2,4,64,128]{3,2,1,0:T(8,128)(2,1)S(1)} %pad_maximum_fusion), channel_id=1, source_target_pairs={{0,2},{2,0},{1,3},{3,1},{4,6},{6,4},{5,7},{7,5},{8,10},{10,8},{9,1... | collective-permute-start | bytes 393224 | tf_op jit(solution)/shard_map/ppermute | solution.py:269
  26.0 0.0 collective-permute-done.entering_ref
  26.0 0.7 collective-permute-start.1
  26.7 0.0 collective-permute-done.1.entering_ref
  26.7 0.7 chain.5
  27.4 0.9 %collective-permute-done.3.refs_4_ = bf16[2,4,64,128]{3,2,1,0:T(8,128)(2,1)S(1)} collective-permute-done((bf16[2,4,64,128]{3,2,1,0:T(8,128)(2,1)S(1)}, bf16[2,4,64,128]{3,2,1,0:T(8,128)(2,1)S(1)}, u32[]{:S(2)}, u32[]{:S(2)}) %collective-permute-start.3) | collective-permute-done | bytes 131104 | tf_op jit(solution)/shard_map/ppermute | solution.py:269
  28.3 14.1 %all_to_all.15.refs_1_ = bf16[16,64,128]{2,1,0:T(8,128)(2,1)S(1)} all-to-all(bf16[16,64,128]{2,1,0:T(8,128)(2,1)S(1)} %get-tuple-element.34), channel_id=1, replica_groups=mesh['zh'=3,'x'=4,'y'=8,'zq'=2,'zp'=2,'core'=2] {'x','zp','core'}, dimensions={0} | all-to-all | bytes 524288 | tf_op jit(solution)/shard_map/all_to_all | solution.py:308
  42.4 2.8 %image.1 = bf16[64,16,128]{2,1,0:T(8,128)(2,1)S(1)} custom-call(s32[1]{0:T(128)} %bitcast.quarter_ref.refs_0_, bf16[16,64,128]{2,1,0:T(8,128)(2,1)S(1)} %all_to_all.15.refs_1_, bf16[4,64,128]{2,1,0:T(8,128)(2,1)S(1)} %get-tuple-element.35.refs_2_, bf16[2,4,64,128]{3,2,1,0:T(8,128)(2,1)S(1)} %collective-permute-done.2.refs_3_, ...), custom_call_target="tpu_custom_call" | custom-call | flops 10000000 | bytes 2000000 | tf_op jit(solution)/shard_map/image/pallas_call | solution.py:311
  45.3 25.4 %all_to_all.16.part_ref = bf16[64,16,128]{2,1,0:T(8,128)(2,1)S(1)} all-to-all(bf16[64,16,128]{2,1,0:T(8,128)(2,1)S(1)} %image.1), channel_id=1, replica_groups=mesh['zh'=3,'x'=4,'y'=8,'zq'=2,'zp'=2,'core'=2] {'y','zq','zp','core'}, dimensions={0} | all-to-all | bytes 524288 | tf_op jit(solution)/shard_map/all_to_all | solution.py:323
  70.6 0.7 %total.1 = f32[1,32,1,256]{3,2,1,0:T(1,128)} custom-call(bf16[64,16,128]{2,1,0:T(8,128)(2,1)S(1)} %all_to_all.16.part_ref), custom_call_target="tpu_custom_call" | custom-call | tf_op jit(solution)/shard_map/total/pallas_call | solution.py:325
  (5 shorter events, 0.1 us)
Async XLA Ops:
  0.0 18.3 %copy-start = (bf16[4,2,64,256]{3,2,1,0:T(8,128)(2,1)S(1)}, bf16[4,2,64,256]{3,2,1,0:T(8,128)(2,1)}, u32[]{:S(2)}) copy-start(bf16[4,2,64,256]{3,2,1,0:T(8,128)(2,1)} %param.4) | copy-start | bytes 786436
  0.0 6.4 %copy-start.1 = (bf16[1,4,2,64,256]{4,3,2,1,0:T(8,128)(2,1)S(1)}, bf16[1,4,2,64,256]{4,3,2,1,0:T(8,128)(2,1)}, u32[]{:S(2)}) copy-start(bf16[1,4,2,64,256]{4,3,2,1,0:T(8,128)(2,1)} %param.7) | copy-start | bytes 786436
  1.6 16.7 %all-to-all-start = ((bf16[4,64,256]{2,1,0:T(8,128)(2,1)}), bf16[4,64,256]{2,1,0:T(8,128)(2,1)S(1)}, u32[]{:S(2)}, u32[]{:S(2)}) async-start(bf16[4,64,256]{2,1,0:T(8,128)(2,1)} %broadcast_in_dim.9), calls=%async_computation | async-start | bytes 262144 | tf_op jit(solution)/shard_map/all_to_all | solution.py:253
  6.7 11.0 %copy-start.2 = (bf16[4,4,2,2,25]{4,3,2,1,0:T(2,128)(2,1)S(1)}, bf16[4,4,2,2,25]{4,3,2,1,0:T(2,128)(2,1)}, u32[]{:S(2)}) copy-start(bf16[4,4,2,2,25]{4,3,2,1,0:T(2,128)(2,1)} %param.6) | copy-start | bytes 9604
  6.7 15.2 %collective-permute-start.2 = (bf16[2,4,64,128]{3,2,1,0:T(8,128)(2,1)S(1)}, bf16[2,4,64,128]{3,2,1,0:T(8,128)(2,1)S(1)}, u32[]{:S(2)}, u32[]{:S(2)}) collective-permute-start(bf16[2,4,64,128]{3,2,1,0:T(8,128)(2,1)S(1)} %get-tuple-element.33), channel_id=1, source_target_pairs={{0,1},{1,0},{2,3},{3,2},{4,5},{5,4},{6,7},{7,6},{8,9},{9,8},{10,11... | collective-permute-start | bytes 393224 | tf_op jit(solution)/shard_map/ppermute | solution.py:268
  20.2 5.8 %collective-permute-start = (bf16[128,256]{1,0:T(8,128)(2,1)S(1)}, bf16[128,256]{1,0:T(8,128)(2,1)S(1)}, u32[]{:S(2)}, u32[]{:S(2)}) collective-permute-start(bf16[128,256]{1,0:T(8,128)(2,1)S(1)} %get-tuple-element.26), channel_id=1, source_target_pairs={{0,256},{1,257},{2,258},{3,259},{4,260},{5,261},{6,262},{7,263},{8... | collective-permute-start | bytes 196616 | tf_op jit(solution)/shard_map/ppermute | solution.py:305
  22.0 6.4 %collective-permute-start.3 = (bf16[2,4,64,128]{3,2,1,0:T(8,128)(2,1)S(1)}, bf16[2,4,64,128]{3,2,1,0:T(8,128)(2,1)S(1)}, u32[]{:S(2)}, u32[]{:S(2)}) collective-permute-start(bf16[2,4,64,128]{3,2,1,0:T(8,128)(2,1)S(1)} %pad_maximum_fusion), channel_id=1, source_target_pairs={{0,2},{2,0},{1,3},{3,1},{4,6},{6,4},{5,7},{7,5},{8,10},{10,8},{9,1... | collective-permute-start | bytes 393224 | tf_op jit(solution)/shard_map/ppermute | solution.py:269
  26.0 0.7 collective-permute-start.1

commit v9 on v8

--- a/solution.py
+++ b/solution.py
@@ -20,10 +20,10 @@
 MID = TAPS // 2
 GROUP = 4
 
-AXES = ("zh", "x", "y", "zq", "zp", "core")
+AXES = ("zh", "x", "yq", "yp", "zl", "core")
 DEPTH = ("zh", "x")
-FREQ = ("y", "zq", "zp", "core")
-QUAD = ("zp", "core")
+FREQ = ("yq", "yp", "zl", "core")
+QUAD = ("yp", "core")
 
 
 def onehot(shape, fit, value=1.0):
@@ -218,14 +218,16 @@
 
 
 def sum_kernel(part_ref, out_ref):
-    groups = part_ref.shape[0] // 4
+    many, line = part_ref.shape[0], 8
     left = lax.broadcasted_iota(jnp.int32, (REACH, LANES), 1) < QUARTER
     for half in range(2):
         totals = []
         for q in (2 * half, 2 * half + 1):
-            total = part_ref[q].astype(jnp.float32)
-            for i in range(1, groups):
-                total = total + part_ref[4 * i + q].astype(jnp.float32)
+            pair, core = divmod(q, 2)
+            total = jnp.zeros((REACH, LANES), jnp.float32)
+            for start in range(pair * line, many, 2 * line):
+                for i in range(start + core, start + line, 2):
+                    total = total + part_ref[i].astype(jnp.float32)
             totals.append(total)
         a, b = totals
         cols = slice(half * LANES, (half + 1) * LANES)
@@ -251,7 +253,7 @@
     copies = jnp.broadcast_to(local[None], (GROUP, NX, NY))
     copies, local_source, table = lax.optimization_barrier((copies, source[0], table))
     all_regions = lax.all_to_all(copies, "x", 0, 0, tiled=True)
-    quarter = (lax.axis_index("zp") * 2 + core).astype(jnp.int32).reshape(1)
+    quarter = (lax.axis_index("yp") * 2 + core).astype(jnp.int32).reshape(1)
     four = jax.ShapeDtypeStruct((GROUP, NX, LANES), jnp.bfloat16)
     pair = jax.ShapeDtypeStruct((2, GROUP, NX, LANES), jnp.bfloat16)
     one = jax.ShapeDtypeStruct((1, GROUP, NX, LANES), jnp.bfloat16)
@@ -267,7 +269,7 @@
     )(quarter, local_source)
     from_core = lax.ppermute(to_core, "core", [(0, 1), (1, 0)])
     from_chip = lax.ppermute(
-        jnp.concatenate([to_chip, from_core[1:]], axis=0), "zp", [(0, 1), (1, 0)]
+        jnp.concatenate([to_chip, from_core[1:]], axis=0), "yp", [(0, 1), (1, 0)]
     )
 
     padded = jnp.pad(table.reshape(GROUP * R * 4, TAPS), ((0, 0), (0, LANES - TAPS)))
@@ -333,7 +335,7 @@
 
 
 def solution(mesh):
-    wide = Mesh(np.asarray(mesh.devices).reshape(3, 4, 8, 2, 2, 2), AXES)
+    wide = Mesh(np.asarray(mesh.devices).reshape(3, 4, 4, 2, 4, 2), AXES)
     in_specs = (
         P(FREQ, None, None, None),
         P(DEPTH, None, None),

time: 72.1 us -> 72.1 us (level)
  starting transfers between devices: 22.1 us -> 21.3 us
  blocking collectives: 39.5 us -> 40.3 us
    all_to_all x1, blocking collectives: 25.4 us -> 26.3 us  [body(): parts = lax.all_to_all(partial_image, FREQ, 0, 0, tiled=True)]
    ppermute x1, starting transfers between devices: 4 us -> 3.2 us  [body(): lax.ppermute(jnp.concatenate([to_chip, from_core[1:]], axis=0), 'yp', [(0...]
where the time goes in v9:
time: 72.1 us; the launch traced here: 71.5 us
  blocking collectives  40.3 us (56%)
  starting transfers between devices  21.3 us (30%)
  Pallas kernels  6.98 us (10%)
  waiting for transfers between devices  1.11 us (2%)
  other arithmetic  0.92 us (1%)
    all_to_all x1, blocking collectives, body(): parts = lax.all_to_all(partial_image, FREQ, 0, 0, tiled=True)  26.3 us
    all_to_all x1, blocking collectives, body(): waves = lax.all_to_all(waves, ('x',) + QUAD, 0, 0, tiled=True)  14 us
    ppermute x1, starting transfers between devices, body(): from_core = lax.ppermute(to_core, 'core', [(0, 1), (1, 0)])  10.9 us
    all_to_all x1, starting transfers between devices, body(): all_regions = lax.all_to_all(copies, 'x', 0, 0, tiled=True)  4.84 us
    ppermute x1, starting transfers between devices, body(): lax.ppermute(jnp.concatenate([to_chip, from_core[1:]], axis=0), 'yp', [(0...  3.2 us
    pallas_call x1, Pallas kernels, body(): pl.pallas_call(lambda *refs: image_kernel(scale, *refs), out_shape=jax.Sh...  2.81 us
    pallas_call x3, Pallas kernels, body(): pl.pallas_call(chain_kernel, out_shape=(jax.ShapeDtypeStruct((GROUP * 4,...  2.59 us
    ppermute x2, starting transfers between devices, body(): entering = lax.ppermute(leaving, 'zh', [(block, block + 1)])  2.38 us
  transfers between devices with their start and end apart: 5, of which 1 were waited for; matrix products, arithmetic and copies ran while one was open for 0% of the time, Pallas kernels for 5%

profile of v9, /device:TPU:1, one launch (start us, length us, event | category | flops | bytes accessed | tf_op | source)
XLA Modules:
  0.0 71.5 jit_solution(7406076404403878700)
XLA Ops:
  0.0 0.0 copy-start
  0.0 0.0 copy-start.1
  0.0 0.9 %convert_bitcast_fusion = bf16[64,256]{1,0:T(8,128)(2,1)S(1)} fusion(s32[1,64,256]{2,1,0:T(8,128)} %param.5), kind=kLoop, calls=%fused_computation.1 | loop fusion | flops 16384 | bytes 98304 | tf_op jit(solution)/shard_map/broadcast_in_dim | solution.py:253
  0.9 0.7 broadcast_in_dim.9
  1.6 4.8 %all-to-all-start = ((bf16[4,64,256]{2,1,0:T(8,128)(2,1)}), bf16[4,64,256]{2,1,0:T(8,128)(2,1)S(1)}, u32[]{:S(2)}, u32[]{:S(2)}) async-start(bf16[4,64,256]{2,1,0:T(8,128)(2,1)} %broadcast_in_dim.9), calls=%async_computation | async-start | bytes 262144 | tf_op jit(solution)/shard_map/all_to_all | solution.py:255
  6.4 0.0 copy-done.1
  6.4 0.3 pack.1
  6.7 0.0 copy-start.2
  6.7 10.9 %collective-permute-start.2 = (bf16[2,4,64,128]{3,2,1,0:T(8,128)(2,1)S(1)}, bf16[2,4,64,128]{3,2,1,0:T(8,128)(2,1)S(1)}, u32[]{:S(2)}, u32[]{:S(2)}) collective-permute-start(bf16[2,4,64,128]{3,2,1,0:T(8,128)(2,1)S(1)} %get-tuple-element.33), channel_id=1, source_target_pairs={{0,1},{1,0},{2,3},{3,2},{4,5},{5,4},{6,7},{7,6},{8,9},{9,8},{10,11... | collective-permute-start | bytes 393224 | tf_op jit(solution)/shard_map/ppermute | solution.py:270
  17.7 0.0 copy-done.2
  17.7 0.5 bands.1
  18.2 0.0 copy-done
  18.3 0.0 all-to-all-done.regions_ref
  18.3 1.9 %chain.3 = (bf16[16,64,128]{2,1,0:T(8,128)(2,1)S(1)}, bf16[128,256]{1,0:T(8,128)(2,1)S(1)}) custom-call(s32[1]{0:T(128)} %bitcast.7.turn_ref, bf16[512,128]{1,0:T(8,128)(2,1)S(1)} %get-tuple-element.22.band_first, bf16[256,512]{1,0:T(8,128)(2,1)S(1)} %get-tuple-element.23.band_even, bf16[256,512]{1,0:T(8,128)(2,1)S(1)} %get-tuple-element.24.band_odd, ...), custom_call_target="tpu_custom_call" | custom-call | flops 300000000 | bytes 4000000 | tf_op jit(solution)/shard_map/chain/pallas_call | solution.py:293
  20.2 1.7 %collective-permute-start = (bf16[128,256]{1,0:T(8,128)(2,1)S(1)}, bf16[128,256]{1,0:T(8,128)(2,1)S(1)}, u32[]{:S(2)}, u32[]{:S(2)}) collective-permute-start(bf16[128,256]{1,0:T(8,128)(2,1)S(1)} %get-tuple-element.26), channel_id=1, source_target_pairs={{0,256},{1,257},{2,258},{3,259},{4,260},{5,261},{6,262},{7,263},{8... | collective-permute-start | bytes 196616 | tf_op jit(solution)/shard_map/ppermute | solution.py:307
  21.9 0.0 collective-permute-done.2.refs_3_
  22.0 3.2 %collective-permute-start.3 = (bf16[2,4,64,128]{3,2,1,0:T(8,128)(2,1)S(1)}, bf16[2,4,64,128]{3,2,1,0:T(8,128)(2,1)S(1)}, u32[]{:S(2)}, u32[]{:S(2)}) collective-permute-start(bf16[2,4,64,128]{3,2,1,0:T(8,128)(2,1)S(1)} %pad_maximum_fusion), channel_id=1, source_target_pairs={{0,8},{8,0},{1,9},{9,1},{2,10},{10,2},{3,11},{11,3},{4,12},{12,4},... | collective-permute-start | bytes 393224 | tf_op jit(solution)/shard_map/ppermute | solution.py:271
  25.2 0.0 collective-permute-done.entering_ref
  25.2 0.7 collective-permute-start.1
  25.9 0.0 collective-permute-done.1.entering_ref
  25.9 0.7 chain.5
  26.6 1.1 %collective-permute-done.3.refs_4_ = bf16[2,4,64,128]{3,2,1,0:T(8,128)(2,1)S(1)} collective-permute-done((bf16[2,4,64,128]{3,2,1,0:T(8,128)(2,1)S(1)}, bf16[2,4,64,128]{3,2,1,0:T(8,128)(2,1)S(1)}, u32[]{:S(2)}, u32[]{:S(2)}) %collective-permute-start.3) | collective-permute-done | bytes 131104 | tf_op jit(solution)/shard_map/ppermute | solution.py:271
  27.7 14.0 %all_to_all.15.refs_1_ = bf16[16,64,128]{2,1,0:T(8,128)(2,1)S(1)} all-to-all(bf16[16,64,128]{2,1,0:T(8,128)(2,1)S(1)} %get-tuple-element.34), channel_id=1, replica_groups=mesh['zh'=3,'x'=4,'yq'=4,'yp'=2,'zl'=4,'core'=2] {'x','yp','core'}, dimensions={0} | all-to-all | bytes 524288 | tf_op jit(solution)/shard_map/all_to_all | solution.py:310
  41.6 2.8 %image.1 = bf16[64,16,128]{2,1,0:T(8,128)(2,1)S(1)} custom-call(s32[1]{0:T(128)} %bitcast.quarter_ref.refs_0_, bf16[16,64,128]{2,1,0:T(8,128)(2,1)S(1)} %all_to_all.15.refs_1_, bf16[4,64,128]{2,1,0:T(8,128)(2,1)S(1)} %get-tuple-element.35.refs_2_, bf16[2,4,64,128]{3,2,1,0:T(8,128)(2,1)S(1)} %collective-permute-done.2.refs_3_, ...), custom_call_target="tpu_custom_call" | custom-call | flops 10000000 | bytes 2000000 | tf_op jit(solution)/shard_map/image/pallas_call | solution.py:313
  44.5 26.3 %all_to_all.16.part_ref = bf16[64,16,128]{2,1,0:T(8,128)(2,1)S(1)} all-to-all(bf16[64,16,128]{2,1,0:T(8,128)(2,1)S(1)} %image.1), channel_id=1, replica_groups=mesh['zh'=3,'x'=4,'yq'=4,'yp'=2,'zl'=4,'core'=2] {'yq','yp','zl','core'}, dimensions={0} | all-to-all | bytes 524288 | tf_op jit(solution)/shard_map/all_to_all | solution.py:325
  70.8 0.7 %total.1 = f32[1,32,1,256]{3,2,1,0:T(1,128)} custom-call(bf16[64,16,128]{2,1,0:T(8,128)(2,1)S(1)} %all_to_all.16.part_ref), custom_call_target="tpu_custom_call" | custom-call | tf_op jit(solution)/shard_map/total/pallas_call | solution.py:327
  (5 shorter events, 0.1 us)
Async XLA Ops:
  0.0 18.3 %copy-start = (bf16[4,2,64,256]{3,2,1,0:T(8,128)(2,1)S(1)}, bf16[4,2,64,256]{3,2,1,0:T(8,128)(2,1)}, u32[]{:S(2)}) copy-start(bf16[4,2,64,256]{3,2,1,0:T(8,128)(2,1)} %param.4) | copy-start | bytes 786436
  0.0 6.4 %copy-start.1 = (bf16[1,4,2,64,256]{4,3,2,1,0:T(8,128)(2,1)S(1)}, bf16[1,4,2,64,256]{4,3,2,1,0:T(8,128)(2,1)}, u32[]{:S(2)}) copy-start(bf16[1,4,2,64,256]{4,3,2,1,0:T(8,128)(2,1)} %param.7) | copy-start | bytes 786436
  1.6 16.7 %all-to-all-start = ((bf16[4,64,256]{2,1,0:T(8,128)(2,1)}), bf16[4,64,256]{2,1,0:T(8,128)(2,1)S(1)}, u32[]{:S(2)}, u32[]{:S(2)}) async-start(bf16[4,64,256]{2,1,0:T(8,128)(2,1)} %broadcast_in_dim.9), calls=%async_computation | async-start | bytes 262144 | tf_op jit(solution)/shard_map/all_to_all | solution.py:255
  6.7 11.0 %copy-start.2 = (bf16[4,4,2,2,25]{4,3,2,1,0:T(2,128)(2,1)S(1)}, bf16[4,4,2,2,25]{4,3,2,1,0:T(2,128)(2,1)}, u32[]{:S(2)}) copy-start(bf16[4,4,2,2,25]{4,3,2,1,0:T(2,128)(2,1)} %param.6) | copy-start | bytes 9604
  6.7 15.2 %collective-permute-start.2 = (bf16[2,4,64,128]{3,2,1,0:T(8,128)(2,1)S(1)}, bf16[2,4,64,128]{3,2,1,0:T(8,128)(2,1)S(1)}, u32[]{:S(2)}, u32[]{:S(2)}) collective-permute-start(bf16[2,4,64,128]{3,2,1,0:T(8,128)(2,1)S(1)} %get-tuple-element.33), channel_id=1, source_target_pairs={{0,1},{1,0},{2,3},{3,2},{4,5},{5,4},{6,7},{7,6},{8,9},{9,8},{10,11... | collective-permute-start | bytes 393224 | tf_op jit(solution)/shard_map/ppermute | solution.py:270
  20.2 5.0 %collective-permute-start = (bf16[128,256]{1,0:T(8,128)(2,1)S(1)}, bf16[128,256]{1,0:T(8,128)(2,1)S(1)}, u32[]{:S(2)}, u32[]{:S(2)}) collective-permute-start(bf16[128,256]{1,0:T(8,128)(2,1)S(1)} %get-tuple-element.26), channel_id=1, source_target_pairs={{0,256},{1,257},{2,258},{3,259},{4,260},{5,261},{6,262},{7,263},{8... | collective-permute-start | bytes 196616 | tf_op jit(solution)/shard_map/ppermute | solution.py:307
  22.0 5.7 %collective-permute-start.3 = (bf16[2,4,64,128]{3,2,1,0:T(8,128)(2,1)S(1)}, bf16[2,4,64,128]{3,2,1,0:T(8,128)(2,1)S(1)}, u32[]{:S(2)}, u32[]{:S(2)}) collective-permute-start(bf16[2,4,64,128]{3,2,1,0:T(8,128)(2,1)S(1)} %pad_maximum_fusion), channel_id=1, source_target_pairs={{0,8},{8,0},{1,9},{9,1},{2,10},{10,2},{3,11},{11,3},{4,12},{12,4},... | collective-permute-start | bytes 393224 | tf_op jit(solution)/shard_map/ppermute | solution.py:271
  25.2 0.7 collective-permute-start.1

commit v10 on v9

--- a/solution.py
+++ b/solution.py
@@ -1,3 +1,4 @@
+import functools
 import math
 
 import jax
@@ -93,17 +94,19 @@
     return out
 
 
-def chain_kernel(turn_ref, band_first, band_even, band_odd, entering_ref, regions_ref, *refs):
-    out_ref, state = refs[-2:]
+def chain_kernel(first, turn_ref, index_ref, band_first, band_even, band_odd, entering_ref, *refs):
+    columns, (out_ref, state, regions_ref) = refs[:GROUP], refs[-3:]
     active = turn_ref[0] == 1
 
     @pl.when(active)
     def _():
+        for k in range(GROUP):
+            regions_ref[index_ref[0] ^ k] = columns[k][...]
         run_steps(band_first, band_even, band_odd, entering_ref, regions_ref, out_ref, state)
 
     @pl.when(jnp.logical_not(active))
     def _():
-        out_ref[...] = refs[0][...] if len(refs) == 3 else jnp.zeros_like(out_ref)
+        out_ref[...] = jnp.zeros_like(out_ref) if first else refs[GROUP][...]
         state[...] = jnp.zeros_like(state)
 
 
@@ -214,7 +217,7 @@
         out_ref[x] = jnp.where(left, total[:REACH], total[REACH:]).astype(jnp.bfloat16)
         return carry
 
-    lax.fori_loop(0, NX, fold, 0, unroll=8)
+    lax.fori_loop(0, NX, fold, 0, unroll=32)
 
 
 def sum_kernel(part_ref, out_ref):
@@ -250,9 +253,10 @@
     core = lax.axis_index("core")
     blocks = lax.axis_size("zh")
     local = regions[0].astype(jnp.bfloat16)
-    copies = jnp.broadcast_to(local[None], (GROUP, NX, NY))
-    copies, local_source, table = lax.optimization_barrier((copies, source[0], table))
-    all_regions = lax.all_to_all(copies, "x", 0, 0, tiled=True)
+    local, local_source, table = lax.optimization_barrier((local, source[0], table))
+    columns = [local] + [
+        lax.ppermute(local, "x", [(i, i ^ k) for i in range(GROUP)]) for k in range(1, GROUP)
+    ]
     quarter = (lax.axis_index("yp") * 2 + core).astype(jnp.int32).reshape(1)
     four = jax.ShapeDtypeStruct((GROUP, NX, LANES), jnp.bfloat16)
     pair = jax.ShapeDtypeStruct((2, GROUP, NX, LANES), jnp.bfloat16)
@@ -290,21 +294,23 @@
     entering = lax.dynamic_index_in_dim(surface, mine_x, 0, keepdims=False).reshape(2 * NX, NY)
     before = ()
     for block in range(blocks):
-        waves, leaving = pl.pallas_call(
-            chain_kernel,
-            out_shape=(
-                jax.ShapeDtypeStruct((GROUP * 4, NX, LANES), jnp.bfloat16),
-                jax.ShapeDtypeStruct((2 * NX, NY), jnp.bfloat16),
-            ),
-            in_specs=[SMEM] + [VMEM] * (5 + len(before)),
-            out_specs=(VMEM,) * 2,
+        wave_shape = jax.ShapeDtypeStruct((GROUP * 4, NX, LANES), jnp.bfloat16)
+        state_shape = (2 * NX, NY)
+        last = block + 1 == blocks
+        waves, *leaving = pl.pallas_call(
+            functools.partial(chain_kernel, block == 0),
+            out_shape=(wave_shape,) + (() if last else (jax.ShapeDtypeStruct(state_shape, jnp.bfloat16),)),
+            in_specs=[SMEM] * 2 + [VMEM] * (4 + GROUP + len(before)),
+            out_specs=(VMEM,) * (1 if last else 2),
+            scratch_shapes=([pltpu.VMEM(state_shape, jnp.bfloat16)] if last else [])
+            + [pltpu.VMEM((GROUP, NX, NY), jnp.bfloat16)],
             compiler_params=PARAMS,
-            cost_estimate=cost(300_000_000, 4_000_000),
+            cost_estimate=cost(100_000_000, 4_000_000),
             name="chain",
-        )((zh == block).astype(jnp.int32).reshape(1), *bands, entering, all_regions, *before)
+        )((zh == block).astype(jnp.int32).reshape(1), mine_x.astype(jnp.int32).reshape(1), *bands, entering, *columns, *before)
         before = (waves,)
-        if block + 1 < blocks:
-            entering = lax.ppermute(leaving, "zh", [(block, block + 1)])
+        if not last:
+            entering = lax.ppermute(leaving[0], "zh", [(block, block + 1)])
 
     waves, from_chip = lax.optimization_barrier((waves, from_chip))
     waves = lax.all_to_all(waves, ("x",) + QUAD, 0, 0, tiled=True)

time: 72.1 us -> 78.8 us (1.093)
  starting transfers between devices: 21.3 us -> 28.1 us
  Pallas kernels: 6.98 us -> 5.95 us
  local copies, waits for them, and re-layouts: 0.7 us -> 1.66 us
    ppermute x2 -> x5, starting transfers between devices: 2.38 us -> 12.4 us  [the longest x3 9.58 us: body(): lax.ppermute(local, 'x', [(i, i ^ k) for i in range(GROUP)])]
    all_to_all x1 -> x0, starting transfers between devices: 4.84 us -> none  [body(): all_regions = lax.all_to_all(copies, 'x', 0, 0, tiled=True)]
    unnamed x6, local copies, waits for them, and re-layouts: 0.01 us -> 1.63 us
    ppermute x1, starting transfers between devices: 10.9 us -> 12.4 us  [body(): from_core = lax.ppermute(to_core, 'core', [(0, 1), (1, 0)])]
    broadcast_in_dim x1 -> x0, other arithmetic: 0.9 us -> none  [body(): copies = jnp.broadcast_to(local[None], (GROUP, NX, NY))]
    convert_element_type x0 -> x1, other arithmetic: none -> 0.89 us  [body(): local = regions[0].astype(jnp.bfloat16)]
    all_to_all x1, blocking collectives: 14 us -> 13.1 us  [body(): waves = lax.all_to_all(waves, ('x',) + QUAD, 0, 0, tiled=True)]
  transfers between devices with their start and end apart: 5 -> 7, of which waited for: 1 -> 1; matrix products, arithmetic and copies ran while one was open for 0% -> 0% of each run, Pallas kernels for 5% -> 3%
where the time goes in v10:
time: 78.8 us; the launch traced here: 78.4 us
  blocking collectives  39.9 us (51%)
  starting transfers between devices  28.1 us (36%)
  Pallas kernels  5.95 us (8%)
  waiting for transfers between devices  1.73 us (2%)
  local copies, waits for them, and re-layouts  1.66 us (2%)
  other arithmetic  0.9 us (1%)
    all_to_all x1, blocking collectives, body(): parts = lax.all_to_all(partial_image, FREQ, 0, 0, tiled=True)  26.8 us
    all_to_all x1, blocking collectives, body(): waves = lax.all_to_all(waves, ('x',) + QUAD, 0, 0, tiled=True)  13.1 us
    ppermute x1, starting transfers between devices, body(): from_core = lax.ppermute(to_core, 'core', [(0, 1), (1, 0)])  12.4 us
    ppermute x3, starting transfers between devices, body(): lax.ppermute(local, 'x', [(i, i ^ k) for i in range(GROUP)])  9.58 us
    ppermute x1, starting transfers between devices, body(): lax.ppermute(jnp.concatenate([to_chip, from_core[1:]], axis=0), 'yp', [(0...  3.2 us
    ppermute x2, starting transfers between devices, body(): entering = lax.ppermute(leaving[0], 'zh', [(block, block + 1)])  2.85 us
    pallas_call x1, Pallas kernels, body(): pl.pallas_call(lambda *refs: image_kernel(scale, *refs), out_shape=jax.Sh...  2.39 us
    pallas_call x3, Pallas kernels, body(): pl.pallas_call(functools.partial(chain_kernel, block == 0), out_shape=(wa...  1.99 us
  transfers between devices with their start and end apart: 7, of which 1 were waited for; matrix products, arithmetic and copies ran while one was open for 0% of the time, Pallas kernels for 3%

profile of v10, /device:TPU:1, one launch (start us, length us, event | category | flops | bytes accessed | tf_op | source)
XLA Modules:
  0.0 78.4 jit_solution(16258582646630632916)
XLA Ops:
  0.0 0.0 copy-start
  0.0 0.9 %convert_bitcast_fusion.refs_0_ = bf16[64,256]{1,0:T(8,128)(2,1)S(1)} fusion(s32[1,64,256]{2,1,0:T(8,128)} %param.5), kind=kLoop, calls=%fused_computation.1 | loop fusion | flops 16384 | bytes 98304 | tf_op jit(solution)/shard_map/convert_element_type | solution.py:255
  0.9 0.0 copy-start.1
  0.9 0.9 %copy-done.1 = bf16[1,4,2,64,256]{4,3,2,1,0:T(8,128)(2,1)S(1)} copy-done((bf16[1,4,2,64,256]{4,3,2,1,0:T(8,128)(2,1)S(1)}, bf16[1,4,2,64,256]{4,3,2,1,0:T(8,128)(2,1)}, u32[]{:S(2)}) %copy-start.1) | copy-done | bytes 262168
  1.8 0.3 pack.1
  2.2 12.4 %collective-permute-start.5 = (bf16[2,4,64,128]{3,2,1,0:T(8,128)(2,1)S(1)}, bf16[2,4,64,128]{3,2,1,0:T(8,128)(2,1)S(1)}, u32[]{:S(2)}, u32[]{:S(2)}) collective-permute-start(bf16[2,4,64,128]{3,2,1,0:T(8,128)(2,1)S(1)} %get-tuple-element.31), channel_id=1, source_target_pairs={{0,1},{1,0},{2,3},{3,2},{4,5},{5,4},{6,7},{7,6},{8,9},{9,8},{10,11... | collective-permute-start | bytes 393224 | tf_op jit(solution)/shard_map/ppermute | solution.py:274
  14.6 1.9 %collective-permute-start = (bf16[64,256]{1,0:T(8,128)(2,1)S(1)}, bf16[64,256]{1,0:T(8,128)(2,1)S(1)}, u32[]{:S(2)}, u32[]{:S(2)}) collective-permute-start(bf16[64,256]{1,0:T(8,128)(2,1)S(1)} %convert_bitcast_fusion.refs_0_), channel_id=1, source_target_pairs={{0,64},{64,0},{128,192},{192,128},{1,65},{65,1},{129,193},{193,129... | collective-permute-start | bytes 98312 | tf_op jit(solution)/shard_map/ppermute | solution.py:258
  16.5 1.9 %collective-permute-start.1 = (bf16[64,256]{1,0:T(8,128)(2,1)S(1)}, bf16[64,256]{1,0:T(8,128)(2,1)S(1)}, u32[]{:S(2)}, u32[]{:S(2)}) collective-permute-start(bf16[64,256]{1,0:T(8,128)(2,1)S(1)} %convert_bitcast_fusion.refs_0_), channel_id=1, source_target_pairs={{0,128},{64,192},{128,0},{192,64},{1,129},{65,193},{129,1},{193,65... | collective-permute-start | bytes 98312 | tf_op jit(solution)/shard_map/ppermute | solution.py:258
  18.4 5.7 %collective-permute-start.2 = (bf16[64,256]{1,0:T(8,128)(2,1)S(1)}, bf16[64,256]{1,0:T(8,128)(2,1)S(1)}, u32[]{:S(2)}, u32[]{:S(2)}) collective-permute-start(bf16[64,256]{1,0:T(8,128)(2,1)S(1)} %convert_bitcast_fusion.refs_0_), channel_id=1, source_target_pairs={{0,192},{64,128},{128,64},{192,0},{1,193},{65,129},{129,65},{193,1... | collective-permute-start | bytes 98312 | tf_op jit(solution)/shard_map/ppermute | solution.py:258
  24.2 0.0 copy-done
  24.2 0.0 copy-start.2
  24.3 0.7 copy-done.2
  24.9 0.5 bands.1
  25.5 0.0 collective-permute-done.refs_1_
  25.5 0.0 collective-permute-done.1.refs_2_
  25.5 0.0 collective-permute-done.2.refs_3_
  25.5 1.9 %chain.3 = (bf16[16,64,128]{2,1,0:T(8,128)(2,1)S(1)}, bf16[128,256]{1,0:T(8,128)(2,1)S(1)}) custom-call(s32[1]{0:T(128)} %bitcast.7.turn_ref, s32[1]{0:T(128)} %bitcast.2.index_ref, bf16[512,128]{1,0:T(8,128)(2,1)S(1)} %get-tuple-element.21.band_first, bf16[256,512]{1,0:T(8,128)(2,1)S(1)} %get-tuple-element.22.band_even, ...), custom_call_target="tpu_custom_call" | custom-call | flops 100000000 | bytes 4000000 | tf_op jit(solution)/shard_map/chain/pallas_call | solution.py:300
  27.4 2.2 %collective-permute-start.3 = (bf16[128,256]{1,0:T(8,128)(2,1)S(1)}, bf16[128,256]{1,0:T(8,128)(2,1)S(1)}, u32[]{:S(2)}, u32[]{:S(2)}) collective-permute-start(bf16[128,256]{1,0:T(8,128)(2,1)S(1)} %get-tuple-element.25), channel_id=1, source_target_pairs={{0,256},{1,257},{2,258},{3,259},{4,260},{5,261},{6,262},{7,263},{8... | collective-permute-start | bytes 196616 | tf_op jit(solution)/shard_map/ppermute | solution.py:313
  29.6 0.0 collective-permute-done.5.refs_3_
  29.7 3.2 %collective-permute-start.6 = (bf16[2,4,64,128]{3,2,1,0:T(8,128)(2,1)S(1)}, bf16[2,4,64,128]{3,2,1,0:T(8,128)(2,1)S(1)}, u32[]{:S(2)}, u32[]{:S(2)}) collective-permute-start(bf16[2,4,64,128]{3,2,1,0:T(8,128)(2,1)S(1)} %pad_maximum_fusion), channel_id=1, source_target_pairs={{0,8},{8,0},{1,9},{9,1},{2,10},{10,2},{3,11},{11,3},{4,12},{12,4},... | collective-permute-start | bytes 393224 | tf_op jit(solution)/shard_map/ppermute | solution.py:275
  32.9 0.0 collective-permute-done.3.entering_ref
  32.9 0.7 collective-permute-start.4
  33.6 0.0 collective-permute-done.4.entering_ref
  33.7 1.7 %collective-permute-done.6.refs_4_ = bf16[2,4,64,128]{3,2,1,0:T(8,128)(2,1)S(1)} collective-permute-done((bf16[2,4,64,128]{3,2,1,0:T(8,128)(2,1)S(1)}, bf16[2,4,64,128]{3,2,1,0:T(8,128)(2,1)S(1)}, u32[]{:S(2)}, u32[]{:S(2)}) %collective-permute-start.6) | collective-permute-done | bytes 131104 | tf_op jit(solution)/shard_map/ppermute | solution.py:275
  35.4 13.1 %all_to_all.10.refs_1_ = bf16[16,64,128]{2,1,0:T(8,128)(2,1)S(1)} all-to-all(bf16[16,64,128]{2,1,0:T(8,128)(2,1)S(1)} %chain.5), channel_id=1, replica_groups=mesh['zh'=3,'x'=4,'yq'=4,'yp'=2,'zl'=4,'core'=2] {'x','yp','core'}, dimensions={0} | all-to-all | bytes 524288 | tf_op jit(solution)/shard_map/all_to_all | solution.py:316
  48.5 2.4 %image.1 = bf16[64,16,128]{2,1,0:T(8,128)(2,1)S(1)} custom-call(s32[1]{0:T(128)} %bitcast.quarter_ref.refs_0_, bf16[16,64,128]{2,1,0:T(8,128)(2,1)S(1)} %all_to_all.10.refs_1_, bf16[4,64,128]{2,1,0:T(8,128)(2,1)S(1)} %get-tuple-element.33.refs_2_, bf16[2,4,64,128]{3,2,1,0:T(8,128)(2,1)S(1)} %collective-permute-done.5.refs_3_, ...), custom_call_target="tpu_custom_call" | custom-call | flops 10000000 | bytes 2000000 | tf_op jit(solution)/shard_map/image/pallas_call | solution.py:319
  50.9 26.8 %all_to_all.11.part_ref = bf16[64,16,128]{2,1,0:T(8,128)(2,1)S(1)} all-to-all(bf16[64,16,128]{2,1,0:T(8,128)(2,1)S(1)} %image.1), channel_id=1, replica_groups=mesh['zh'=3,'x'=4,'yq'=4,'yp'=2,'zl'=4,'core'=2] {'yq','yp','zl','core'}, dimensions={0} | all-to-all | bytes 524288 | tf_op jit(solution)/shard_map/all_to_all | solution.py:331
  77.7 0.7 total.1
  (6 shorter events, 0.1 us)
Async XLA Ops:
  0.0 24.2 %copy-start = (bf16[4,2,64,256]{3,2,1,0:T(8,128)(2,1)S(1)}, bf16[4,2,64,256]{3,2,1,0:T(8,128)(2,1)}, u32[]{:S(2)}) copy-start(bf16[4,2,64,256]{3,2,1,0:T(8,128)(2,1)} %param.4) | copy-start | bytes 786436
  0.9 0.9 %copy-start.1 = (bf16[1,4,2,64,256]{4,3,2,1,0:T(8,128)(2,1)S(1)}, bf16[1,4,2,64,256]{4,3,2,1,0:T(8,128)(2,1)}, u32[]{:S(2)}) copy-start(bf16[1,4,2,64,256]{4,3,2,1,0:T(8,128)(2,1)} %param.7) | copy-start | bytes 786436
  2.2 27.5 %collective-permute-start.5 = (bf16[2,4,64,128]{3,2,1,0:T(8,128)(2,1)S(1)}, bf16[2,4,64,128]{3,2,1,0:T(8,128)(2,1)S(1)}, u32[]{:S(2)}, u32[]{:S(2)}) collective-permute-start(bf16[2,4,64,128]{3,2,1,0:T(8,128)(2,1)S(1)} %get-tuple-element.31), channel_id=1, source_target_pairs={{0,1},{1,0},{2,3},{3,2},{4,5},{5,4},{6,7},{7,6},{8,9},{9,8},{10,11... | collective-permute-start | bytes 393224 | tf_op jit(solution)/shard_map/ppermute | solution.py:274
  14.6 10.9 %collective-permute-start = (bf16[64,256]{1,0:T(8,128)(2,1)S(1)}, bf16[64,256]{1,0:T(8,128)(2,1)S(1)}, u32[]{:S(2)}, u32[]{:S(2)}) collective-permute-start(bf16[64,256]{1,0:T(8,128)(2,1)S(1)} %convert_bitcast_fusion.refs_0_), channel_id=1, source_target_pairs={{0,64},{64,0},{128,192},{192,128},{1,65},{65,1},{129,193},{193,129... | collective-permute-start | bytes 98312 | tf_op jit(solution)/shard_map/ppermute | solution.py:258
  16.5 9.0 %collective-permute-start.1 = (bf16[64,256]{1,0:T(8,128)(2,1)S(1)}, bf16[64,256]{1,0:T(8,128)(2,1)S(1)}, u32[]{:S(2)}, u32[]{:S(2)}) collective-permute-start(bf16[64,256]{1,0:T(8,128)(2,1)S(1)} %convert_bitcast_fusion.refs_0_), channel_id=1, source_target_pairs={{0,128},{64,192},{128,0},{192,64},{1,129},{65,193},{129,1},{193,65... | collective-permute-start | bytes 98312 | tf_op jit(solution)/shard_map/ppermute | solution.py:258
  18.4 7.1 %collective-permute-start.2 = (bf16[64,256]{1,0:T(8,128)(2,1)S(1)}, bf16[64,256]{1,0:T(8,128)(2,1)S(1)}, u32[]{:S(2)}, u32[]{:S(2)}) collective-permute-start(bf16[64,256]{1,0:T(8,128)(2,1)S(1)} %convert_bitcast_fusion.refs_0_), channel_id=1, source_target_pairs={{0,192},{64,128},{128,64},{192,0},{1,193},{65,129},{129,65},{193,1... | collective-permute-start | bytes 98312 | tf_op jit(solution)/shard_map/ppermute | solution.py:258
  24.2 0.7 copy-start.2
  27.4 5.5 %collective-permute-start.3 = (bf16[128,256]{1,0:T(8,128)(2,1)S(1)}, bf16[128,256]{1,0:T(8,128)(2,1)S(1)}, u32[]{:S(2)}, u32[]{:S(2)}) collective-permute-start(bf16[128,256]{1,0:T(8,128)(2,1)S(1)} %get-tuple-element.25), channel_id=1, source_target_pairs={{0,256},{1,257},{2,258},{3,259},{4,260},{5,261},{6,262},{7,263},{8... | collective-permute-start | bytes 196616 | tf_op jit(solution)/shard_map/ppermute | solution.py:313
  29.7 5.7 %collective-permute-start.6 = (bf16[2,4,64,128]{3,2,1,0:T(8,128)(2,1)S(1)}, bf16[2,4,64,128]{3,2,1,0:T(8,128)(2,1)S(1)}, u32[]{:S(2)}, u32[]{:S(2)}) collective-permute-start(bf16[2,4,64,128]{3,2,1,0:T(8,128)(2,1)S(1)} %pad_maximum_fusion), channel_id=1, source_target_pairs={{0,8},{8,0},{1,9},{9,1},{2,10},{10,2},{3,11},{11,3},{4,12},{12,4},... | collective-permute-start | bytes 393224 | tf_op jit(solution)/shard_map/ppermute | solution.py:275
  32.9 0.7 collective-permute-start.4

commit v11 on v10

--- a/solution.py
+++ b/solution.py
@@ -94,19 +94,17 @@
     return out
 
 
-def chain_kernel(first, turn_ref, index_ref, band_first, band_even, band_odd, entering_ref, *refs):
-    columns, (out_ref, state, regions_ref) = refs[:GROUP], refs[-3:]
+def chain_kernel(first, turn_ref, band_first, band_even, band_odd, entering_ref, regions_ref, *refs):
+    out_ref, state = refs[-2:]
     active = turn_ref[0] == 1
 
     @pl.when(active)
     def _():
-        for k in range(GROUP):
-            regions_ref[index_ref[0] ^ k] = columns[k][...]
         run_steps(band_first, band_even, band_odd, entering_ref, regions_ref, out_ref, state)
 
     @pl.when(jnp.logical_not(active))
     def _():
-        out_ref[...] = jnp.zeros_like(out_ref) if first else refs[GROUP][...]
+        out_ref[...] = jnp.zeros_like(out_ref) if first else refs[0][...]
         state[...] = jnp.zeros_like(state)
 
 
@@ -253,10 +251,9 @@
     core = lax.axis_index("core")
     blocks = lax.axis_size("zh")
     local = regions[0].astype(jnp.bfloat16)
-    local, local_source, table = lax.optimization_barrier((local, source[0], table))
-    columns = [local] + [
-        lax.ppermute(local, "x", [(i, i ^ k) for i in range(GROUP)]) for k in range(1, GROUP)
-    ]
+    copies = jnp.broadcast_to(local[None], (GROUP, NX, NY))
+    copies, local_source, table = lax.optimization_barrier((copies, source[0], table))
+    all_regions = lax.all_to_all(copies, "x", 0, 0, tiled=True)
     quarter = (lax.axis_index("yp") * 2 + core).astype(jnp.int32).reshape(1)
     four = jax.ShapeDtypeStruct((GROUP, NX, LANES), jnp.bfloat16)
     pair = jax.ShapeDtypeStruct((2, GROUP, NX, LANES), jnp.bfloat16)
@@ -300,14 +297,13 @@
         waves, *leaving = pl.pallas_call(
             functools.partial(chain_kernel, block == 0),
             out_shape=(wave_shape,) + (() if last else (jax.ShapeDtypeStruct(state_shape, jnp.bfloat16),)),
-            in_specs=[SMEM] * 2 + [VMEM] * (4 + GROUP + len(before)),
+            in_specs=[SMEM] + [VMEM] * (5 + len(before)),
             out_specs=(VMEM,) * (1 if last else 2),
-            scratch_shapes=([pltpu.VMEM(state_shape, jnp.bfloat16)] if last else [])
-            + [pltpu.VMEM((GROUP, NX, NY), jnp.bfloat16)],
+            scratch_shapes=[pltpu.VMEM(state_shape, jnp.bfloat16)] if last else [],
             compiler_params=PARAMS,
-            cost_estimate=cost(100_000_000, 4_000_000),
+            cost_estimate=cost(300_000_000, 4_000_000),
             name="chain",
-        )((zh == block).astype(jnp.int32).reshape(1), mine_x.astype(jnp.int32).reshape(1), *bands, entering, *columns, *before)
+        )((zh == block).astype(jnp.int32).reshape(1), *bands, entering, all_regions, *before)
         before = (waves,)
         if not last:
             entering = lax.ppermute(leaving[0], "zh", [(block, block + 1)])

time: 78.8 us -> 71.5 us (0.907)
  starting transfers between devices: 28.1 us -> 21.3 us
  local copies, waits for them, and re-layouts: 1.66 us -> 0.7 us
    ppermute x3 -> x0, starting transfers between devices: 9.58 us -> none  [body(): lax.ppermute(local, 'x', [(i, i ^ k) for i in range(GROUP)])]
    all_to_all x0 -> x1, starting transfers between devices: none -> 4.84 us  [body(): all_regions = lax.all_to_all(copies, 'x', 0, 0, tiled=True)]
    unnamed x6, local copies, waits for them, and re-layouts: 1.63 us -> 0.01 us
    ppermute x1, starting transfers between devices: 12.4 us -> 10.9 us  [body(): from_core = lax.ppermute(to_core, 'core', [(0, 1), (1, 0)])]
    broadcast_in_dim x0 -> x1, other arithmetic: none -> 0.9 us  [body(): copies = jnp.broadcast_to(local[None], (GROUP, NX, NY))]
    convert_element_type x1 -> x0, other arithmetic: 0.89 us -> none  [body(): local = regions[0].astype(jnp.bfloat16)]
    all_to_all x1, blocking collectives: 13.1 us -> 14 us  [body(): waves = lax.all_to_all(waves, ('x',) + QUAD, 0, 0, tiled=True)]
  transfers between devices with their start and end apart: 7 -> 5, of which waited for: 1 -> 1; matrix products, arithmetic and copies ran while one was open for 0% -> 0% of each run, Pallas kernels for 3% -> 4%
where the time goes in v11:
time: 71.5 us; the launch traced here: 71.1 us
  blocking collectives  40.3 us (56%)
  starting transfers between devices  21.3 us (30%)
  Pallas kernels  5.93 us (8%)
  waiting for transfers between devices  1.73 us (2%)
  other arithmetic  0.92 us (1%)
    all_to_all x1, blocking collectives, body(): parts = lax.all_to_all(partial_image, FREQ, 0, 0, tiled=True)  26.3 us
    all_to_all x1, blocking collectives, body(): waves = lax.all_to_all(waves, ('x',) + QUAD, 0, 0, tiled=True)  14 us
    ppermute x1, starting transfers between devices, body(): from_core = lax.ppermute(to_core, 'core', [(0, 1), (1, 0)])  10.9 us
    all_to_all x1, starting transfers between devices, body(): all_regions = lax.all_to_all(copies, 'x', 0, 0, tiled=True)  4.84 us
    ppermute x1, starting transfers between devices, body(): lax.ppermute(jnp.concatenate([to_chip, from_core[1:]], axis=0), 'yp', [(0...  3.2 us
    pallas_call x1, Pallas kernels, body(): pl.pallas_call(lambda *refs: image_kernel(scale, *refs), out_shape=jax.Sh...  2.39 us
    ppermute x2, starting transfers between devices, body(): entering = lax.ppermute(leaving[0], 'zh', [(block, block + 1)])  2.38 us
    pallas_call x3, Pallas kernels, body(): pl.pallas_call(functools.partial(chain_kernel, block == 0), out_shape=(wa...  1.97 us
  transfers between devices with their start and end apart: 5, of which 1 were waited for; matrix products, arithmetic and copies ran while one was open for 0% of the time, Pallas kernels for 4%

profile of v11, /device:TPU:1, one launch (start us, length us, event | category | flops | bytes accessed | tf_op | source)
XLA Modules:
  0.0 71.1 jit_solution(10510182519691444186)
XLA Ops:
  0.0 0.0 copy-start
  0.0 0.0 copy-start.1
  0.0 0.9 %convert_bitcast_fusion = bf16[64,256]{1,0:T(8,128)(2,1)S(1)} fusion(s32[1,64,256]{2,1,0:T(8,128)} %param.5), kind=kLoop, calls=%fused_computation.1 | loop fusion | flops 16384 | bytes 98304 | tf_op jit(solution)/shard_map/broadcast_in_dim | solution.py:254
  0.9 0.7 broadcast_in_dim.9
  1.6 4.8 %all-to-all-start = ((bf16[4,64,256]{2,1,0:T(8,128)(2,1)}), bf16[4,64,256]{2,1,0:T(8,128)(2,1)S(1)}, u32[]{:S(2)}, u32[]{:S(2)}) async-start(bf16[4,64,256]{2,1,0:T(8,128)(2,1)} %broadcast_in_dim.9), calls=%async_computation | async-start | bytes 262144 | tf_op jit(solution)/shard_map/all_to_all | solution.py:256
  6.4 0.0 copy-done.1
  6.4 0.3 pack.1
  6.7 0.0 copy-start.2
  6.7 10.9 %collective-permute-start.2 = (bf16[2,4,64,128]{3,2,1,0:T(8,128)(2,1)S(1)}, bf16[2,4,64,128]{3,2,1,0:T(8,128)(2,1)S(1)}, u32[]{:S(2)}, u32[]{:S(2)}) collective-permute-start(bf16[2,4,64,128]{3,2,1,0:T(8,128)(2,1)S(1)} %get-tuple-element.31), channel_id=1, source_target_pairs={{0,1},{1,0},{2,3},{3,2},{4,5},{5,4},{6,7},{7,6},{8,9},{9,8},{10,11... | collective-permute-start | bytes 393224 | tf_op jit(solution)/shard_map/ppermute | solution.py:271
  17.7 0.0 copy-done.2
  17.7 0.5 bands.1
  18.2 0.0 copy-done
  18.3 0.0 all-to-all-done.regions_ref
  18.3 1.9 %chain.3 = (bf16[16,64,128]{2,1,0:T(8,128)(2,1)S(1)}, bf16[128,256]{1,0:T(8,128)(2,1)S(1)}) custom-call(s32[1]{0:T(128)} %bitcast.7.turn_ref, bf16[512,128]{1,0:T(8,128)(2,1)S(1)} %get-tuple-element.21.band_first, bf16[256,512]{1,0:T(8,128)(2,1)S(1)} %get-tuple-element.22.band_even, bf16[256,512]{1,0:T(8,128)(2,1)S(1)} %get-tuple-element.23.band_odd, ...), custom_call_target="tpu_custom_call" | custom-call | flops 300000000 | bytes 4000000 | tf_op jit(solution)/shard_map/chain/pallas_call | solution.py:297
  20.2 1.7 %collective-permute-start = (bf16[128,256]{1,0:T(8,128)(2,1)S(1)}, bf16[128,256]{1,0:T(8,128)(2,1)S(1)}, u32[]{:S(2)}, u32[]{:S(2)}) collective-permute-start(bf16[128,256]{1,0:T(8,128)(2,1)S(1)} %get-tuple-element.25), channel_id=1, source_target_pairs={{0,256},{1,257},{2,258},{3,259},{4,260},{5,261},{6,262},{7,263},{8... | collective-permute-start | bytes 196616 | tf_op jit(solution)/shard_map/ppermute | solution.py:309
  21.9 0.0 collective-permute-done.2.refs_3_
  22.0 3.2 %collective-permute-start.3 = (bf16[2,4,64,128]{3,2,1,0:T(8,128)(2,1)S(1)}, bf16[2,4,64,128]{3,2,1,0:T(8,128)(2,1)S(1)}, u32[]{:S(2)}, u32[]{:S(2)}) collective-permute-start(bf16[2,4,64,128]{3,2,1,0:T(8,128)(2,1)S(1)} %pad_maximum_fusion), channel_id=1, source_target_pairs={{0,8},{8,0},{1,9},{9,1},{2,10},{10,2},{3,11},{11,3},{4,12},{12,4},... | collective-permute-start | bytes 393224 | tf_op jit(solution)/shard_map/ppermute | solution.py:272
  25.2 0.0 collective-permute-done.entering_ref
  25.2 0.7 collective-permute-start.1
  25.9 0.0 collective-permute-done.1.entering_ref
  26.0 1.7 %collective-permute-done.3.refs_4_ = bf16[2,4,64,128]{3,2,1,0:T(8,128)(2,1)S(1)} collective-permute-done((bf16[2,4,64,128]{3,2,1,0:T(8,128)(2,1)S(1)}, bf16[2,4,64,128]{3,2,1,0:T(8,128)(2,1)S(1)}, u32[]{:S(2)}, u32[]{:S(2)}) %collective-permute-start.3) | collective-permute-done | bytes 131104 | tf_op jit(solution)/shard_map/ppermute | solution.py:272
  27.7 14.0 %all_to_all.15.refs_1_ = bf16[16,64,128]{2,1,0:T(8,128)(2,1)S(1)} all-to-all(bf16[16,64,128]{2,1,0:T(8,128)(2,1)S(1)} %chain.5), channel_id=1, replica_groups=mesh['zh'=3,'x'=4,'yq'=4,'yp'=2,'zl'=4,'core'=2] {'x','yp','core'}, dimensions={0} | all-to-all | bytes 524288 | tf_op jit(solution)/shard_map/all_to_all | solution.py:312
  41.6 2.4 %image.1 = bf16[64,16,128]{2,1,0:T(8,128)(2,1)S(1)} custom-call(s32[1]{0:T(128)} %bitcast.quarter_ref.refs_0_, bf16[16,64,128]{2,1,0:T(8,128)(2,1)S(1)} %all_to_all.15.refs_1_, bf16[4,64,128]{2,1,0:T(8,128)(2,1)S(1)} %get-tuple-element.33.refs_2_, bf16[2,4,64,128]{3,2,1,0:T(8,128)(2,1)S(1)} %collective-permute-done.2.refs_3_, ...), custom_call_target="tpu_custom_call" | custom-call | flops 10000000 | bytes 2000000 | tf_op jit(solution)/shard_map/image/pallas_call | solution.py:315
  44.0 26.3 %all_to_all.16.part_ref = bf16[64,16,128]{2,1,0:T(8,128)(2,1)S(1)} all-to-all(bf16[64,16,128]{2,1,0:T(8,128)(2,1)S(1)} %image.1), channel_id=1, replica_groups=mesh['zh'=3,'x'=4,'yq'=4,'yp'=2,'zl'=4,'core'=2] {'yq','yp','zl','core'}, dimensions={0} | all-to-all | bytes 524288 | tf_op jit(solution)/shard_map/all_to_all | solution.py:327
  70.4 0.7 %total.1 = f32[1,32,1,256]{3,2,1,0:T(1,128)} custom-call(bf16[64,16,128]{2,1,0:T(8,128)(2,1)S(1)} %all_to_all.16.part_ref), custom_call_target="tpu_custom_call" | custom-call | tf_op jit(solution)/shard_map/total/pallas_call | solution.py:329
  (6 shorter events, 0.1 us)
Async XLA Ops:
  0.0 18.3 %copy-start = (bf16[4,2,64,256]{3,2,1,0:T(8,128)(2,1)S(1)}, bf16[4,2,64,256]{3,2,1,0:T(8,128)(2,1)}, u32[]{:S(2)}) copy-start(bf16[4,2,64,256]{3,2,1,0:T(8,128)(2,1)} %param.4) | copy-start | bytes 786436
  0.0 6.4 %copy-start.1 = (bf16[1,4,2,64,256]{4,3,2,1,0:T(8,128)(2,1)S(1)}, bf16[1,4,2,64,256]{4,3,2,1,0:T(8,128)(2,1)}, u32[]{:S(2)}) copy-start(bf16[1,4,2,64,256]{4,3,2,1,0:T(8,128)(2,1)} %param.7) | copy-start | bytes 786436
  1.6 16.7 %all-to-all-start = ((bf16[4,64,256]{2,1,0:T(8,128)(2,1)}), bf16[4,64,256]{2,1,0:T(8,128)(2,1)S(1)}, u32[]{:S(2)}, u32[]{:S(2)}) async-start(bf16[4,64,256]{2,1,0:T(8,128)(2,1)} %broadcast_in_dim.9), calls=%async_computation | async-start | bytes 262144 | tf_op jit(solution)/shard_map/all_to_all | solution.py:256
  6.7 11.0 %copy-start.2 = (bf16[4,4,2,2,25]{4,3,2,1,0:T(2,128)(2,1)S(1)}, bf16[4,4,2,2,25]{4,3,2,1,0:T(2,128)(2,1)}, u32[]{:S(2)}) copy-start(bf16[4,4,2,2,25]{4,3,2,1,0:T(2,128)(2,1)} %param.6) | copy-start | bytes 9604
  6.7 15.2 %collective-permute-start.2 = (bf16[2,4,64,128]{3,2,1,0:T(8,128)(2,1)S(1)}, bf16[2,4,64,128]{3,2,1,0:T(8,128)(2,1)S(1)}, u32[]{:S(2)}, u32[]{:S(2)}) collective-permute-start(bf16[2,4,64,128]{3,2,1,0:T(8,128)(2,1)S(1)} %get-tuple-element.31), channel_id=1, source_target_pairs={{0,1},{1,0},{2,3},{3,2},{4,5},{5,4},{6,7},{7,6},{8,9},{9,8},{10,11... | collective-permute-start | bytes 393224 | tf_op jit(solution)/shard_map/ppermute | solution.py:271
  20.2 5.0 %collective-permute-start = (bf16[128,256]{1,0:T(8,128)(2,1)S(1)}, bf16[128,256]{1,0:T(8,128)(2,1)S(1)}, u32[]{:S(2)}, u32[]{:S(2)}) collective-permute-start(bf16[128,256]{1,0:T(8,128)(2,1)S(1)} %get-tuple-element.25), channel_id=1, source_target_pairs={{0,256},{1,257},{2,258},{3,259},{4,260},{5,261},{6,262},{7,263},{8... | collective-permute-start | bytes 196616 | tf_op jit(solution)/shard_map/ppermute | solution.py:309
  22.0 5.7 %collective-permute-start.3 = (bf16[2,4,64,128]{3,2,1,0:T(8,128)(2,1)S(1)}, bf16[2,4,64,128]{3,2,1,0:T(8,128)(2,1)S(1)}, u32[]{:S(2)}, u32[]{:S(2)}) collective-permute-start(bf16[2,4,64,128]{3,2,1,0:T(8,128)(2,1)S(1)} %pad_maximum_fusion), channel_id=1, source_target_pairs={{0,8},{8,0},{1,9},{9,1},{2,10},{10,2},{3,11},{11,3},{4,12},{12,4},... | collective-permute-start | bytes 393224 | tf_op jit(solution)/shard_map/ppermute | solution.py:272
  25.2 0.7 collective-permute-start.1

commit v12 on v11

--- a/solution.py
+++ b/solution.py
@@ -153,7 +153,7 @@
 
 
 def pack_kernel(quarter_ref, source_ref, *refs):
-    own_ref, core_ref, chip_ref, packed = refs
+    own_ref, chip_ref, core_ref, packed = refs
     row_at = lax.broadcasted_iota(jnp.int32, (NX, NX), 0)
     col_at = lax.broadcasted_iota(jnp.int32, (NX, NX), 1)
     flip = (row_at + col_at == NX - 1).astype(jnp.bfloat16)
@@ -169,13 +169,13 @@
             packed[half * 2 + 1, f] = jnp.where(left, b, a).astype(jnp.bfloat16)
     mine = quarter_ref[0]
     own_ref[...] = packed[mine]
+    chip_ref[0] = packed[mine ^ 2]
+    chip_ref[1] = packed[mine ^ 3]
     core_ref[0] = packed[mine ^ 1]
-    core_ref[1] = packed[mine ^ 3]
-    chip_ref[0] = packed[mine ^ 2]
 
 
 def image_kernel(scale, quarter_ref, wave_ref, own_ref, core_ref, chip_ref, out_ref, wave, src, totals):
-    sources = [own_ref, core_ref.at[0], chip_ref.at[0], chip_ref.at[1]]
+    sources = [own_ref, core_ref.at[0], chip_ref.at[0], core_ref.at[1]]
     edge = jnp.zeros((4 * GROUP, REACH, LANES), jnp.float32)
     for ref in (wave, src):
         ref[:, :REACH, :] = edge
@@ -215,7 +215,7 @@
         out_ref[x] = jnp.where(left, total[:REACH], total[REACH:]).astype(jnp.bfloat16)
         return carry
 
-    lax.fori_loop(0, NX, fold, 0, unroll=32)
+    lax.fori_loop(0, NX, fold, 0, unroll=True)
 
 
 def sum_kernel(part_ref, out_ref):
@@ -258,7 +258,7 @@
     four = jax.ShapeDtypeStruct((GROUP, NX, LANES), jnp.bfloat16)
     pair = jax.ShapeDtypeStruct((2, GROUP, NX, LANES), jnp.bfloat16)
     one = jax.ShapeDtypeStruct((1, GROUP, NX, LANES), jnp.bfloat16)
-    packed, to_core, to_chip = pl.pallas_call(
+    packed, to_chip, to_core = pl.pallas_call(
         pack_kernel,
         out_shape=(four, pair, one),
         in_specs=[SMEM, VMEM],
@@ -268,9 +268,9 @@
         cost_estimate=cost(20_000_000, 1_000_000),
         name="pack",
     )(quarter, local_source)
-    from_core = lax.ppermute(to_core, "core", [(0, 1), (1, 0)])
-    from_chip = lax.ppermute(
-        jnp.concatenate([to_chip, from_core[1:]], axis=0), "yp", [(0, 1), (1, 0)]
+    from_chip = lax.ppermute(to_chip, "yp", [(0, 1), (1, 0)])
+    from_core = lax.ppermute(
+        jnp.concatenate([to_core, from_chip[1:]], axis=0), "core", [(0, 1), (1, 0)]
     )
 
     padded = jnp.pad(table.reshape(GROUP * R * 4, TAPS), ((0, 0), (0, LANES - TAPS)))
@@ -308,7 +308,7 @@
         if not last:
             entering = lax.ppermute(leaving[0], "zh", [(block, block + 1)])
 
-    waves, from_chip = lax.optimization_barrier((waves, from_chip))
+    waves, from_core = lax.optimization_barrier((waves, from_core))
     waves = lax.all_to_all(waves, ("x",) + QUAD, 0, 0, tiled=True)
 
     scale = 1.0 / math.sqrt(surface.shape[0] * lax.axis_size(FREQ))

time: 71.5 us -> 72.1 us (level)
  the two profiles are of different devices: /device:TPU:1 before, /device:TPU:513 now
where the time goes in v12:
time: 72.1 us; the launch traced here: 71.7 us
  blocking collectives  42.1 us (58%)
  starting transfers between devices  12.9 us (18%)
  waiting for transfers between devices  9.18 us (13%)
  Pallas kernels  5.8 us (8%)
  other arithmetic  0.92 us (1%)
    all_to_all x1, blocking collectives, body(): parts = lax.all_to_all(partial_image, FREQ, 0, 0, tiled=True)  27.8 us
    all_to_all x1, blocking collectives, body(): waves = lax.all_to_all(waves, ('x',) + QUAD, 0, 0, tiled=True)  14.3 us
    ppermute x2, waiting for transfers between devices, body(): entering = lax.ppermute(leaving[0], 'zh', [(block, block + 1)])  7.71 us
    all_to_all x1, starting transfers between devices, body(): all_regions = lax.all_to_all(copies, 'x', 0, 0, tiled=True)  4.01 us
    ppermute x1, starting transfers between devices, body(): lax.ppermute(jnp.concatenate([to_core, from_chip[1:]], axis=0), 'core', [...  3.72 us
    ppermute x1, starting transfers between devices, body(): from_chip = lax.ppermute(to_chip, 'yp', [(0, 1), (1, 0)])  3.21 us
    pallas_call x1, Pallas kernels, body(): pl.pallas_call(lambda *refs: image_kernel(scale, *refs), out_shape=jax.Sh...  2.26 us
    pallas_call x3, Pallas kernels, body(): pl.pallas_call(functools.partial(chain_kernel, block == 0), out_shape=(wa...  1.98 us
  transfers between devices with their start and end apart: 5, of which 3 were waited for; matrix products, arithmetic and copies ran while one was open for 0% of the time, Pallas kernels for 4%

profile of v12, /device:TPU:513, one launch (start us, length us, event | category | flops | bytes accessed | tf_op | source)
XLA Modules:
  0.0 71.7 jit_solution(2924663776103044181)
XLA Ops:
  0.0 0.0 copy-start
  0.0 0.0 copy-start.1
  0.0 0.9 %convert_bitcast_fusion = bf16[64,256]{1,0:T(8,128)(2,1)S(1)} fusion(s32[1,64,256]{2,1,0:T(8,128)} %param.5), kind=kLoop, calls=%fused_computation.1 | loop fusion | flops 16384 | bytes 98304 | tf_op jit(solution)/shard_map/broadcast_in_dim | solution.py:254
  0.9 0.7 broadcast_in_dim.9
  1.6 4.0 %all-to-all-start = ((bf16[4,64,256]{2,1,0:T(8,128)(2,1)}), bf16[4,64,256]{2,1,0:T(8,128)(2,1)S(1)}, u32[]{:S(2)}, u32[]{:S(2)}) async-start(bf16[4,64,256]{2,1,0:T(8,128)(2,1)} %broadcast_in_dim.9), calls=%async_computation | async-start | bytes 262144 | tf_op jit(solution)/shard_map/all_to_all | solution.py:256
  5.6 0.0 copy-done.1
  5.6 0.3 pack.1
  5.9 0.0 copy-start.2
  5.9 3.2 %collective-permute-start.2 = (bf16[2,4,64,128]{3,2,1,0:T(8,128)(2,1)S(1)}, bf16[2,4,64,128]{3,2,1,0:T(8,128)(2,1)S(1)}, u32[]{:S(2)}, u32[]{:S(2)}) collective-permute-start(bf16[2,4,64,128]{3,2,1,0:T(8,128)(2,1)S(1)} %get-tuple-element.31), channel_id=1, source_target_pairs={{0,8},{8,0},{1,9},{9,1},{2,10},{10,2},{3,11},{11,3},{4,12},{12,4},... | collective-permute-start | bytes 393224 | tf_op jit(solution)/shard_map/ppermute | solution.py:271
  9.1 0.0 copy-done.2
  9.2 0.5 bands.1
  9.7 0.0 copy-done
  9.7 0.7 all-to-all-done.regions_ref
  10.5 0.7 collective-permute-start
  11.1 0.8 %collective-permute-done.2.refs_4_ = bf16[2,4,64,128]{3,2,1,0:T(8,128)(2,1)S(1)} collective-permute-done((bf16[2,4,64,128]{3,2,1,0:T(8,128)(2,1)S(1)}, bf16[2,4,64,128]{3,2,1,0:T(8,128)(2,1)S(1)}, u32[]{:S(2)}, u32[]{:S(2)}) %collective-permute-start.2) | collective-permute-done | bytes 131104 | tf_op jit(solution)/shard_map/ppermute | solution.py:271
  11.9 3.7 %collective-permute-start.3 = (bf16[2,4,64,128]{3,2,1,0:T(8,128)(2,1)S(1)}, bf16[2,4,64,128]{3,2,1,0:T(8,128)(2,1)S(1)}, u32[]{:S(2)}, u32[]{:S(2)}) collective-permute-start(bf16[2,4,64,128]{3,2,1,0:T(8,128)(2,1)S(1)} %pad_maximum_fusion), channel_id=1, source_target_pairs={{0,1},{1,0},{2,3},{3,2},{4,5},{5,4},{6,7},{7,6},{8,9},{9,8},{10,11... | collective-permute-start | bytes 393224 | tf_op jit(solution)/shard_map/ppermute | solution.py:272
  15.7 0.0 collective-permute-done.entering_ref
  15.7 1.3 %collective-permute-start.1 = (bf16[128,256]{1,0:T(8,128)(2,1)S(1)}, bf16[128,256]{1,0:T(8,128)(2,1)S(1)}, u32[]{:S(2)}, u32[]{:S(2)}) collective-permute-start(bf16[128,256]{1,0:T(8,128)(2,1)S(1)} %get-tuple-element.27), channel_id=1, source_target_pairs={{256,512},{257,513},{258,514},{259,515},{260,516},{261,517},{262,5... | collective-permute-start | bytes 196616 | tf_op jit(solution)/shard_map/ppermute | solution.py:309
  17.0 7.7 %collective-permute-done.1.entering_ref = bf16[128,256]{1,0:T(8,128)(2,1)S(1)} collective-permute-done((bf16[128,256]{1,0:T(8,128)(2,1)S(1)}, bf16[128,256]{1,0:T(8,128)(2,1)S(1)}, u32[]{:S(2)}, u32[]{:S(2)}) %collective-permute-start.1) | collective-permute-done | bytes 65568 | tf_op jit(solution)/shard_map/ppermute | solution.py:309
  24.7 1.9 %chain.5 = bf16[16,64,128]{2,1,0:T(8,128)(2,1)S(1)} custom-call(s32[1]{0:T(128)} %bitcast.1.turn_ref, bf16[512,128]{1,0:T(8,128)(2,1)S(1)} %get-tuple-element.21.band_first, bf16[256,512]{1,0:T(8,128)(2,1)S(1)} %get-tuple-element.22.band_even, bf16[256,512]{1,0:T(8,128)(2,1)S(1)} %get-tuple-element.23.band_odd, ...), custom_call_target="tpu_custom_call" | custom-call | flops 300000000 | bytes 4000000 | tf_op jit(solution)/shard_map/chain/pallas_call | solution.py:297
  26.6 0.0 collective-permute-done.3.refs_3_
  26.6 14.3 %all_to_all.15.refs_1_ = bf16[16,64,128]{2,1,0:T(8,128)(2,1)S(1)} all-to-all(bf16[16,64,128]{2,1,0:T(8,128)(2,1)S(1)} %chain.5), channel_id=1, replica_groups=mesh['zh'=3,'x'=4,'yq'=4,'yp'=2,'zl'=4,'core'=2] {'x','yp','core'}, dimensions={0} | all-to-all | bytes 524288 | tf_op jit(solution)/shard_map/all_to_all | solution.py:312
  40.9 2.3 %image.1 = bf16[64,16,128]{2,1,0:T(8,128)(2,1)S(1)} custom-call(s32[1]{0:T(128)} %bitcast.quarter_ref.refs_0_, bf16[16,64,128]{2,1,0:T(8,128)(2,1)S(1)} %all_to_all.15.refs_1_, bf16[4,64,128]{2,1,0:T(8,128)(2,1)S(1)} %get-tuple-element.33.refs_2_, bf16[2,4,64,128]{3,2,1,0:T(8,128)(2,1)S(1)} %collective-permute-done.3.refs_3_, ...), custom_call_target="tpu_custom_call" | custom-call | flops 10000000 | bytes 2000000 | tf_op jit(solution)/shard_map/image/pallas_call | solution.py:315
  43.2 27.8 %all_to_all.16.part_ref = bf16[64,16,128]{2,1,0:T(8,128)(2,1)S(1)} all-to-all(bf16[64,16,128]{2,1,0:T(8,128)(2,1)S(1)} %image.1), channel_id=1, replica_groups=mesh['zh'=3,'x'=4,'yq'=4,'yp'=2,'zl'=4,'core'=2] {'yq','yp','zl','core'}, dimensions={0} | all-to-all | bytes 524288 | tf_op jit(solution)/shard_map/all_to_all | solution.py:327
  71.0 0.7 %total.1 = f32[1,32,1,256]{3,2,1,0:T(1,128)} custom-call(bf16[64,16,128]{2,1,0:T(8,128)(2,1)S(1)} %all_to_all.16.part_ref), custom_call_target="tpu_custom_call" | custom-call | tf_op jit(solution)/shard_map/total/pallas_call | solution.py:329
  (6 shorter events, 0.1 us)
Async XLA Ops:
  0.0 9.7 %copy-start = (bf16[4,2,64,256]{3,2,1,0:T(8,128)(2,1)S(1)}, bf16[4,2,64,256]{3,2,1,0:T(8,128)(2,1)}, u32[]{:S(2)}) copy-start(bf16[4,2,64,256]{3,2,1,0:T(8,128)(2,1)} %param.4) | copy-start | bytes 786436
  0.0 5.6 %copy-start.1 = (bf16[1,4,2,64,256]{4,3,2,1,0:T(8,128)(2,1)S(1)}, bf16[1,4,2,64,256]{4,3,2,1,0:T(8,128)(2,1)}, u32[]{:S(2)}) copy-start(bf16[1,4,2,64,256]{4,3,2,1,0:T(8,128)(2,1)} %param.7) | copy-start | bytes 786436
  1.6 8.8 %all-to-all-start = ((bf16[4,64,256]{2,1,0:T(8,128)(2,1)}), bf16[4,64,256]{2,1,0:T(8,128)(2,1)S(1)}, u32[]{:S(2)}, u32[]{:S(2)}) async-start(bf16[4,64,256]{2,1,0:T(8,128)(2,1)} %broadcast_in_dim.9), calls=%async_computation | async-start | bytes 262144 | tf_op jit(solution)/shard_map/all_to_all | solution.py:256
  5.9 3.2 %copy-start.2 = (bf16[4,4,2,2,25]{4,3,2,1,0:T(2,128)(2,1)S(1)}, bf16[4,4,2,2,25]{4,3,2,1,0:T(2,128)(2,1)}, u32[]{:S(2)}) copy-start(bf16[4,4,2,2,25]{4,3,2,1,0:T(2,128)(2,1)} %param.6) | copy-start | bytes 9604
  5.9 6.0 %collective-permute-start.2 = (bf16[2,4,64,128]{3,2,1,0:T(8,128)(2,1)S(1)}, bf16[2,4,64,128]{3,2,1,0:T(8,128)(2,1)S(1)}, u32[]{:S(2)}, u32[]{:S(2)}) collective-permute-start(bf16[2,4,64,128]{3,2,1,0:T(8,128)(2,1)S(1)} %get-tuple-element.31), channel_id=1, source_target_pairs={{0,8},{8,0},{1,9},{9,1},{2,10},{10,2},{3,11},{11,3},{4,12},{12,4},... | collective-permute-start | bytes 393224 | tf_op jit(solution)/shard_map/ppermute | solution.py:271
  10.5 5.2 %collective-permute-start = (bf16[128,256]{1,0:T(8,128)(2,1)S(1)}, bf16[128,256]{1,0:T(8,128)(2,1)S(1)}, u32[]{:S(2)}, u32[]{:S(2)}) collective-permute-start(bf16[128,256]{1,0:T(8,128)(2,1)S(1)} %get-tuple-element.25), channel_id=1, source_target_pairs={{0,256},{1,257},{2,258},{3,259},{4,260},{5,261},{6,262},{7,263},{8... | collective-permute-start | bytes 196616 | tf_op jit(solution)/shard_map/ppermute | solution.py:309
  11.9 14.7 %collective-permute-start.3 = (bf16[2,4,64,128]{3,2,1,0:T(8,128)(2,1)S(1)}, bf16[2,4,64,128]{3,2,1,0:T(8,128)(2,1)S(1)}, u32[]{:S(2)}, u32[]{:S(2)}) collective-permute-start(bf16[2,4,64,128]{3,2,1,0:T(8,128)(2,1)S(1)} %pad_maximum_fusion), channel_id=1, source_target_pairs={{0,1},{1,0},{2,3},{3,2},{4,5},{5,4},{6,7},{7,6},{8,9},{9,8},{10,11... | collective-permute-start | bytes 393224 | tf_op jit(solution)/shard_map/ppermute | solution.py:272
  15.7 9.0 %collective-permute-start.1 = (bf16[128,256]{1,0:T(8,128)(2,1)S(1)}, bf16[128,256]{1,0:T(8,128)(2,1)S(1)}, u32[]{:S(2)}, u32[]{:S(2)}) collective-permute-start(bf16[128,256]{1,0:T(8,128)(2,1)S(1)} %get-tuple-element.27), channel_id=1, source_target_pairs={{256,512},{257,513},{258,514},{259,515},{260,516},{261,517},{262,5... | collective-permute-start | bytes 196616 | tf_op jit(solution)/shard_map/ppermute | solution.py:309

commit v13 on v12

--- a/solution.py
+++ b/solution.py
@@ -21,10 +21,10 @@
 MID = TAPS // 2
 GROUP = 4
 
-AXES = ("zh", "x", "yq", "yp", "zl", "core")
+AXES = ("zh", "x", "y", "zq", "zp", "core")
 DEPTH = ("zh", "x")
-FREQ = ("yq", "yp", "zl", "core")
-QUAD = ("yp", "core")
+FREQ = ("y", "zq", "zp", "core")
+QUAD = ("zp", "core")
 
 
 def onehot(shape, fit, value=1.0):
@@ -219,16 +219,14 @@
 
 
 def sum_kernel(part_ref, out_ref):
-    many, line = part_ref.shape[0], 8
+    many = part_ref.shape[0]
     left = lax.broadcasted_iota(jnp.int32, (REACH, LANES), 1) < QUARTER
     for half in range(2):
         totals = []
         for q in (2 * half, 2 * half + 1):
-            pair, core = divmod(q, 2)
             total = jnp.zeros((REACH, LANES), jnp.float32)
-            for start in range(pair * line, many, 2 * line):
-                for i in range(start + core, start + line, 2):
-                    total = total + part_ref[i].astype(jnp.float32)
+            for i in range(q, many, 4):
+                total = total + part_ref[i].astype(jnp.float32)
             totals.append(total)
         a, b = totals
         cols = slice(half * LANES, (half + 1) * LANES)
@@ -254,7 +252,7 @@
     copies = jnp.broadcast_to(local[None], (GROUP, NX, NY))
     copies, local_source, table = lax.optimization_barrier((copies, source[0], table))
     all_regions = lax.all_to_all(copies, "x", 0, 0, tiled=True)
-    quarter = (lax.axis_index("yp") * 2 + core).astype(jnp.int32).reshape(1)
+    quarter = (lax.axis_index("zp") * 2 + core).astype(jnp.int32).reshape(1)
     four = jax.ShapeDtypeStruct((GROUP, NX, LANES), jnp.bfloat16)
     pair = jax.ShapeDtypeStruct((2, GROUP, NX, LANES), jnp.bfloat16)
     one = jax.ShapeDtypeStruct((1, GROUP, NX, LANES), jnp.bfloat16)
@@ -268,7 +266,7 @@
         cost_estimate=cost(20_000_000, 1_000_000),
         name="pack",
     )(quarter, local_source)
-    from_chip = lax.ppermute(to_chip, "yp", [(0, 1), (1, 0)])
+    from_chip = lax.ppermute(to_chip, "zp", [(0, 1), (1, 0)])
     from_core = lax.ppermute(
         jnp.concatenate([to_core, from_chip[1:]], axis=0), "core", [(0, 1), (1, 0)]
     )
@@ -337,7 +335,7 @@
 
 
 def solution(mesh):
-    wide = Mesh(np.asarray(mesh.devices).reshape(3, 4, 4, 2, 4, 2), AXES)
+    wide = Mesh(np.asarray(mesh.devices).reshape(3, 4, 8, 2, 2, 2), AXES)
     in_specs = (
         P(FREQ, None, None, None),
         P(DEPTH, None, None),

time: 72.1 us -> 72.1 us (level)
    all_to_all x1, blocking collectives: 27.8 us -> 26.6 us  [body(): parts = lax.all_to_all(partial_image, FREQ, 0, 0, tiled=True)]
    all_to_all x1, blocking collectives: 14.3 us -> 15.5 us  [body(): waves = lax.all_to_all(waves, ('x',) + QUAD, 0, 0, tiled=True)]
where the time goes in v13:
time: 72.1 us; the launch traced here: 71.7 us
  blocking collectives  42 us (58%)
  starting transfers between devices  12.8 us (18%)
  waiting for transfers between devices  9.27 us (13%)
  Pallas kernels  5.8 us (8%)
  other arithmetic  0.92 us (1%)
    all_to_all x1, blocking collectives, body(): parts = lax.all_to_all(partial_image, FREQ, 0, 0, tiled=True)  26.6 us
    all_to_all x1, blocking collectives, body(): waves = lax.all_to_all(waves, ('x',) + QUAD, 0, 0, tiled=True)  15.5 us
    ppermute x2, waiting for transfers between devices, body(): entering = lax.ppermute(leaving[0], 'zh', [(block, block + 1)])  7.71 us
    all_to_all x1, starting transfers between devices, body(): all_regions = lax.all_to_all(copies, 'x', 0, 0, tiled=True)  4.01 us
    ppermute x1, starting transfers between devices, body(): lax.ppermute(jnp.concatenate([to_core, from_chip[1:]], axis=0), 'core', [...  3.72 us
    ppermute x1, starting transfers between devices, body(): from_chip = lax.ppermute(to_chip, 'zp', [(0, 1), (1, 0)])  3.11 us
    pallas_call x1, Pallas kernels, body(): pl.pallas_call(lambda *refs: image_kernel(scale, *refs), out_shape=jax.Sh...  2.26 us
    pallas_call x3, Pallas kernels, body(): pl.pallas_call(functools.partial(chain_kernel, block == 0), out_shape=(wa...  1.98 us
  transfers between devices with their start and end apart: 5, of which 3 were waited for; matrix products, arithmetic and copies ran while one was open for 0% of the time, Pallas kernels for 4%

profile of v13, /device:TPU:513, one launch (start us, length us, event | category | flops | bytes accessed | tf_op | source)
XLA Modules:
  0.0 71.7 jit_solution(4311664166826009519)
XLA Ops:
  0.0 0.0 copy-start
  0.0 0.0 copy-start.1
  0.0 0.9 %convert_bitcast_fusion = bf16[64,256]{1,0:T(8,128)(2,1)S(1)} fusion(s32[1,64,256]{2,1,0:T(8,128)} %param.5), kind=kLoop, calls=%fused_computation.1 | loop fusion | flops 16384 | bytes 98304 | tf_op jit(solution)/shard_map/broadcast_in_dim | solution.py:252
  0.9 0.7 broadcast_in_dim.9
  1.6 4.0 %all-to-all-start = ((bf16[4,64,256]{2,1,0:T(8,128)(2,1)}), bf16[4,64,256]{2,1,0:T(8,128)(2,1)S(1)}, u32[]{:S(2)}, u32[]{:S(2)}) async-start(bf16[4,64,256]{2,1,0:T(8,128)(2,1)} %broadcast_in_dim.9), calls=%async_computation | async-start | bytes 262144 | tf_op jit(solution)/shard_map/all_to_all | solution.py:254
  5.6 0.0 copy-done.1
  5.6 0.3 pack.1
  5.9 0.0 copy-start.2
  5.9 3.1 %collective-permute-start.2 = (bf16[2,4,64,128]{3,2,1,0:T(8,128)(2,1)S(1)}, bf16[2,4,64,128]{3,2,1,0:T(8,128)(2,1)S(1)}, u32[]{:S(2)}, u32[]{:S(2)}) collective-permute-start(bf16[2,4,64,128]{3,2,1,0:T(8,128)(2,1)S(1)} %get-tuple-element.31), channel_id=1, source_target_pairs={{0,2},{2,0},{1,3},{3,1},{4,6},{6,4},{5,7},{7,5},{8,10},{10,8},{9,1... | collective-permute-start | bytes 393224 | tf_op jit(solution)/shard_map/ppermute | solution.py:269
  9.0 0.0 copy-done.2
  9.1 0.5 bands.1
  9.6 0.0 copy-done
  9.6 0.8 %all-to-all-done.regions_ref = bf16[4,64,256]{2,1,0:T(8,128)(2,1)S(1)} async-done(((bf16[4,64,256]{2,1,0:T(8,128)(2,1)}), bf16[4,64,256]{2,1,0:T(8,128)(2,1)S(1)}, u32[]{:S(2)}, u32[]{:S(2)}) %all-to-all-start) | async-done | bytes 131104 | tf_op jit(solution)/shard_map/all_to_all | solution.py:254
  10.5 0.7 collective-permute-start
  11.1 0.8 %collective-permute-done.2.refs_4_ = bf16[2,4,64,128]{3,2,1,0:T(8,128)(2,1)S(1)} collective-permute-done((bf16[2,4,64,128]{3,2,1,0:T(8,128)(2,1)S(1)}, bf16[2,4,64,128]{3,2,1,0:T(8,128)(2,1)S(1)}, u32[]{:S(2)}, u32[]{:S(2)}) %collective-permute-start.2) | collective-permute-done | bytes 131104 | tf_op jit(solution)/shard_map/ppermute | solution.py:269
  11.9 3.7 %collective-permute-start.3 = (bf16[2,4,64,128]{3,2,1,0:T(8,128)(2,1)S(1)}, bf16[2,4,64,128]{3,2,1,0:T(8,128)(2,1)S(1)}, u32[]{:S(2)}, u32[]{:S(2)}) collective-permute-start(bf16[2,4,64,128]{3,2,1,0:T(8,128)(2,1)S(1)} %pad_maximum_fusion), channel_id=1, source_target_pairs={{0,1},{1,0},{2,3},{3,2},{4,5},{5,4},{6,7},{7,6},{8,9},{9,8},{10,11... | collective-permute-start | bytes 393224 | tf_op jit(solution)/shard_map/ppermute | solution.py:270
  15.7 0.0 collective-permute-done.entering_ref
  15.7 1.3 %collective-permute-start.1 = (bf16[128,256]{1,0:T(8,128)(2,1)S(1)}, bf16[128,256]{1,0:T(8,128)(2,1)S(1)}, u32[]{:S(2)}, u32[]{:S(2)}) collective-permute-start(bf16[128,256]{1,0:T(8,128)(2,1)S(1)} %get-tuple-element.27), channel_id=1, source_target_pairs={{256,512},{257,513},{258,514},{259,515},{260,516},{261,517},{262,5... | collective-permute-start | bytes 196616 | tf_op jit(solution)/shard_map/ppermute | solution.py:307
  17.0 7.7 %collective-permute-done.1.entering_ref = bf16[128,256]{1,0:T(8,128)(2,1)S(1)} collective-permute-done((bf16[128,256]{1,0:T(8,128)(2,1)S(1)}, bf16[128,256]{1,0:T(8,128)(2,1)S(1)}, u32[]{:S(2)}, u32[]{:S(2)}) %collective-permute-start.1) | collective-permute-done | bytes 65568 | tf_op jit(solution)/shard_map/ppermute | solution.py:307
  24.7 1.9 %chain.5 = bf16[16,64,128]{2,1,0:T(8,128)(2,1)S(1)} custom-call(s32[1]{0:T(128)} %bitcast.1.turn_ref, bf16[512,128]{1,0:T(8,128)(2,1)S(1)} %get-tuple-element.21.band_first, bf16[256,512]{1,0:T(8,128)(2,1)S(1)} %get-tuple-element.22.band_even, bf16[256,512]{1,0:T(8,128)(2,1)S(1)} %get-tuple-element.23.band_odd, ...), custom_call_target="tpu_custom_call" | custom-call | flops 300000000 | bytes 4000000 | tf_op jit(solution)/shard_map/chain/pallas_call | solution.py:295
  26.6 0.0 collective-permute-done.3.refs_3_
  26.6 15.5 %all_to_all.15.refs_1_ = bf16[16,64,128]{2,1,0:T(8,128)(2,1)S(1)} all-to-all(bf16[16,64,128]{2,1,0:T(8,128)(2,1)S(1)} %chain.5), channel_id=1, replica_groups=mesh['zh'=3,'x'=4,'y'=8,'zq'=2,'zp'=2,'core'=2] {'x','zp','core'}, dimensions={0} | all-to-all | bytes 524288 | tf_op jit(solution)/shard_map/all_to_all | solution.py:310
  42.1 2.3 %image.1 = bf16[64,16,128]{2,1,0:T(8,128)(2,1)S(1)} custom-call(s32[1]{0:T(128)} %bitcast.quarter_ref.refs_0_, bf16[16,64,128]{2,1,0:T(8,128)(2,1)S(1)} %all_to_all.15.refs_1_, bf16[4,64,128]{2,1,0:T(8,128)(2,1)S(1)} %get-tuple-element.33.refs_2_, bf16[2,4,64,128]{3,2,1,0:T(8,128)(2,1)S(1)} %collective-permute-done.3.refs_3_, ...), custom_call_target="tpu_custom_call" | custom-call | flops 10000000 | bytes 2000000 | tf_op jit(solution)/shard_map/image/pallas_call | solution.py:313
  44.4 26.6 %all_to_all.16.part_ref = bf16[64,16,128]{2,1,0:T(8,128)(2,1)S(1)} all-to-all(bf16[64,16,128]{2,1,0:T(8,128)(2,1)S(1)} %image.1), channel_id=1, replica_groups=mesh['zh'=3,'x'=4,'y'=8,'zq'=2,'zp'=2,'core'=2] {'y','zq','zp','core'}, dimensions={0} | all-to-all | bytes 524288 | tf_op jit(solution)/shard_map/all_to_all | solution.py:325
  71.0 0.7 %total.1 = f32[1,32,1,256]{3,2,1,0:T(1,128)} custom-call(bf16[64,16,128]{2,1,0:T(8,128)(2,1)S(1)} %all_to_all.16.part_ref), custom_call_target="tpu_custom_call" | custom-call | tf_op jit(solution)/shard_map/total/pallas_call | solution.py:327
  (6 shorter events, 0.1 us)
Async XLA Ops:
  0.0 9.6 %copy-start = (bf16[4,2,64,256]{3,2,1,0:T(8,128)(2,1)S(1)}, bf16[4,2,64,256]{3,2,1,0:T(8,128)(2,1)}, u32[]{:S(2)}) copy-start(bf16[4,2,64,256]{3,2,1,0:T(8,128)(2,1)} %param.4) | copy-start | bytes 786436
  0.0 5.6 %copy-start.1 = (bf16[1,4,2,64,256]{4,3,2,1,0:T(8,128)(2,1)S(1)}, bf16[1,4,2,64,256]{4,3,2,1,0:T(8,128)(2,1)}, u32[]{:S(2)}) copy-start(bf16[1,4,2,64,256]{4,3,2,1,0:T(8,128)(2,1)} %param.7) | copy-start | bytes 786436
  1.6 8.8 %all-to-all-start = ((bf16[4,64,256]{2,1,0:T(8,128)(2,1)}), bf16[4,64,256]{2,1,0:T(8,128)(2,1)S(1)}, u32[]{:S(2)}, u32[]{:S(2)}) async-start(bf16[4,64,256]{2,1,0:T(8,128)(2,1)} %broadcast_in_dim.9), calls=%async_computation | async-start | bytes 262144 | tf_op jit(solution)/shard_map/all_to_all | solution.py:254
  5.9 3.1 %copy-start.2 = (bf16[4,4,2,2,25]{4,3,2,1,0:T(2,128)(2,1)S(1)}, bf16[4,4,2,2,25]{4,3,2,1,0:T(2,128)(2,1)}, u32[]{:S(2)}) copy-start(bf16[4,4,2,2,25]{4,3,2,1,0:T(2,128)(2,1)} %param.6) | copy-start | bytes 9604
  5.9 6.0 %collective-permute-start.2 = (bf16[2,4,64,128]{3,2,1,0:T(8,128)(2,1)S(1)}, bf16[2,4,64,128]{3,2,1,0:T(8,128)(2,1)S(1)}, u32[]{:S(2)}, u32[]{:S(2)}) collective-permute-start(bf16[2,4,64,128]{3,2,1,0:T(8,128)(2,1)S(1)} %get-tuple-element.31), channel_id=1, source_target_pairs={{0,2},{2,0},{1,3},{3,1},{4,6},{6,4},{5,7},{7,5},{8,10},{10,8},{9,1... | collective-permute-start | bytes 393224 | tf_op jit(solution)/shard_map/ppermute | solution.py:269
  10.5 5.2 %collective-permute-start = (bf16[128,256]{1,0:T(8,128)(2,1)S(1)}, bf16[128,256]{1,0:T(8,128)(2,1)S(1)}, u32[]{:S(2)}, u32[]{:S(2)}) collective-permute-start(bf16[128,256]{1,0:T(8,128)(2,1)S(1)} %get-tuple-element.25), channel_id=1, source_target_pairs={{0,256},{1,257},{2,258},{3,259},{4,260},{5,261},{6,262},{7,263},{8... | collective-permute-start | bytes 196616 | tf_op jit(solution)/shard_map/ppermute | solution.py:307
  11.9 14.7 %collective-permute-start.3 = (bf16[2,4,64,128]{3,2,1,0:T(8,128)(2,1)S(1)}, bf16[2,4,64,128]{3,2,1,0:T(8,128)(2,1)S(1)}, u32[]{:S(2)}, u32[]{:S(2)}) collective-permute-start(bf16[2,4,64,128]{3,2,1,0:T(8,128)(2,1)S(1)} %pad_maximum_fusion), channel_id=1, source_target_pairs={{0,1},{1,0},{2,3},{3,2},{4,5},{5,4},{6,7},{7,6},{8,9},{9,8},{10,11... | collective-permute-start | bytes 393224 | tf_op jit(solution)/shard_map/ppermute | solution.py:270
  15.7 9.0 %collective-permute-start.1 = (bf16[128,256]{1,0:T(8,128)(2,1)S(1)}, bf16[128,256]{1,0:T(8,128)(2,1)S(1)}, u32[]{:S(2)}, u32[]{:S(2)}) collective-permute-start(bf16[128,256]{1,0:T(8,128)(2,1)S(1)} %get-tuple-element.27), channel_id=1, source_target_pairs={{256,512},{257,513},{258,514},{259,515},{260,516},{261,517},{262,5... | collective-permute-start | bytes 196616 | tf_op jit(solution)/shard_map/ppermute | solution.py:307

commit v14 on v11

--- a/solution.py
+++ b/solution.py
@@ -215,7 +215,7 @@
         out_ref[x] = jnp.where(left, total[:REACH], total[REACH:]).astype(jnp.bfloat16)
         return carry
 
-    lax.fori_loop(0, NX, fold, 0, unroll=32)
+    lax.fori_loop(0, NX, fold, 0, unroll=True)
 
 
 def sum_kernel(part_ref, out_ref):
@@ -250,8 +250,8 @@
     mine_x = lax.axis_index("x")
     core = lax.axis_index("core")
     blocks = lax.axis_size("zh")
-    local = regions[0].astype(jnp.bfloat16)
-    copies = jnp.broadcast_to(local[None], (GROUP, NX, NY))
+    slot = lax.broadcasted_iota(jnp.int32, (GROUP, NX, NY), 0)
+    copies = jnp.where(slot < GROUP + mine_x, regions, 0).astype(jnp.bfloat16)
     copies, local_source, table = lax.optimization_barrier((copies, source[0], table))
     all_regions = lax.all_to_all(copies, "x", 0, 0, tiled=True)
     quarter = (lax.axis_index("yp") * 2 + core).astype(jnp.int32).reshape(1)

time: 71.5 us -> 71.5 us (level)
  other arithmetic: 0.92 us -> 1.65 us
    convert_element_type x0 -> x1, other arithmetic: none -> 1.63 us  [body(): copies = jnp.where(slot < GROUP + mine_x, regions, 0).astype(jnp.bfloat16)]
    broadcast_in_dim x1 -> x0, other arithmetic: 0.9 us -> none  [body(): copies = jnp.broadcast_to(local[None], (GROUP, NX, NY))]
where the time goes in v14:
time: 71.5 us; the launch traced here: 71 us
  blocking collectives  40.3 us (56%)
  starting transfers between devices  21.3 us (30%)
  Pallas kernels  5.81 us (8%)
  waiting for transfers between devices  1.73 us (2%)
  other arithmetic  1.65 us (2%)
    all_to_all x1, blocking collectives, body(): parts = lax.all_to_all(partial_image, FREQ, 0, 0, tiled=True)  26.3 us
    all_to_all x1, blocking collectives, body(): waves = lax.all_to_all(waves, ('x',) + QUAD, 0, 0, tiled=True)  14 us
    ppermute x1, starting transfers between devices, body(): from_core = lax.ppermute(to_core, 'core', [(0, 1), (1, 0)])  10.9 us
    all_to_all x1, starting transfers between devices, body(): all_regions = lax.all_to_all(copies, 'x', 0, 0, tiled=True)  4.84 us
    ppermute x1, starting transfers between devices, body(): lax.ppermute(jnp.concatenate([to_chip, from_core[1:]], axis=0), 'yp', [(0...  3.2 us
    ppermute x2, starting transfers between devices, body(): entering = lax.ppermute(leaving[0], 'zh', [(block, block + 1)])  2.37 us
    pallas_call x1, Pallas kernels, body(): pl.pallas_call(lambda *refs: image_kernel(scale, *refs), out_shape=jax.Sh...  2.26 us
    pallas_call x3, Pallas kernels, body(): pl.pallas_call(functools.partial(chain_kernel, block == 0), out_shape=(wa...  1.98 us
  transfers between devices with their start and end apart: 5, of which 1 were waited for; matrix products, arithmetic and copies ran while one was open for 0% of the time, Pallas kernels for 4%

profile of v14, /device:TPU:1, one launch (start us, length us, event | category | flops | bytes accessed | tf_op | source)
XLA Modules:
  0.0 71.0 jit_solution(5139343802513137703)
XLA Ops:
  0.0 0.0 copy-start
  0.0 0.0 copy-start.1
  0.0 1.6 %select_convert_fusion = bf16[4,64,256]{2,1,0:T(8,128)(2,1)} fusion(s32[64,256]{1,0:T(8,128)} %bitcast.11, pred[4]{0:T(512)(128)(4,1)S(1)} %iota_compare_fusion), kind=kLoop, calls=%fused_computation | loop fusion | flops 131072 | bytes 196612 | tf_op jit(solution)/shard_map/convert_element_type | solution.py:254
  1.6 4.8 %all-to-all-start = ((bf16[4,64,256]{2,1,0:T(8,128)(2,1)}), bf16[4,64,256]{2,1,0:T(8,128)(2,1)S(1)}, u32[]{:S(2)}, u32[]{:S(2)}) async-start(bf16[4,64,256]{2,1,0:T(8,128)(2,1)} %select_convert_fusion), calls=%async_computation | async-start | bytes 262144 | tf_op jit(solution)/shard_map/all_to_all | solution.py:256
  6.5 0.0 copy-done.1
  6.5 0.3 pack.1
  6.8 0.0 copy-start.2
  6.8 10.9 %collective-permute-start.2 = (bf16[2,4,64,128]{3,2,1,0:T(8,128)(2,1)S(1)}, bf16[2,4,64,128]{3,2,1,0:T(8,128)(2,1)S(1)}, u32[]{:S(2)}, u32[]{:S(2)}) collective-permute-start(bf16[2,4,64,128]{3,2,1,0:T(8,128)(2,1)S(1)} %get-tuple-element.31), channel_id=1, source_target_pairs={{0,1},{1,0},{2,3},{3,2},{4,5},{5,4},{6,7},{7,6},{8,9},{9,8},{10,11... | collective-permute-start | bytes 393224 | tf_op jit(solution)/shard_map/ppermute | solution.py:271
  17.8 0.0 copy-done.2
  17.8 0.5 bands.1
  18.3 0.0 copy-done
  18.4 0.0 all-to-all-done.regions_ref
  18.4 1.9 %chain.3 = (bf16[16,64,128]{2,1,0:T(8,128)(2,1)S(1)}, bf16[128,256]{1,0:T(8,128)(2,1)S(1)}) custom-call(s32[1]{0:T(128)} %bitcast.7.turn_ref, bf16[512,128]{1,0:T(8,128)(2,1)S(1)} %get-tuple-element.21.band_first, bf16[256,512]{1,0:T(8,128)(2,1)S(1)} %get-tuple-element.22.band_even, bf16[256,512]{1,0:T(8,128)(2,1)S(1)} %get-tuple-element.23.band_odd, ...), custom_call_target="tpu_custom_call" | custom-call | flops 300000000 | bytes 4000000 | tf_op jit(solution)/shard_map/chain/pallas_call | solution.py:297
  20.3 1.7 %collective-permute-start = (bf16[128,256]{1,0:T(8,128)(2,1)S(1)}, bf16[128,256]{1,0:T(8,128)(2,1)S(1)}, u32[]{:S(2)}, u32[]{:S(2)}) collective-permute-start(bf16[128,256]{1,0:T(8,128)(2,1)S(1)} %get-tuple-element.25), channel_id=1, source_target_pairs={{0,256},{1,257},{2,258},{3,259},{4,260},{5,261},{6,262},{7,263},{8... | collective-permute-start | bytes 196616 | tf_op jit(solution)/shard_map/ppermute | solution.py:309
  22.0 0.0 collective-permute-done.2.refs_3_
  22.0 3.2 %collective-permute-start.3 = (bf16[2,4,64,128]{3,2,1,0:T(8,128)(2,1)S(1)}, bf16[2,4,64,128]{3,2,1,0:T(8,128)(2,1)S(1)}, u32[]{:S(2)}, u32[]{:S(2)}) collective-permute-start(bf16[2,4,64,128]{3,2,1,0:T(8,128)(2,1)S(1)} %pad_maximum_fusion), channel_id=1, source_target_pairs={{0,8},{8,0},{1,9},{9,1},{2,10},{10,2},{3,11},{11,3},{4,12},{12,4},... | collective-permute-start | bytes 393224 | tf_op jit(solution)/shard_map/ppermute | solution.py:272
  25.3 0.0 collective-permute-done.entering_ref
  25.3 0.7 collective-permute-start.1
  26.0 0.0 collective-permute-done.1.entering_ref
  26.0 1.7 %collective-permute-done.3.refs_4_ = bf16[2,4,64,128]{3,2,1,0:T(8,128)(2,1)S(1)} collective-permute-done((bf16[2,4,64,128]{3,2,1,0:T(8,128)(2,1)S(1)}, bf16[2,4,64,128]{3,2,1,0:T(8,128)(2,1)S(1)}, u32[]{:S(2)}, u32[]{:S(2)}) %collective-permute-start.3) | collective-permute-done | bytes 131104 | tf_op jit(solution)/shard_map/ppermute | solution.py:272
  27.8 14.0 %all_to_all.15.refs_1_ = bf16[16,64,128]{2,1,0:T(8,128)(2,1)S(1)} all-to-all(bf16[16,64,128]{2,1,0:T(8,128)(2,1)S(1)} %chain.5), channel_id=1, replica_groups=mesh['zh'=3,'x'=4,'yq'=4,'yp'=2,'zl'=4,'core'=2] {'x','yp','core'}, dimensions={0} | all-to-all | bytes 524288 | tf_op jit(solution)/shard_map/all_to_all | solution.py:312
  41.7 2.3 %image.1 = bf16[64,16,128]{2,1,0:T(8,128)(2,1)S(1)} custom-call(s32[1]{0:T(128)} %bitcast.quarter_ref.refs_0_, bf16[16,64,128]{2,1,0:T(8,128)(2,1)S(1)} %all_to_all.15.refs_1_, bf16[4,64,128]{2,1,0:T(8,128)(2,1)S(1)} %get-tuple-element.33.refs_2_, bf16[2,4,64,128]{3,2,1,0:T(8,128)(2,1)S(1)} %collective-permute-done.2.refs_3_, ...), custom_call_target="tpu_custom_call" | custom-call | flops 10000000 | bytes 2000000 | tf_op jit(solution)/shard_map/image/pallas_call | solution.py:315
  44.0 26.3 %all_to_all.16.part_ref = bf16[64,16,128]{2,1,0:T(8,128)(2,1)S(1)} all-to-all(bf16[64,16,128]{2,1,0:T(8,128)(2,1)S(1)} %image.1), channel_id=1, replica_groups=mesh['zh'=3,'x'=4,'yq'=4,'yp'=2,'zl'=4,'core'=2] {'yq','yp','zl','core'}, dimensions={0} | all-to-all | bytes 524288 | tf_op jit(solution)/shard_map/all_to_all | solution.py:327
  70.3 0.7 %total.1 = f32[1,32,1,256]{3,2,1,0:T(1,128)} custom-call(bf16[64,16,128]{2,1,0:T(8,128)(2,1)S(1)} %all_to_all.16.part_ref), custom_call_target="tpu_custom_call" | custom-call | tf_op jit(solution)/shard_map/total/pallas_call | solution.py:329
  (7 shorter events, 0.1 us)
Async XLA Ops:
  0.0 18.3 %copy-start = (bf16[4,2,64,256]{3,2,1,0:T(8,128)(2,1)S(1)}, bf16[4,2,64,256]{3,2,1,0:T(8,128)(2,1)}, u32[]{:S(2)}) copy-start(bf16[4,2,64,256]{3,2,1,0:T(8,128)(2,1)} %param.4) | copy-start | bytes 786436
  0.0 6.5 %copy-start.1 = (bf16[1,4,2,64,256]{4,3,2,1,0:T(8,128)(2,1)S(1)}, bf16[1,4,2,64,256]{4,3,2,1,0:T(8,128)(2,1)}, u32[]{:S(2)}) copy-start(bf16[1,4,2,64,256]{4,3,2,1,0:T(8,128)(2,1)} %param.7) | copy-start | bytes 786436
  1.6 16.7 %all-to-all-start = ((bf16[4,64,256]{2,1,0:T(8,128)(2,1)}), bf16[4,64,256]{2,1,0:T(8,128)(2,1)S(1)}, u32[]{:S(2)}, u32[]{:S(2)}) async-start(bf16[4,64,256]{2,1,0:T(8,128)(2,1)} %select_convert_fusion), calls=%async_computation | async-start | bytes 262144 | tf_op jit(solution)/shard_map/all_to_all | solution.py:256
  6.8 11.0 %copy-start.2 = (bf16[4,4,2,2,25]{4,3,2,1,0:T(2,128)(2,1)S(1)}, bf16[4,4,2,2,25]{4,3,2,1,0:T(2,128)(2,1)}, u32[]{:S(2)}) copy-start(bf16[4,4,2,2,25]{4,3,2,1,0:T(2,128)(2,1)} %param.6) | copy-start | bytes 9604
  6.8 15.2 %collective-permute-start.2 = (bf16[2,4,64,128]{3,2,1,0:T(8,128)(2,1)S(1)}, bf16[2,4,64,128]{3,2,1,0:T(8,128)(2,1)S(1)}, u32[]{:S(2)}, u32[]{:S(2)}) collective-permute-start(bf16[2,4,64,128]{3,2,1,0:T(8,128)(2,1)S(1)} %get-tuple-element.31), channel_id=1, source_target_pairs={{0,1},{1,0},{2,3},{3,2},{4,5},{5,4},{6,7},{7,6},{8,9},{9,8},{10,11... | collective-permute-start | bytes 393224 | tf_op jit(solution)/shard_map/ppermute | solution.py:271
  20.3 5.0 %collective-permute-start = (bf16[128,256]{1,0:T(8,128)(2,1)S(1)}, bf16[128,256]{1,0:T(8,128)(2,1)S(1)}, u32[]{:S(2)}, u32[]{:S(2)}) collective-permute-start(bf16[128,256]{1,0:T(8,128)(2,1)S(1)} %get-tuple-element.25), channel_id=1, source_target_pairs={{0,256},{1,257},{2,258},{3,259},{4,260},{5,261},{6,262},{7,263},{8... | collective-permute-start | bytes 196616 | tf_op jit(solution)/shard_map/ppermute | solution.py:309
  22.0 5.7 %collective-permute-start.3 = (bf16[2,4,64,128]{3,2,1,0:T(8,128)(2,1)S(1)}, bf16[2,4,64,128]{3,2,1,0:T(8,128)(2,1)S(1)}, u32[]{:S(2)}, u32[]{:S(2)}) collective-permute-start(bf16[2,4,64,128]{3,2,1,0:T(8,128)(2,1)S(1)} %pad_maximum_fusion), channel_id=1, source_target_pairs={{0,8},{8,0},{1,9},{9,1},{2,10},{10,2},{3,11},{11,3},{4,12},{12,4},... | collective-permute-start | bytes 393224 | tf_op jit(solution)/shard_map/ppermute | solution.py:272
  25.3 0.7 collective-permute-start.1
